TPU v7x, 256 devices: a whole 4x4x8 slice. The times are simulated.
256 devices in a mesh: dp: 32 (over z, y), tensor: 8 (over x, core).
Axes of the slice: x: 4, y: 4, z: 8, core: 2. Of those that a mesh axis runs over, the one named last changes fastest.
Arguments:
- tokens: bfloat16 [4096, 8192], P('dp', 'tensor'), may hold values from -6 to 6
- gate_up: bfloat16 [8192, 2, 16384], P('tensor', None, 'dp'), may hold values from -0.0625 to 0.0625
- adapter_in: bfloat16 [32, 2, 16, 8192], P(None, None, None, 'tensor'), may hold values from -0.0625 to 0.0625
- adapter_out: bfloat16 [32, 2, 16, 16384], P(None, None, None, 'dp'), may hold values from -1.5 to 1.5
- d_hidden: bfloat16 [4096, 16384], P('tensor', 'dp'), may hold values from -0.1796875 to 0.1796875
- block_adapter: int32 [32], replicated, may hold values from 0 to 31
- block_live: int32 [32], replicated, may hold values from 1 to 128, as said below
- owner_slot: int32 [32], replicated, may hold values from 0 to 63, as said below
Outputs:
- hidden: bfloat16 [4096, 16384], P('tensor', 'dp')
- grad_in: float32 [64, 2, 16, 8192], P('dp', None, None, 'tensor')
- grad_out: float32 [64, 2, 16, 16384], P('dp', None, None, 'tensor')
Inputs may be any that keep to these rules, and one draw needn't show every extreme that they name: `block_live`: block lengths; some block is full in every draw. `owner_slot`: distinct slots; slot s belongs to data group s // 2; some group holds 2 adapters in every draw.
All inputs are finite; a program needn't handle non-finite values.
Results may differ from a plain program's by a relative error of at most 0.0057.
Values may be sent and summed in bfloat16 or wider, within the bound.
No kernel may reach another device: no remote copies, remote signals or barrier semaphores. Data moves between devices by JAX's collectives and lax.ppermute only.
A program may use at most 128 MiB of HBM per device.

v0:
```python
import jax
import jax.numpy as jnp
from jax import lax
from jax.sharding import PartitionSpec as P

R = 16
ADAPTERS = 32
BLOCK_ROWS = 128


def body(tokens, gate_up, adapter_in, adapter_out, d_hidden, block_adapter, block_live, owner_slot):
    dp_index = lax.axis_index("dp")
    tensor_index = lax.axis_index("tensor")
    n_tensor = lax.axis_size("tensor")
    n_dp = lax.axis_size("dp")
    d_part = tokens.shape[1]
    hidden_part = gate_up.shape[2]
    gathered = lax.all_gather(tokens, "dp", axis=0, tiled=True)
    total_rows = gathered.shape[0]
    local_rows = total_rows // n_tensor
    blocks_all = total_rows // BLOCK_ROWS
    resident_blocks = local_rows // BLOCK_ROWS
    weights = gate_up.reshape(d_part, 2 * hidden_part)
    base_output = lax.psum_scatter(
        jnp.dot(gathered, weights, preferred_element_type=jnp.float32),
        "tensor",
        scatter_dimension=0,
        tiled=True,
    )
    in_sel = adapter_in[block_adapter]
    low_part = jnp.einsum(
        "brd,bgkd->brgk",
        gathered.reshape(blocks_all, BLOCK_ROWS, d_part),
        in_sel,
        preferred_element_type=jnp.float32,
    )
    low_sum = lax.psum_scatter(
        low_part.reshape(total_rows, 2 * R), "tensor", scatter_dimension=0, tiled=True
    )
    rank_state = low_sum.astype(jnp.bfloat16).reshape(resident_blocks, BLOCK_ROWS, 2, R)
    local_ids = lax.dynamic_slice_in_dim(
        block_adapter, tensor_index * resident_blocks, resident_blocks, 0
    )
    local_live = lax.dynamic_slice_in_dim(
        block_live, tensor_index * resident_blocks, resident_blocks, 0
    )
    output_selector = adapter_out[local_ids]
    adapter_output = jnp.einsum(
        "iacz,iczs->iacs", rank_state, output_selector, preferred_element_type=jnp.float32
    )
    gate_input = base_output.reshape(resident_blocks, BLOCK_ROWS, 2, hidden_part) + adapter_output
    gate = gate_input[:, :, 0]
    up_part = gate_input[:, :, 1]
    hidden = (jax.nn.silu(gate) * up_part).astype(jnp.bfloat16).reshape(local_rows, hidden_part)
    live = (jnp.arange(BLOCK_ROWS, dtype=jnp.int32)[None, :] < local_live[:, None]).astype(
        jnp.float32
    )
    cotan = (
        d_hidden.reshape(resident_blocks, BLOCK_ROWS, hidden_part).astype(jnp.float32)
        * live[:, :, None]
    )
    sigma = jax.nn.sigmoid(gate)
    dgate = cotan * up_part * sigma * (1.0 + gate * (1.0 - sigma))
    dup = cotan * gate * sigma
    dpre = jnp.stack([dgate, dup], 2).astype(jnp.bfloat16)
    dlow_part = jnp.einsum(
        "brgf,bgkf->brgk", dpre, output_selector, preferred_element_type=jnp.float32
    ).reshape(local_rows, 2 * R)
    dlow_local = lax.psum(dlow_part, "dp").astype(jnp.bfloat16)
    dlow_all = lax.all_gather(dlow_local, "tensor", axis=0, tiled=True)
    own_count = 2 * ADAPTERS // n_dp
    slot_all = owner_slot[block_adapter] - dp_index * own_count
    selector = (jnp.arange(own_count, dtype=jnp.int32)[:, None] == slot_all[None, :]).astype(
        jnp.bfloat16
    )
    weighted = selector[:, :, None, None] * dlow_all.reshape(blocks_all, BLOCK_ROWS, 2 * R)[None]
    weighted = weighted.reshape(own_count, total_rows, 2 * R)
    grad_in = jnp.einsum(
        "srk,rd->skd", weighted, gathered, preferred_element_type=jnp.float32
    ).reshape(own_count, 2, R, d_part)
    block_grad = jnp.einsum("brgk,brgf->bgkf", rank_state, dpre, preferred_element_type=jnp.float32)
    slot_local = owner_slot[local_ids]
    picker = (jnp.arange(2 * ADAPTERS, dtype=jnp.int32)[:, None] == slot_local[None, :]).astype(
        jnp.float32
    )
    slotted = jnp.einsum("sb,bgkf->sgkf", picker, block_grad, precision=lax.Precision.HIGHEST)
    moved = lax.all_to_all(slotted, "dp", split_axis=0, concat_axis=3, tiled=True)
    grad_out = lax.psum_scatter(moved, "tensor", scatter_dimension=3, tiled=True)
    return (hidden, grad_in, grad_out)


def solution(mesh):
    placed = (
        P("dp", "tensor"),
        P("tensor", None, "dp"),
        P(None, None, None, "tensor"),
        P(None, None, None, "dp"),
        P("tensor", "dp"),
        P(),
        P(),
        P(),
    )
    return jax.shard_map(
        body,
        mesh=mesh,
        in_specs=placed,
        out_specs=(P("tensor", "dp"), P("dp", None, None, "tensor"), P("dp", None, None, "tensor")),
        check_vma=False,
    )
```

profile of v0, /device:TPU:1, one launch (start us, length us, event | category | flops | bytes accessed | tf_op | source)
XLA Modules:
  0.0 538.2 jit_solution(6852887776408108788)
XLA Ops:
  7.2 0.7 all-gather.2.cloned.1.call-update
  8.0 3.5 copy.30
  11.5 2.0 gather_fusion.1
  13.6 99.0 %all-gather.2.cloned.1.call-done = bf16[4096,1024]{1,0:T(8,128)(2,1)} async-done(((bf16[128,1024]{1,0:T(8,128)(2,1)}), bf16[4096,1024]{1,0:T(8,128)(2,1)}) %all-gather.2.cloned.1.call-update) | async-done | bytes 8388624 | tf_op jit(solution)/shard_map/all_gather | solution.py:18
  112.6 6.9 %convolution_bitcast_fusion = f32[32,128,2,16]{1,3,2,0:T(8,128)S(1)} fusion(bf16[32,2,16,1024]{3,2,1,0:T(8,128)(2,1)} %gather_fusion.1, bf16[32,128,1024,1]{2,1,3,0:T(8,128)(2,1)} %bitcast.77), kind=kOutput, calls=%fused_computation.7 | convolution fusion | flops 268435456 | bytes 11010048 | tf_op jit(solution)/shard_map/brd,bgkd->brgk/dot_general | solution.py:31
  119.8 1.1 copy.44
  121.0 16.1 %fusion.27 = f32[4096,1024]{1,0:T(8,128)} fusion(bf16[4096,1024]{1,0:T(8,128)(2,1)} %all-gather.2.cloned.1.call-done, bf16[1024,1024]{1,0:T(8,128)(2,1)} %bitcast.81), kind=kOutput, calls=%fused_computation.51 | convolution fusion | flops 8589934592 | bytes 27262976 | tf_op jit(solution)/shard_map/dot_general | solution.py:25
  137.9 1.8 gather_fusion
  140.4 9.3 %reduce-scatter.6.cloned.1.call-done = f32[512,32]{0,1:T(8,128)} async-done(((f32[4096,32]{0,1:T(8,128)}), f32[512,32]{0,1:T(8,128)}) %reduce-scatter.6.cloned.1.call-update) | async-done | bytes 65552 | tf_op jit(solution)/shard_map/reduce_scatter | solution.py:37
  149.8 0.8 convert_element_type.40
  150.6 96.9 %reduce-scatter.4.cloned.1.call-done = f32[512,1024]{1,0:T(8,128)} async-done(((f32[4096,1024]{1,0:T(8,128)}), f32[512,1024]{1,0:T(8,128)}) %reduce-scatter.4.cloned.1.call-update) | async-done | bytes 2097168 | tf_op jit(solution)/shard_map/reduce_scatter | solution.py:24
  247.5 4.0 reshape.99
  251.5 2.2 bitcast_add_fusion
  253.8 1.5 fusion.6
  256.2 1.9 fusion.15
  258.1 2.4 copy.24
  260.6 102.4 %all_to_all.18 = f32[64,2,16,512]{3,2,1,0:T(8,128)S(1)} all-to-all(f32[64,2,16,512]{3,2,1,0:T(8,128)S(1)} %copy.24), channel_id=1, replica_groups=mesh['dp'=32,'tensor'=8] {'dp'}, dimensions={0} | all-to-all | bytes 8388608 | tf_op jit(solution)/shard_map/all_to_all | solution.py:87
  363.0 2.5 copy.29
  365.6 0.7 gather_fusion.2
  366.4 1.6 convolution_bitcast_fusion.1
  368.1 111.7 %psum.7 = bf16[512,32]{0,1:T(8,128)(2,1)S(1)} all-reduce(f32[512,32]{0,1:T(8,128)S(1)} %bitcast.87), channel_id=1, replica_groups=mesh['dp'=32,'tensor'=8] {'dp'}, use_global_device_ids=true, to_apply=%region_2.3 | all-reduce | flops 16384 | bytes 98304 | tf_op jit(solution)/shard_map/psum | solution.py:69
  479.8 43.7 %all_gather.7 = bf16[4096,32]{0,1:T(8,128)(2,1)S(1)} all-gather(bf16[512,32]{0,1:T(8,128)(2,1)S(1)} %psum.7), channel_id=1, replica_groups=mesh['dp'=32,'tensor'=8] {'tensor'}, dimensions={0}, use_global_device_ids=true | all-gather | bytes 294912 | tf_op jit(solution)/shard_map/all_gather | solution.py:70
  523.5 2.4 fusion.9
  526.0 5.7 %fusion = f32[2,2,16,1024]{3,2,1,0:T(8,128)} fusion(bf16[4096,1024]{1,0:T(8,128)(2,1)} %all-gather.2.cloned.1.call-done, bf16[2,16,4096]{2,1,0:T(8,128)(2,1)S(1)} %bitcast.84, bf16[2,4096]{1,0:T(2,128)(2,1)S(1)} %bitcast.88), kind=kOutput, calls=%fused_computation.4 | convolution fusion | flops 537133056 | bytes 8929280 | tf_op jit(solution)/shard_map/srk,rd->skd/dot_general | solution.py:78
  (38 shorter events, 3.2 us)
Async XLA Ops:
  7.2 4.4 copy-start
  7.2 105.4 %all-gather.2.cloned.1.call-start = ((), (), s32[]{:S(2)}) async-start(), calls=%async_computation.4 | async-start | bytes 8650752 | tf_op jit(solution)/shard_map/all_gather | solution.py:18
  7.9 141.8 %reduce-scatter.6.cloned.1.call-start = ((), (), s32[]{:S(2)}) async-start(), calls=%async_computation.6 | async-start | bytes 589824 | tf_op jit(solution)/shard_map/reduce_scatter | solution.py:37
  8.0 3.5 copy-start.6
  121.0 126.5 %reduce-scatter.4.cloned.1.call-start = ((), (), s32[]{:S(2)}) async-start(), calls=%async_computation.5 | async-start | bytes 18874368 | tf_op jit(solution)/shard_map/reduce_scatter | solution.py:24
  137.1 0.7 copy-start.5
  137.1 2.6 copy-start.1
  137.1 394.5 %reduce-scatter.8.cloned.1.call-start = ((), (), s32[]{:S(2)}) async-start(), calls=%async_computation.7 | async-start | bytes 4718592 | tf_op jit(solution)/shard_map/reduce_scatter | solution.py:88
  251.5 2.2 copy-start.2
  255.3 0.8 copy-start.3
  255.3 1.0 copy-start.4
Sparse Core Ops, SparseCore 0:
  10.6 101.9 all-gather.1
  121.1 28.6 reduce-scatter.5
  152.6 94.8 reduce-scatter.3
  365.7 36.9 reduce-scatter.7
where the time goes:
time: 539 us; the launch traced here: 538 us
  blocking collectives  258 us (48%)
  waiting for transfers between devices  206 us (38%)
  matrix products  34.6 us (6%)
  local copies, waits for them, and re-layouts  20.5 us (4%)
  between operations  13.9 us (3%)
    psum x1, blocking collectives, body(): dlow_local = lax.psum(dlow_part, 'dp').astype(jnp.bfloat16)  112 us
    all_to_all x1, blocking collectives, body(): lax.all_to_all(slotted, 'dp', split_axis=0, concat_axis=3, tiled=True)  102 us
    all_gather x1, waiting for transfers between devices, body(): gathered = lax.all_gather(tokens, 'dp', axis=0, tiled=True)  99 us
    reduce_scatter x1, waiting for transfers between devices, body(): lax.psum_scatter(jnp.dot(gathered, weights, preferred_element_type=jnp.fl...  96.9 us
    all_gather x1, blocking collectives, body(): dlow_all = lax.all_gather(dlow_local, 'tensor', axis=0, tiled=True)  43.7 us
    dot_general x1, matrix products, body(): jnp.dot(gathered, weights, preferred_element_type=jnp.float32)  16.1 us
  transfers between devices with their start and end apart: 4, of which 3 were waited for; matrix products, arithmetic and copies ran while one was open for 7% of the time, Pallas kernels for 0%

commit v1 on v0

v1 whole, which is shorter than its diff:
```python
import jax
import jax.numpy as jnp
from jax import lax
from jax.experimental import pallas as pl
from jax.experimental.pallas import tpu as pltpu
from jax.sharding import PartitionSpec as P

R = 16
RANKS = 2 * R
BLOCK_ROWS = 128
Z, Y, X, C = 8, 4, 4, 2
N_DP, N_TENSOR = Z * Y, X * C
OWN = 2
SLOTS = OWN * N_DP
BF16, F32 = jnp.bfloat16, jnp.float32

SWAP = [((z * Y + y) * N_TENSOR + t, (t * Y + y) * N_TENSOR + z)
        for z in range(Z) for y in range(Y) for t in range(N_TENSOR)]


def shift_x(step):
    return [(x * C + c, ((x + step) % X) * C + c) for x in range(X) for c in range(C)]


SIBLING = [(x * C + c, x * C + 1 - c) for x in range(X) for c in range(C)]


def gather_weights(own):
    half = own.shape[0] // 2
    x, c = lax.axis_index("tensor") // C, lax.axis_index("tensor") % C
    left = lax.ppermute(own, "tensor", shift_x(1))
    right = lax.ppermute(own, "tensor", shift_x(-1))
    far_a = lax.ppermute(left[:half], "tensor", shift_x(1))
    far_b = lax.ppermute(right[half:], "tensor", shift_x(-1))
    pieces = [(0, 0, own), (1, 0, left), (3, 0, right), (2, 0, far_a), (2, half, far_b)]
    full = jnp.zeros((N_TENSOR,) + own.shape, own.dtype)
    for back, row, piece in pieces:
        place = ((x - back) % X) * C
        other = lax.ppermute(piece, "tensor", SIBLING)
        full = lax.dynamic_update_slice(full, piece[None], (place + c, row, 0))
        full = lax.dynamic_update_slice(full, other[None], (place + 1 - c, row, 0))
    return full


def block_kernel(live_ref, x_ref, w_ref, low_ref, out_map_ref, cot_ref,
                 hidden_ref, dlow_ref, grad_ref, acc_ref):
    k = pl.program_id(0)
    part = jnp.dot(x_ref[0], w_ref[0], preferred_element_type=F32)

    @pl.when(k == 0)
    def _():
        acc_ref[...] = part

    @pl.when(k > 0)
    def _():
        acc_ref[...] += part

    @pl.when(k == pl.num_programs(0) - 1)
    def _():
        half = cot_ref.shape[1]
        for b in range(acc_ref.shape[0] // BLOCK_ROWS):
            rows = slice(b * BLOCK_ROWS, (b + 1) * BLOCK_ROWS)
            ranks = slice(b * RANKS, (b + 1) * RANKS)
            low = low_ref[ranks, :]
            out_map = out_map_ref[b]
            pre = acc_ref[rows, :] + lax.dot_general(
                low, out_map, (((0,), (0,)), ((), ())), preferred_element_type=F32)
            gate, up = pre[:, :half], pre[:, half:]
            sigma = jax.nn.sigmoid(gate)
            gated = gate * sigma
            hidden_ref[rows, :] = (gated * up).astype(BF16)
            live = lax.broadcasted_iota(jnp.int32, (BLOCK_ROWS, half), 0) < live_ref[b]
            cotan = jnp.where(live, cot_ref[rows, :].astype(F32), 0.0)
            dgate = cotan * up * sigma * (1.0 + gate * (1.0 - sigma))
            dup = cotan * gated
            dpre = jnp.concatenate([dgate, dup], 1).astype(BF16)
            dlow_ref[ranks, :] = lax.dot_general(
                out_map, dpre, (((1,), (1,)), ((), ())), preferred_element_type=F32)
            grad = jnp.dot(low, dpre, preferred_element_type=F32)
            grad_ref[b, :R, :] = grad[:R, :half]
            grad_ref[b, R:, :] = grad[R:, half:]


def project(live, rows, weights, low, out_map, cotan):
    parts, n_rows, depth = rows.shape
    width = weights.shape[2]
    blocks = n_rows // BLOCK_ROWS
    half = width // 2
    return pl.pallas_call(
        block_kernel,
        grid_spec=pltpu.PrefetchScalarGridSpec(
            num_scalar_prefetch=1,
            grid=(parts,),
            in_specs=[
                pl.BlockSpec((1, n_rows, depth), lambda k, s: (k, 0, 0)),
                pl.BlockSpec((1, depth, width), lambda k, s: (k, 0, 0)),
                pl.BlockSpec(low.shape, lambda k, s: (0, 0)),
                pl.BlockSpec(out_map.shape, lambda k, s: (0, 0, 0)),
                pl.BlockSpec(cotan.shape, lambda k, s: (0, 0)),
            ],
            out_specs=[
                pl.BlockSpec((n_rows, half), lambda k, s: (0, 0)),
                pl.BlockSpec(low.shape, lambda k, s: (0, 0)),
                pl.BlockSpec((blocks, RANKS, half), lambda k, s: (0, 0, 0)),
            ],
            scratch_shapes=[pltpu.VMEM((n_rows, width), F32)],
        ),
        out_shape=[
            jax.ShapeDtypeStruct((n_rows, half), BF16),
            jax.ShapeDtypeStruct(low.shape, F32),
            jax.ShapeDtypeStruct((blocks, RANKS, half), F32),
        ],
        compiler_params=pltpu.CompilerParams(vmem_limit_bytes=40 * 2 ** 20),
        cost_estimate=pl.CostEstimate(
            flops=2 * parts * n_rows * depth * width,
            bytes_accessed=2 * parts * depth * (n_rows + width),
            transcendentals=n_rows * half),
    )(live, rows, weights, low, out_map, cotan)


def body(tokens, gate_up, adapter_in, adapter_out, d_hidden, block_adapter, block_live, owner_slot):
    dp, tensor = lax.axis_index("dp"), lax.axis_index("tensor")
    d_part, hidden_part = tokens.shape[1], gate_up.shape[2]
    blocks = d_hidden.shape[0] // BLOCK_ROWS
    n_rows = blocks * BLOCK_ROWS
    lanes = RANKS * blocks

    swapped = lax.ppermute(tokens, ("dp", "tensor"), SWAP)
    rows = lax.all_gather(swapped, "dp", axis=0, tiled=True).reshape(Z, n_rows, d_part)
    weights = gather_weights(gate_up.reshape(d_part, 2 * hidden_part))

    in_map = lax.dynamic_index_in_dim(adapter_in, block_adapter[dp], 0, False).reshape(RANKS, d_part)
    low_part = lax.dot_general(in_map, tokens, (((1,), (1,)), ((), ())), preferred_element_type=F32)
    per = RANKS // N_TENSOR
    low_sum = lax.all_to_all(low_part.reshape(N_TENSOR, per, BLOCK_ROWS), "tensor", 0, 0, tiled=True).sum(0)
    low_own = lax.ppermute(low_sum.astype(BF16), ("dp", "tensor"), SWAP)
    low = lax.all_to_all(jnp.broadcast_to(low_own[None], (N_DP,) + low_own.shape), "dp", 0, 0, tiled=True)
    low = low.reshape(Z, blocks, per, BLOCK_ROWS).transpose(1, 0, 2, 3).reshape(lanes, BLOCK_ROWS)

    local_ids = lax.dynamic_slice_in_dim(block_adapter, tensor * blocks, blocks, 0)
    local_live = lax.dynamic_slice_in_dim(block_live, tensor * blocks, blocks, 0)
    picked = adapter_out[local_ids]
    out_map = jnp.concatenate([
        jnp.pad(picked[:, 0], ((0, 0), (0, 0), (0, hidden_part))),
        jnp.pad(picked[:, 1], ((0, 0), (0, 0), (hidden_part, 0)))], 1)

    hidden, dlow_part, block_grad = project(local_live, rows, weights, low, out_map, d_hidden)

    shared = lax.all_to_all(
        block_grad.astype(BF16).reshape(blocks, N_TENSOR, per, hidden_part).transpose(1, 0, 2, 3),
        "tensor", 0, 0, tiled=True).reshape(N_TENSOR * blocks, per * hidden_part)
    slot_of = owner_slot[block_adapter]
    picker = (jnp.arange(SLOTS, dtype=jnp.int32)[:, None] == slot_of[None, :]).astype(BF16)
    slotted = jnp.dot(picker, shared, preferred_element_type=F32).astype(BF16)

    local_slot = lax.dynamic_slice_in_dim(slot_of, tensor * blocks, blocks, 0)
    owner = jnp.repeat(local_slot // OWN, RANKS)
    owned = jnp.arange(N_DP, dtype=jnp.int32)[:, None] == owner[None, :]
    dlow_out = jnp.where(owned[:, :, None], dlow_part.astype(BF16)[None], jnp.zeros((), BF16))
    n_slot = OWN * per * hidden_part // BLOCK_ROWS
    sent = jnp.concatenate([slotted.reshape(N_DP, n_slot, BLOCK_ROWS), dlow_out], 1)
    got = lax.all_to_all(sent, "dp", 0, 0, tiled=True)
    dlow = got[:, n_slot:].astype(F32).sum(0)

    mine = (jnp.arange(OWN, dtype=jnp.int32)[:, None] + OWN * dp == local_slot[None, :])
    weighted = jnp.where(mine[:, None, :, None], dlow.reshape(blocks, RANKS, BLOCK_ROWS).transpose(1, 0, 2)[None], 0.0)
    weighted = weighted.reshape(OWN * RANKS, n_rows).astype(BF16)
    in_part = jnp.einsum("mr,zrk->zmk", weighted, rows, preferred_element_type=F32).astype(BF16)

    out_part = got[:, :n_slot].reshape(N_TENSOR, -1, d_part)
    n_in = OWN * RANKS
    last = lax.all_to_all(jnp.concatenate([in_part, out_part], 1), "tensor", 0, 0, tiled=True)
    grad_in = last[:, :n_in].astype(F32).sum(0).reshape(OWN, 2, R, d_part)
    grad_out = last[:, n_in:].reshape(N_TENSOR, Y, OWN, per, hidden_part).transpose(2, 0, 3, 1, 4)
    grad_out = grad_out.reshape(OWN, 2, R, Y * hidden_part).astype(F32)
    return hidden, grad_in, grad_out


def solution(mesh):
    placed = (
        P("dp", "tensor"),
        P("tensor", None, "dp"),
        P(None, None, None, "tensor"),
        P(None, None, None, "dp"),
        P("tensor", "dp"),
        P(),
        P(),
        P(),
    )
    return jax.shard_map(
        body,
        mesh=mesh,
        in_specs=placed,
        out_specs=(P("tensor", "dp"), P("dp", None, None, "tensor"), P("dp", None, None, "tensor")),
        check_vma=False,
    )
```

time: 539 us -> 280 us (0.52)
  blocking collectives: 258 us -> 23.4 us
  waiting for transfers between devices: 206 us -> 92.5 us
  starting transfers between devices: 0.34 us -> 56.3 us
  local copies, waits for them, and re-layouts: 20.5 us -> 60.1 us
  matrix products: 34.6 us -> 7.68 us
  Pallas kernels: 0 us -> 16.6 us
    psum x1 -> x0, blocking collectives: 112 us -> none  [body(): dlow_local = lax.psum(dlow_part, 'dp').astype(jnp.bfloat16)]
    reduce_scatter x3 -> x0, waiting for transfers between devices: 106 us -> none  [the longest x1 96.9 us: body(): lax.psum_scatter(jnp.dot(gathered, weights, preferred_element_type=jnp.fl...]
    all_gather x1, waiting for transfers between devices: 99 us -> 0.01 us  [body(): lax.all_gather(swapped, 'dp', axis=0, tiled=True).reshape(Z, n_rows, d_part)]
    all_to_all x1, blocking collectives: 102 us -> 23.4 us  [body(): lax.all_to_all(jnp.concatenate([in_part, out_part], 1), 'tensor', 0, 0, t...]
    ppermute x0 -> x11, waiting for transfers between devices: none -> 48.1 us  [the longest x1 43.5 us: gather_weights(): left = lax.ppermute(own, 'tensor', shift_x(1))]
    all_to_all x0 -> x4, waiting for transfers between devices: none -> 44.3 us  [the longest x1 31.8 us: body(): got = lax.all_to_all(sent, 'dp', 0, 0, tiled=True)]
    all_gather x1 -> x0, blocking collectives: 43.7 us -> none  [body(): dlow_all = lax.all_gather(dlow_local, 'tensor', axis=0, tiled=True)]
    ppermute x0 -> x11, starting transfers between devices: none -> 36.7 us  [the longest x1 11.5 us: gather_weights(): left = lax.ppermute(own, 'tensor', shift_x(1))]
  transfers between devices with their start and end apart: 4 -> 16, of which waited for: 3 -> 5; matrix products, arithmetic and copies ran while one was open for 7% -> 17% of each run, Pallas kernels for 0% -> 0%
where the time goes in v1:
time: 280 us; the launch traced here: 279 us
  waiting for transfers between devices  92.5 us (33%)
  local copies, waits for them, and re-layouts  60.1 us (21%)
  starting transfers between devices  56.3 us (20%)
  blocking collectives  23.4 us (8%)
  Pallas kernels  16.6 us (6%)
  between operations  16.2 us (6%)
  matrix products  7.68 us (3%)
  other arithmetic  6.26 us (2%)
    ppermute x1, waiting for transfers between devices, gather_weights(): left = lax.ppermute(own, 'tensor', shift_x(1))  43.5 us
    all_to_all x1, waiting for transfers between devices, body(): got = lax.all_to_all(sent, 'dp', 0, 0, tiled=True)  31.8 us
    all_to_all x1, blocking collectives, body(): lax.all_to_all(jnp.concatenate([in_part, out_part], 1), 'tensor', 0, 0, t...  23.4 us
    pallas_call x1, Pallas kernels, project(): pl.pallas_call(block_kernel, grid_spec=pltpu.PrefetchScalarGridSpec(num_s...  16.6 us
    dynamic_update_slice x5, local copies, waits for them, and re-layouts, gather_weights(): full = lax.dynamic_update_slice(full, other[None], (place + 1 - c, row, 0))  11.5 us
    ppermute x1, starting transfers between devices, gather_weights(): left = lax.ppermute(own, 'tensor', shift_x(1))  11.5 us
    dynamic_update_slice x5, local copies, waits for them, and re-layouts, gather_weights(): full = lax.dynamic_update_slice(full, piece[None], (place + c, row, 0))  11.1 us
    all_to_all x1, starting transfers between devices, body(): lax.all_to_all(jnp.broadcast_to(low_own[None], (N_DP,) + low_own.shape),...  8.79 us
  transfers between devices with their start and end apart: 16, of which 5 were waited for; matrix products, arithmetic and copies ran while one was open for 17% of the time, Pallas kernels for 0%

profile of v1, /device:TPU:1, one launch (start us, length us, event | category | flops | bytes accessed | tf_op | source)
XLA Modules:
  0.0 278.9 jit_solution(12335822519146023846)
XLA Ops:
  7.3 5.1 %collective-permute-start = (bf16[128,1024]{1,0:T(8,128)(2,1)}, bf16[128,1024]{1,0:T(8,128)(2,1)S(1)}, u32[]{:S(2)}, u32[]{:S(2)}) collective-permute-start(bf16[128,1024]{1,0:T(8,128)(2,1)} %param.8), channel_id=1, source_target_pairs={{0,0},{1,32},{2,64},{3,96},{4,128},{5,160},{6,192},{7,224},{8,8},{... | collective-permute-start | bytes 786440 | tf_op jit(solution)/shard_map/ppermute | solution.py:128
  12.3 4.6 %collective-permute-done = bf16[128,1024]{1,0:T(8,128)(2,1)S(1)} collective-permute-done((bf16[128,1024]{1,0:T(8,128)(2,1)}, bf16[128,1024]{1,0:T(8,128)(2,1)S(1)}, u32[]{:S(2)}, u32[]{:S(2)}) %collective-permute-start) | collective-permute-done | bytes 262176 | tf_op jit(solution)/shard_map/ppermute | solution.py:128
  17.7 3.5 %copy.28 = bf16[128,8,2,512]{3,1,2,0:T(8,128)(2,1)} copy(bf16[128,8,2,512]{3,2,1,0:T(2,128)(2,1)} %bitcast.59) | data formatting | bytes 4194304
  21.1 11.5 %collective-permute-start.2 = (bf16[1024,1024]{1,0:T(8,128)(2,1)}, bf16[1024,1024]{1,0:T(8,128)(2,1)}, u32[]{:S(2)}, u32[]{:S(2)}) collective-permute-start(bf16[1024,1024]{1,0:T(8,128)(2,1)} %bitcast.30), channel_id=1, source_target_pairs={{0,2},{1,3},{2,4},{3,5},{4,6},{5,7},{6,0},{7,1},{8,10},{9,11},{10,... | collective-permute-start | bytes 6291464 | tf_op jit(solution)/shard_map/ppermute | solution.py:31
  32.6 8.3 %collective-permute-start.4 = (bf16[1024,1024]{1,0:T(8,128)(2,1)}, bf16[1024,1024]{1,0:T(8,128)(2,1)}, u32[]{:S(2)}, u32[]{:S(2)}) collective-permute-start(bf16[1024,1024]{1,0:T(8,128)(2,1)} %bitcast.30), channel_id=1, source_target_pairs={{0,6},{1,7},{2,0},{3,1},{4,2},{5,3},{6,4},{7,5},{8,14},{9,15},{10,... | collective-permute-start | bytes 6291464 | tf_op jit(solution)/shard_map/ppermute | solution.py:32
  43.8 43.5 %collective-permute-done.2 = bf16[1024,1024]{1,0:T(8,128)(2,1)} collective-permute-done((bf16[1024,1024]{1,0:T(8,128)(2,1)}, bf16[1024,1024]{1,0:T(8,128)(2,1)}, u32[]{:S(2)}, u32[]{:S(2)}) %collective-permute-start.2) | collective-permute-done | bytes 2097184 | tf_op jit(solution)/shard_map/ppermute | solution.py:31
  88.6 3.3 %all-to-all-start = ((f32[8,4,128]{2,1,0:T(4,128)}), f32[8,4,128]{2,1,0:T(4,128)S(1)}, u32[]{:S(2)}, u32[]{:S(2)}) async-start(f32[8,4,128]{2,1,0:T(4,128)} %fusion.4), calls=%async_computation | async-start | bytes 32768 | tf_op jit(solution)/shard_map/all_to_all | solution.py:135
  93.0 4.5 %broadcast_in_dim_reshape.4 = bf16[1,1024,1024]{2,1,0:T(8,128)(2,1)} reshape(bf16[1024,2,512]{2,1,0:T(2,128)(2,1)} %param.9) | data formatting | bytes 4194304 | tf_op jit(solution)/shard_map/broadcast_in_dim;reshape | solution.py:40
  99.6 6.0 %broadcast_in_dim.94 = bf16[8,1024,1024]{2,1,0:T(8,128)(2,1)} broadcast(bf16[]{:T(256)} %constant.82.clone.1), dimensions={} | broadcast | bytes 16777218 | tf_op jit(solution)/shard_map/broadcast_in_dim | solution.py:36
  117.7 8.8 %all-to-all-start.1 = ((bf16[32,4,128]{2,1,0:T(4,128)(2,1)}), bf16[32,4,128]{2,1,0:T(4,128)(2,1)S(1)}, u32[]{:S(2)}, u32[]{:S(2)}) async-start(bf16[32,4,128]{2,1,0:T(4,128)(2,1)} %broadcast_in_dim.104), calls=%async_computation.1 | async-start | bytes 65536 | tf_op jit(solution)/shard_map/all_to_all | solution.py:137
  127.3 7.9 %all-to-all-done.1 = bf16[32,4,128]{2,1,0:T(4,128)(2,1)S(1)} async-done(((bf16[32,4,128]{2,1,0:T(4,128)(2,1)}), bf16[32,4,128]{2,1,0:T(4,128)(2,1)S(1)}, u32[]{:S(2)}, u32[]{:S(2)}) %all-to-all-start.1) | async-done | bytes 32800 | tf_op jit(solution)/shard_map/all_to_all | solution.py:137
  135.3 3.1 %bitcast_dynamic-update-slice_fusion.4 = bf16[8,1024,1024]{2,1,0:T(8,128)(2,1)} fusion(bf16[8,1024,1024]{2,1,0:T(8,128)(2,1)} %constant_dynamic-update-slice_fusion, s32[]{:T(128)S(6)} %select_n.99, bf16[1024,1024]{1,0:T(8,128)(2,1)} %collective-permute-done.1), kind=kLoop, calls=%fused_computation.7 | loop fusion | bytes 4194308 | tf_op jit(solution)/shard_map/dynamic_update_slice | solution.py:41
  138.4 3.1 %bitcast_dynamic-update-slice_fusion.3 = bf16[8,1024,1024]{2,1,0:T(8,128)(2,1)} fusion(bf16[8,1024,1024]{2,1,0:T(8,128)(2,1)} %bitcast_dynamic-update-slice_fusion.4, s32[]{:T(128)S(6)} %select_n.101, bf16[1024,1024]{1,0:T(8,128)(2,1)} %collective-permute-done.2), kind=kLoop, calls=%fused_computation.6 | loop fusion | bytes 4194308 | tf_op jit(solution)/shard_map/dynamic_update_slice | solution.py:40
  141.4 5.8 %collective-permute-start.7 = (bf16[512,1024]{1,0:T(8,128)(2,1)S(1)}, bf16[512,1024]{1,0:T(8,128)(2,1)S(1)}, u32[]{:S(2)}, u32[]{:S(2)}) collective-permute-start(bf16[512,1024]{1,0:T(8,128)(2,1)S(1)} %collective-permute-done.6), channel_id=1, source_target_pairs={{0,1},{1,0},{2,3},{3,2},{4,5},{5,4},{6,7},{7,6},{8,9},{9,8},{10,11... | collective-permute-start | bytes 3145736 | tf_op jit(solution)/shard_map/ppermute | solution.py:39
  150.6 3.1 %bitcast_dynamic-update-slice_fusion.1 = bf16[8,1024,1024]{2,1,0:T(8,128)(2,1)} fusion(bf16[8,1024,1024]{2,1,0:T(8,128)(2,1)} %bitcast_dynamic-update-slice_fusion.2, s32[]{:T(128)S(6)} %select_n.104, bf16[1024,1024]{1,0:T(8,128)(2,1)} %collective-permute-done.4), kind=kLoop, calls=%fused_computation.4 | loop fusion | bytes 4194308 | tf_op jit(solution)/shard_map/dynamic_update_slice | solution.py:40
  153.8 3.1 %bitcast_dynamic-update-slice_fusion = bf16[8,1024,1024]{2,1,0:T(8,128)(2,1)} fusion(bf16[8,1024,1024]{2,1,0:T(8,128)(2,1)} %bitcast_dynamic-update-slice_fusion.1, s32[]{:T(128)S(6)} %select_n.105, bf16[1024,1024]{1,0:T(8,128)(2,1)} %collective-permute-done.5), kind=kLoop, calls=%fused_computation.3 | loop fusion | bytes 4194308 | tf_op jit(solution)/shard_map/dynamic_update_slice | solution.py:41
  162.5 3.4 %copy-done.1 = bf16[4096,1024]{1,0:T(8,128)(2,1)S(1)} copy-done((bf16[4096,1024]{1,0:T(8,128)(2,1)S(1)}, bf16[4096,1024]{1,0:T(8,128)(2,1)}, u32[]{:S(2)}) %copy-start.1) | copy-done | bytes 8388632
  165.9 16.6 %shard_map.103 = (bf16[512,512]{1,0:T(8,128)(2,1)}, f32[128,128]{1,0:T(8,128)S(1)}, f32[4,32,512]{2,1,0:T(8,128)S(1)}) custom-call(s32[4]{0:T(128)S(1)} %dynamic_slice.16.live_ref, bf16[8,512,1024]{2,1,0:T(8,128)(2,1)S(1)} %bitcast.57, bf16[8,1024,1024]{2,1,0:T(8,128)(2,1)} %bitcast_dynamic-update-slice_fusion.5.w_ref, bf16[128,128]{1,0:T(8,128)(2,1)S(1)} %bitcast.58, ...), custom_call_target="tpu_custom_call" | custom-call | flops 8589934592 | bytes 25165824 | tf_op jit(solution)/shard_map/pallas_call | solution.py:89
  183.3 3.5 %all-to-all-start.2 = ((bf16[8,4,4,512]{3,2,1,0:T(4,128)(2,1)}), bf16[8,4,4,512]{3,2,1,0:T(4,128)(2,1)S(1)}, u32[]{:S(2)}, u32[]{:S(2)}) async-start(bf16[8,4,4,512]{3,2,1,0:T(4,128)(2,1)} %bitcast.55), calls=%async_computation.2 | async-start | bytes 262144 | tf_op jit(solution)/shard_map/all_to_all | solution.py:149
  187.5 4.6 %all-to-all-done.2 = bf16[8,4,4,512]{3,2,1,0:T(4,128)(2,1)S(1)} async-done(((bf16[8,4,4,512]{3,2,1,0:T(4,128)(2,1)}), bf16[8,4,4,512]{3,2,1,0:T(4,128)(2,1)S(1)}, u32[]{:S(2)}, u32[]{:S(2)}) %all-to-all-start.2) | async-done | bytes 131104 | tf_op jit(solution)/shard_map/all_to_all | solution.py:149
  195.3 4.0 %all-to-all-start.3 = ((bf16[32,160,128]{2,1,0:T(8,128)(2,1)}), bf16[32,160,128]{2,1,0:T(8,128)(2,1)S(1)}, u32[]{:S(2)}, u32[]{:S(2)}) async-start(bf16[32,160,128]{2,1,0:T(8,128)(2,1)} %pad_maximum_fusion), calls=%async_computation.3 | async-start | bytes 2621440 | tf_op jit(solution)/shard_map/all_to_all | solution.py:162
  199.3 31.8 %all-to-all-done.3 = bf16[32,160,128]{2,1,0:T(8,128)(2,1)S(1)} async-done(((bf16[32,160,128]{2,1,0:T(8,128)(2,1)}), bf16[32,160,128]{2,1,0:T(8,128)(2,1)S(1)}, u32[]{:S(2)}, u32[]{:S(2)}) %all-to-all-start.3) | async-done | bytes 1310752 | tf_op jit(solution)/shard_map/all_to_all | solution.py:162
  231.5 6.0 %fusion = bf16[8,64,1024]{2,1,0:T(8,128)(2,1)} fusion(bf16[64,512,1]{1,0,2:T(8,128)(2,1)S(1)} %reshape.147, bf16[8,512,1024]{2,1,0:T(8,128)(2,1)} %bitcast.56), kind=kOutput, calls=%fused_computation.11 | convolution fusion | flops 537395200 | bytes 9502720 | tf_op jit(solution)/shard_map/mr,zrk->zmk/dot_general | solution.py:168
  240.6 23.4 %all_to_all.25 = bf16[8,80,1024]{2,1,0:T(8,128)(2,1)S(1)} all-to-all(bf16[8,80,1024]{2,1,0:T(8,128)(2,1)S(1)} %pad_maximum_fusion.1), channel_id=1, replica_groups=mesh['dp'=32,'tensor'=8] {'tensor'}, dimensions={0} | all-to-all | bytes 2621440 | tf_op jit(solution)/shard_map/all_to_all | solution.py:172
  (88 shorter events, 44.4 us)
Async XLA Ops:
  7.2 36.6 %copy-start = (bf16[32,2,16,1024]{3,2,1,0:T(8,128)(2,1)S(1)}, bf16[32,2,16,1024]{3,2,1,0:T(8,128)(2,1)}, u32[]{:S(2)}) copy-start(bf16[32,2,16,1024]{3,2,1,0:T(8,128)(2,1)} %param.10) | copy-start | bytes 6291460
  7.2 80.7 %copy-start.7 = (bf16[128,1024]{1,0:T(8,128)(2,1)S(1)}, bf16[128,1024]{1,0:T(8,128)(2,1)}, u32[]{:S(2)}) copy-start(bf16[128,1024]{1,0:T(8,128)(2,1)} %param.8) | copy-start | bytes 786436
  7.2 34.0 %copy-start.6 = (s32[32]{0:T(128)S(1)}, s32[32]{0:T(128)}, u32[]{:S(2)}) copy-start(s32[32]{0:T(128)} %param.13) | copy-start | bytes 388
  7.2 84.8 %copy-start.3 = (s32[32]{0:T(128)S(1)}, s32[32]{0:T(128)}, u32[]{:S(2)}) copy-start(s32[32]{0:T(128)} %param.15) | copy-start | bytes 388
  7.2 155.3 %all-gather.2.cloned.1.call-start = ((), (), s32[]{:S(2)}) async-start(), calls=%async_computation.5 | async-start | bytes 8650752 | tf_op jit(solution)/shard_map/all_gather | solution.py:129
  7.3 9.7 %collective-permute-start = (bf16[128,1024]{1,0:T(8,128)(2,1)}, bf16[128,1024]{1,0:T(8,128)(2,1)S(1)}, u32[]{:S(2)}, u32[]{:S(2)}) collective-permute-start(bf16[128,1024]{1,0:T(8,128)(2,1)} %param.8), channel_id=1, source_target_pairs={{0,0},{1,32},{2,64},{3,96},{4,128},{5,160},{6,192},{7,224},{8,8},{... | collective-permute-start | bytes 786440 | tf_op jit(solution)/shard_map/ppermute | solution.py:128
  21.1 66.1 %collective-permute-start.2 = (bf16[1024,1024]{1,0:T(8,128)(2,1)}, bf16[1024,1024]{1,0:T(8,128)(2,1)}, u32[]{:S(2)}, u32[]{:S(2)}) collective-permute-start(bf16[1024,1024]{1,0:T(8,128)(2,1)} %bitcast.30), channel_id=1, source_target_pairs={{0,2},{1,3},{2,4},{3,5},{4,6},{5,7},{6,0},{7,1},{8,10},{9,11},{10,... | collective-permute-start | bytes 6291464 | tf_op jit(solution)/shard_map/ppermute | solution.py:31
  32.6 60.3 %collective-permute-start.4 = (bf16[1024,1024]{1,0:T(8,128)(2,1)}, bf16[1024,1024]{1,0:T(8,128)(2,1)}, u32[]{:S(2)}, u32[]{:S(2)}) collective-permute-start(bf16[1024,1024]{1,0:T(8,128)(2,1)} %bitcast.30), channel_id=1, source_target_pairs={{0,6},{1,7},{2,0},{3,1},{4,2},{5,3},{6,4},{7,5},{8,14},{9,15},{10,... | collective-permute-start | bytes 6291464 | tf_op jit(solution)/shard_map/ppermute | solution.py:32
  40.9 94.3 %collective-permute-start.1 = (bf16[1024,1024]{1,0:T(8,128)(2,1)}, bf16[1024,1024]{1,0:T(8,128)(2,1)}, u32[]{:S(2)}, u32[]{:S(2)}) collective-permute-start(bf16[1024,1024]{1,0:T(8,128)(2,1)} %bitcast.30), channel_id=1, source_target_pairs={{0,1},{1,0},{2,3},{3,2},{4,5},{5,4},{6,7},{7,6},{8,9},{9,8},{10,11... | collective-permute-start | bytes 6291464 | tf_op jit(solution)/shard_map/ppermute | solution.py:39
  87.3 60.3 %collective-permute-start.3 = (bf16[1024,1024]{1,0:T(8,128)(2,1)}, bf16[1024,1024]{1,0:T(8,128)(2,1)}, u32[]{:S(2)}, u32[]{:S(2)}) collective-permute-start(bf16[1024,1024]{1,0:T(8,128)(2,1)} %collective-permute-done.2), channel_id=1, source_target_pairs={{0,1},{1,0},{2,3},{3,2},{4,5},{5,4},{6,7},{7,6},{8,9},{9,8},{10,11... | collective-permute-start | bytes 6291464 | tf_op jit(solution)/shard_map/ppermute | solution.py:39
  88.6 8.8 %all-to-all-start = ((f32[8,4,128]{2,1,0:T(4,128)}), f32[8,4,128]{2,1,0:T(4,128)S(1)}, u32[]{:S(2)}, u32[]{:S(2)}) async-start(f32[8,4,128]{2,1,0:T(4,128)} %fusion.4), calls=%async_computation | async-start | bytes 32768 | tf_op jit(solution)/shard_map/all_to_all | solution.py:135
  92.9 60.9 %collective-permute-start.5 = (bf16[1024,1024]{1,0:T(8,128)(2,1)}, bf16[1024,1024]{1,0:T(8,128)(2,1)}, u32[]{:S(2)}, u32[]{:S(2)}) collective-permute-start(bf16[1024,1024]{1,0:T(8,128)(2,1)} %collective-permute-done.4), channel_id=1, source_target_pairs={{0,1},{1,0},{2,3},{3,2},{4,5},{5,4},{6,7},{7,6},{8,9},{9,8},{10,11... | collective-permute-start | bytes 6291464 | tf_op jit(solution)/shard_map/ppermute | solution.py:39
  97.5 8.1 %copy-start.4 = (bf16[1,1024,1024]{2,1,0:T(8,128)(2,1)S(1)}, bf16[1,1024,1024]{2,1,0:T(8,128)(2,1)}, u32[]{:S(2)}) copy-start(bf16[1,1024,1024]{2,1,0:T(8,128)(2,1)} %broadcast_in_dim_reshape.4) | copy-start | bytes 6291460
  97.5 16.9 %collective-permute-start.10 = (bf16[4,128]{1,0:T(4,128)(2,1)S(1)}, bf16[4,128]{1,0:T(4,128)(2,1)S(1)}, u32[]{:S(2)}, u32[]{:S(2)}) collective-permute-start(bf16[4,128]{1,0:T(4,128)(2,1)S(1)} %reduce_sum.27), channel_id=1, source_target_pairs={{0,0},{1,32},{2,64},{3,96},{4,128},{5,160},{6,192},{7,224},{8,8},{... | collective-permute-start | bytes 3080 | tf_op jit(solution)/shard_map/ppermute | solution.py:136
  107.0 7.5 %copy-start.8 = (s32[32]{0:T(128)S(1)}, s32[32]{0:T(128)}, u32[]{:S(2)}) copy-start(s32[32]{0:T(128)} %param.14) | copy-start | bytes 388
  109.4 32.1 %collective-permute-start.6 = (bf16[512,1024]{1,0:T(8,128)(2,1)}, bf16[512,1024]{1,0:T(8,128)(2,1)S(1)}, u32[]{:S(2)}, u32[]{:S(2)}) collective-permute-start(bf16[512,1024]{1,0:T(8,128)(2,1)} %slice.36), channel_id=1, source_target_pairs={{0,2},{1,3},{2,4},{3,5},{4,6},{5,7},{6,0},{7,1},{8,10},{9,11},{10,... | collective-permute-start | bytes 3145736 | tf_op jit(solution)/shard_map/ppermute | solution.py:33
  114.4 32.9 %collective-permute-start.8 = (bf16[512,1024]{1,0:T(8,128)(2,1)}, bf16[512,1024]{1,0:T(8,128)(2,1)}, u32[]{:S(2)}, u32[]{:S(2)}) collective-permute-start(bf16[512,1024]{1,0:T(8,128)(2,1)} %slice.37), channel_id=1, source_target_pairs={{0,6},{1,7},{2,0},{3,1},{4,2},{5,3},{6,4},{7,5},{8,14},{9,15},{10,... | collective-permute-start | bytes 3145736 | tf_op jit(solution)/shard_map/ppermute | solution.py:34
  117.7 17.5 %all-to-all-start.1 = ((bf16[32,4,128]{2,1,0:T(4,128)(2,1)}), bf16[32,4,128]{2,1,0:T(4,128)(2,1)S(1)}, u32[]{:S(2)}, u32[]{:S(2)}) async-start(bf16[32,4,128]{2,1,0:T(4,128)(2,1)} %broadcast_in_dim.104), calls=%async_computation.1 | async-start | bytes 65536 | tf_op jit(solution)/shard_map/all_to_all | solution.py:137
  141.4 16.5 %collective-permute-start.7 = (bf16[512,1024]{1,0:T(8,128)(2,1)S(1)}, bf16[512,1024]{1,0:T(8,128)(2,1)S(1)}, u32[]{:S(2)}, u32[]{:S(2)}) collective-permute-start(bf16[512,1024]{1,0:T(8,128)(2,1)S(1)} %collective-permute-done.6), channel_id=1, source_target_pairs={{0,1},{1,0},{2,3},{3,2},{4,5},{5,4},{6,7},{7,6},{8,9},{9,8},{10,11... | collective-permute-start | bytes 3145736 | tf_op jit(solution)/shard_map/ppermute | solution.py:39
  147.3 14.2 %collective-permute-start.9 = (bf16[512,1024]{1,0:T(8,128)(2,1)}, bf16[512,1024]{1,0:T(8,128)(2,1)S(1)}, u32[]{:S(2)}, u32[]{:S(2)}) collective-permute-start(bf16[512,1024]{1,0:T(8,128)(2,1)} %collective-permute-done.8), channel_id=1, source_target_pairs={{0,1},{1,0},{2,3},{3,2},{4,5},{5,4},{6,7},{7,6},{8,9},{9,8},{10,11... | collective-permute-start | bytes 3145736 | tf_op jit(solution)/shard_map/ppermute | solution.py:39
  159.1 3.4 %copy-start.2 = (bf16[512,512]{1,0:T(8,128)(2,1)S(1)}, bf16[512,512]{1,0:T(8,128)(2,1)}, u32[]{:S(2)}) copy-start(bf16[512,512]{1,0:T(8,128)(2,1)} %cot_ref.1) | copy-start | bytes 1572868
  162.5 3.4 %copy-start.1 = (bf16[4096,1024]{1,0:T(8,128)(2,1)S(1)}, bf16[4096,1024]{1,0:T(8,128)(2,1)}, u32[]{:S(2)}) copy-start(bf16[4096,1024]{1,0:T(8,128)(2,1)} %all-gather.2.cloned.1.call-done) | copy-start | bytes 25165828
  183.3 8.8 %all-to-all-start.2 = ((bf16[8,4,4,512]{3,2,1,0:T(4,128)(2,1)}), bf16[8,4,4,512]{3,2,1,0:T(4,128)(2,1)S(1)}, u32[]{:S(2)}, u32[]{:S(2)}) async-start(bf16[8,4,4,512]{3,2,1,0:T(4,128)(2,1)} %bitcast.55), calls=%async_computation.2 | async-start | bytes 262144 | tf_op jit(solution)/shard_map/all_to_all | solution.py:149
  195.3 35.9 %all-to-all-start.3 = ((bf16[32,160,128]{2,1,0:T(8,128)(2,1)}), bf16[32,160,128]{2,1,0:T(8,128)(2,1)S(1)}, u32[]{:S(2)}, u32[]{:S(2)}) async-start(bf16[32,160,128]{2,1,0:T(8,128)(2,1)} %pad_maximum_fusion), calls=%async_computation.3 | async-start | bytes 2621440 | tf_op jit(solution)/shard_map/all_to_all | solution.py:162
  (1 other events, 0.7 us)
Sparse Core Ops, SparseCore 0:
  17.8 115.6 all-gather.1

commit v2 on v0

v2 whole, which is shorter than its diff:
```python
import jax
import jax.numpy as jnp
from jax import lax
from jax.experimental import pallas as pl
from jax.experimental.pallas import tpu as pltpu
from jax.sharding import Mesh, PartitionSpec as P

R = 16
RANKS = 2 * R
BLOCK_ROWS = 128
HEAD = 64
Z, Y, X, C = 8, 4, 4, 2
N_DP, N_TENSOR = Z * Y, X * C
OWN = 2
SLOTS = OWN * N_DP
DP, TENSOR = ("z", "y"), ("x", "c")
BF16, F32 = jnp.bfloat16, jnp.float32
VMEM_LIMIT = 48 * 2 ** 20


def swap(skew):
    return [((z * Y + y) * N_TENSOR + t, (((t + skew * z) % Z) * Y + y) * N_TENSOR + z)
            for z in range(Z) for y in range(Y) for t in range(N_TENSOR)]


def exchange(x, axes):
    return lax.all_to_all(x, axes, 0, 0, tiled=True)


def spread(x, axis, n):
    return exchange(jnp.broadcast_to(x[None], (n,) + x.shape), axis)


def ring(x, axis, n):
    def send(v, step):
        return lax.ppermute(v, axis, [(i, (i + step) % n) for i in range(n)])

    half = x.shape[0] // 2
    pieces, up, down = [(0, None, x)], x, x
    for back in range(1, n // 2):
        up, down = send(up, 1), send(down, -1)
        pieces += [(back, None, up), (n - back, None, down)]
    return pieces + [(n // 2, 0, send(up[:half], 1)), (n // 2, 1, send(down[half:], -1))]


def block_kernel(n_head, heads, tails, where_ref, *refs):
    pieces, refs = refs[:len(heads) + len(tails)], refs[len(heads) + len(tails):]
    (w_ref, low_ref, out_map_ref, cot_ref, rows_ref, hidden_ref, dlow_ref, grad_ref,
     x_buf, w_buf, acc_ref, x_sem, w_sem, out_sem) = refs
    parts, blocks, _, depth = x_buf.shape
    z, y, t = where_ref[0], where_ref[1], where_ref[2]

    def feature(k):
        return lax.rem(k - t + parts, parts)

    loads = []
    for i, (back, part) in enumerate(heads):
        at = lax.rem(z - back + parts, parts)
        span = slice(0, blocks) if part is None else slice(part * blocks // 2, (part + 1) * blocks // 2)
        loads.append((pieces[i], x_buf.at[at, span, pl.ds(0, n_head)]))
    for i, (back, part) in enumerate(tails):
        at = lax.rem(y - back + blocks, blocks)
        span = slice(0, parts) if part is None else slice(part * parts // 2, (part + 1) * parts // 2)
        loads.append((pieces[len(heads) + i], x_buf.at[span, at, pl.ds(n_head, BLOCK_ROWS - n_head)]))
    loads = [pltpu.make_async_copy(src, dst, x_sem.at[i]) for i, (src, dst) in enumerate(loads)]
    for load in loads:
        load.start()

    def weight(k):
        return pltpu.make_async_copy(w_ref.at[feature(k)], w_buf.at[k], w_sem.at[k])

    def keep(k):
        return pltpu.make_async_copy(x_buf.at[k], rows_ref.at[feature(k)], out_sem.at[k])

    @pl.loop(0, parts)
    def _(k):
        weight(k).start()

    acc_ref[...] = jnp.zeros_like(acc_ref)
    for load in loads:
        load.wait()

    @pl.loop(0, parts)
    def _(k):
        weight(k).wait()
        keep(k).start()
        rows = x_buf[k].reshape(blocks * BLOCK_ROWS, depth)
        acc_ref[...] += jnp.dot(rows, w_buf[k], preferred_element_type=F32)

    half = cot_ref.shape[1]
    for b in range(blocks):
        rows = slice(b * BLOCK_ROWS, (b + 1) * BLOCK_ROWS)
        ranks = slice(b * RANKS, (b + 1) * RANKS)
        low = low_ref[ranks, :]
        out_map = out_map_ref[b]
        pre = acc_ref[rows, :] + lax.dot_general(
            low, out_map, (((0,), (0,)), ((), ())), preferred_element_type=F32)
        gate, up = pre[:, :half], pre[:, half:]
        sigma = jax.nn.sigmoid(gate)
        gated = gate * sigma
        hidden_ref[rows, :] = (gated * up).astype(BF16)
        live = lax.broadcasted_iota(jnp.int32, (BLOCK_ROWS, half), 0) < where_ref[3 + b]
        cotan = jnp.where(live, cot_ref[rows, :].astype(F32), 0.0)
        dgate = cotan * up * sigma * (1.0 + gate * (1.0 - sigma))
        dup = cotan * gated
        dpre = jnp.concatenate([dgate, dup], 1).astype(BF16)
        dlow_ref[ranks, :] = lax.dot_general(
            out_map, dpre, (((1,), (1,)), ((), ())), preferred_element_type=F32)
        grad = jnp.dot(low, dpre, preferred_element_type=F32)
        grad_ref[b, :R, :] = grad[:R, :half].astype(BF16)
        grad_ref[b, R:, :] = grad[R:, half:].astype(BF16)

    @pl.loop(0, parts)
    def _(k):
        keep(k).wait()


def project(where, heads, tails, weights, low, out_map, cotan):
    parts, depth, width = weights.shape
    n_rows, half = cotan.shape
    blocks = n_rows // BLOCK_ROWS
    n_head = heads[0][2].shape[-2]
    any_spec = pl.BlockSpec(memory_space=pl.ANY)
    vmem_spec = pl.BlockSpec(memory_space=pltpu.VMEM)
    n_pieces = len(heads) + len(tails)

    def kernel(*refs):
        block_kernel(n_head, [h[:2] for h in heads], [t[:2] for t in tails], *refs)

    return pl.pallas_call(
        kernel,
        in_specs=[pl.BlockSpec(memory_space=pltpu.SMEM)] + [any_spec] * (n_pieces + 1) + [vmem_spec] * 3,
        out_specs=[any_spec, vmem_spec, vmem_spec, vmem_spec],
        out_shape=[
            jax.ShapeDtypeStruct((parts, blocks, BLOCK_ROWS, depth), BF16),
            jax.ShapeDtypeStruct((n_rows, half), BF16),
            jax.ShapeDtypeStruct(low.shape, F32),
            jax.ShapeDtypeStruct((blocks, RANKS, half), BF16),
        ],
        scratch_shapes=[
            pltpu.VMEM((parts, blocks, BLOCK_ROWS, depth), BF16),
            pltpu.VMEM((parts, depth, width), BF16),
            pltpu.VMEM((n_rows, width), F32),
            pltpu.SemaphoreType.DMA((n_pieces,)),
            pltpu.SemaphoreType.DMA((parts,)),
            pltpu.SemaphoreType.DMA((parts,)),
        ],
        compiler_params=pltpu.CompilerParams(vmem_limit_bytes=VMEM_LIMIT),
        cost_estimate=pl.CostEstimate(
            flops=2 * parts * n_rows * depth * width,
            bytes_accessed=2 * parts * depth * (2 * n_rows + width),
            transcendentals=n_rows * half),
    )(where, *[h[2] for h in heads], *[t[2] for t in tails], weights, low, out_map, cotan)


def in_grad_kernel(mine_ref, dlow_ref, rows_ref, out_ref, left_ref):
    blocks = rows_ref.shape[1]

    @pl.when(pl.program_id(0) == 0)
    def _():
        for s in range(OWN):
            for b in range(blocks):
                picked = dlow_ref[b * RANKS:(b + 1) * RANKS, :].astype(F32)
                picked = jnp.where(mine_ref[s * blocks + b] == 1, picked, 0.0)
                left_ref[s * RANKS:(s + 1) * RANKS, b * BLOCK_ROWS:(b + 1) * BLOCK_ROWS] = picked.astype(BF16)

    rows = rows_ref[0].reshape(blocks * BLOCK_ROWS, rows_ref.shape[3])
    out_ref[0] = jnp.dot(left_ref[...], rows, preferred_element_type=F32).astype(BF16)


def in_grad(mine, dlow, rows):
    parts, blocks, _, depth = rows.shape
    n_out, n_rows = OWN * RANKS, blocks * BLOCK_ROWS
    return pl.pallas_call(
        in_grad_kernel,
        grid_spec=pltpu.PrefetchScalarGridSpec(
            num_scalar_prefetch=1,
            grid=(parts,),
            in_specs=[
                pl.BlockSpec(dlow.shape, lambda k, s: (0, 0)),
                pl.BlockSpec((1,) + rows.shape[1:], lambda k, s: (k, 0, 0, 0)),
            ],
            out_specs=pl.BlockSpec((1, n_out, depth), lambda k, s: (k, 0, 0)),
            scratch_shapes=[pltpu.VMEM((n_out, n_rows), BF16)],
        ),
        out_shape=jax.ShapeDtypeStruct((parts, n_out, depth), BF16),
        compiler_params=pltpu.CompilerParams(vmem_limit_bytes=VMEM_LIMIT),
        cost_estimate=pl.CostEstimate(
            flops=2 * parts * n_out * n_rows * depth,
            bytes_accessed=2 * parts * depth * (n_rows + n_out), transcendentals=0),
    )(mine, dlow, rows)


def out_grad_kernel(got_ref, out_ref):
    parts, quarters, _, width = got_ref.shape
    per = RANKS // parts
    for p in range(parts):
        for q in range(quarters):
            piece = got_ref[p, q].astype(F32)
            for s in range(OWN):
                out_ref[s, p * per:(p + 1) * per, q * width:(q + 1) * width] = piece[s * per:(s + 1) * per]


def body(tokens, gate_up, adapter_in, adapter_out, d_hidden, block_adapter, block_live, owner_slot):
    z, y = lax.axis_index("z"), lax.axis_index("y")
    dp, tensor = lax.axis_index(DP), lax.axis_index(TENSOR)
    d_part, hidden_part = tokens.shape[1], gate_up.shape[2]
    blocks = d_hidden.shape[0] // BLOCK_ROWS
    lanes = RANKS * blocks
    per = RANKS // N_TENSOR

    weights = lax.all_gather(gate_up.reshape(d_part, 2 * hidden_part), TENSOR, axis=0, tiled=False)

    swapped = lax.ppermute(tokens, DP + TENSOR, swap(1))
    heads = ring(spread(swapped[:HEAD], "y", Y), "z", Z)
    tails = ring(spread(swapped[HEAD:], "z", Z), "y", Y)

    in_map = lax.dynamic_index_in_dim(adapter_in, block_adapter[dp], 0, False).reshape(RANKS, d_part)
    low_part = lax.dot_general(in_map, tokens, (((1,), (1,)), ((), ())), preferred_element_type=F32)
    low_sum = exchange(low_part.reshape(N_TENSOR, per, BLOCK_ROWS), TENSOR).sum(0)
    low_own = lax.ppermute(low_sum.astype(BF16), DP + TENSOR, swap(0))
    low = spread(low_own, DP, N_DP).reshape(Z, Y, per, BLOCK_ROWS)
    low = low.transpose(1, 0, 2, 3).reshape(lanes, BLOCK_ROWS)

    local_ids = lax.dynamic_slice_in_dim(block_adapter, tensor * blocks, blocks, 0)
    local_live = lax.dynamic_slice_in_dim(block_live, tensor * blocks, blocks, 0)
    picked = adapter_out[local_ids]
    out_map = jnp.concatenate([
        jnp.pad(picked[:, 0], ((0, 0), (0, 0), (0, hidden_part))),
        jnp.pad(picked[:, 1], ((0, 0), (0, 0), (hidden_part, 0)))], 1)
    where = jnp.concatenate([jnp.stack([z, y, tensor]).astype(jnp.int32), local_live])

    rows, hidden, dlow_part, block_grad = project(where, heads, tails, weights, low, out_map, d_hidden)

    slot_of = owner_slot[block_adapter]
    local_slot = lax.dynamic_slice_in_dim(slot_of, tensor * blocks, blocks, 0)
    mine = jnp.arange(OWN, dtype=jnp.int32)[:, None] + OWN * dp == local_slot[None, :]

    dlow_sum = exchange(dlow_part.reshape(N_DP, lanes // N_DP, BLOCK_ROWS), DP).sum(0).astype(BF16)
    dlow = spread(dlow_sum, DP, N_DP).reshape(lanes, BLOCK_ROWS)
    in_part = in_grad(mine.reshape(-1).astype(jnp.int32), dlow, rows)
    grad_in = exchange(in_part, TENSOR).astype(F32).sum(0).reshape(OWN, 2, R, d_part)

    shared = exchange(
        block_grad.reshape(blocks, N_TENSOR, per, hidden_part).transpose(1, 0, 2, 3), TENSOR)
    picker = (jnp.arange(SLOTS, dtype=jnp.int32)[:, None] == slot_of[None, :]).astype(BF16)
    slotted = jnp.dot(picker, shared.reshape(N_TENSOR * blocks, per * hidden_part), preferred_element_type=F32)
    got = exchange(slotted.astype(BF16).reshape(N_DP, OWN * per, hidden_part), DP)
    got = exchange(got.reshape(N_TENSOR, Y, OWN * per, hidden_part), TENSOR)
    grad_out = pl.pallas_call(
        out_grad_kernel,
        out_shape=jax.ShapeDtypeStruct((OWN, RANKS, Y * hidden_part), F32),
    )(got).reshape(OWN, 2, R, Y * hidden_part)
    return hidden, grad_in, grad_out


def solution(mesh):
    mesh = Mesh(mesh.devices.reshape(Z, Y, X, C), DP + TENSOR)

    return jax.shard_map(
        body,
        mesh=mesh,
        in_specs=(P(DP, TENSOR), P(TENSOR, None, DP), P(None, None, None, TENSOR), P(None, None, None, DP),
                  P(TENSOR, DP), P(), P(), P()),
        out_specs=(P(TENSOR, DP), P(DP, None, None, TENSOR), P(DP, None, None, TENSOR)),
        check_vma=False,
    )
```

time: 539 us -> 274 us (0.51)
  blocking collectives: 258 us -> 23.5 us
  waiting for transfers between devices: 206 us -> 94.5 us
  starting transfers between devices: 0.34 us -> 85.3 us
  matrix products: 34.6 us -> 1.01 us
  Pallas kernels: 0 us -> 27.6 us
    psum x1 -> x0, blocking collectives: 112 us -> none  [body(): dlow_local = lax.psum(dlow_part, 'dp').astype(jnp.bfloat16)]
    reduce_scatter x3 -> x0, waiting for transfers between devices: 106 us -> none  [the longest x1 96.9 us: body(): lax.psum_scatter(jnp.dot(gathered, weights, preferred_element_type=jnp.fl...]
    all_gather x1, waiting for transfers between devices: 99 us -> 0.02 us  [body(): lax.all_gather(gate_up.reshape(d_part, 2 * hidden_part), TENSOR, axis=0,...]
    all_to_all x1 -> x2, blocking collectives: 102 us -> 23.5 us  [exchange(): return lax.all_to_all(x, axes, 0, 0, tiled=True)]
    all_to_all x0 -> x8, waiting for transfers between devices: none -> 70.8 us  [exchange(): return lax.all_to_all(x, axes, 0, 0, tiled=True)]
    all_to_all x0 -> x8, starting transfers between devices: none -> 67.3 us  [exchange(): return lax.all_to_all(x, axes, 0, 0, tiled=True)]
    all_gather x1 -> x0, blocking collectives: 43.7 us -> none  [body(): dlow_all = lax.all_gather(dlow_local, 'tensor', axis=0, tiled=True)]
    dot_general x7 -> x2, matrix products: 34.6 us -> 1.01 us  [the longest x1 0.81 us: body(): lax.dot_general(in_map, tokens, (((1,), (1,)), ((), ())), preferred_eleme...]
  transfers between devices with their start and end apart: 4 -> 23, of which waited for: 3 -> 12; matrix products, arithmetic and copies ran while one was open for 7% -> 5% of each run, Pallas kernels for 0% -> 4%
where the time goes in v2:
time: 274 us; the launch traced here: 273 us
  waiting for transfers between devices  94.5 us (34%)
  starting transfers between devices  85.3 us (31%)
  Pallas kernels  27.6 us (10%)
  blocking collectives  23.5 us (9%)
  local copies, waits for them, and re-layouts  22.3 us (8%)
  between operations  16.2 us (6%)
    all_to_all x8, waiting for transfers between devices, exchange(): return lax.all_to_all(x, axes, 0, 0, tiled=True)  70.8 us
    all_to_all x8, starting transfers between devices, exchange(): return lax.all_to_all(x, axes, 0, 0, tiled=True)  67.3 us
    all_to_all x2, blocking collectives, exchange(): return lax.all_to_all(x, axes, 0, 0, tiled=True)  23.5 us
    pallas_call x1, Pallas kernels, project(): pl.pallas_call(kernel, in_specs=[pl.BlockSpec(memory_space=pltpu.SMEM)] +...  17.5 us
    ppermute x12, waiting for transfers between devices, send(): return lax.ppermute(v, axis, [(i, (i + step) % n) for i in range(n)])  14.9 us
    ppermute x12, starting transfers between devices, send(): return lax.ppermute(v, axis, [(i, (i + step) % n) for i in range(n)])  11.1 us
    pallas_call x1, Pallas kernels, in_grad(): pl.pallas_call(in_grad_kernel, grid_spec=pltpu.PrefetchScalarGridSpec(num...  8.3 us
    ppermute x1, waiting for transfers between devices, body(): swapped = lax.ppermute(tokens, DP + TENSOR, swap(1))  5.5 us
  transfers between devices with their start and end apart: 23, of which 12 were waited for; matrix products, arithmetic and copies ran while one was open for 5% of the time, Pallas kernels for 4%

profile of v2, /device:TPU:1, one launch (start us, length us, event | category | flops | bytes accessed | tf_op | source)
XLA Modules:
  0.0 272.9 jit_solution(8038498620730441450)
XLA Ops:
  7.2 4.6 %all_gather_reshape.3 = bf16[1,1024,1024]{2,1,0:T(8,128)(2,1)} reshape(bf16[1024,2,512]{2,1,0:T(2,128)(2,1)} %param.9) | data formatting | bytes 4194304 | tf_op jit(solution)/shard_map/all_gather;reshape | solution.py:212
  12.7 4.9 %collective-permute-start = (bf16[128,1024]{1,0:T(8,128)(2,1)S(1)}, bf16[128,1024]{1,0:T(8,128)(2,1)S(1)}, u32[]{:S(2)}, u32[]{:S(2)}) collective-permute-start(bf16[128,1024]{1,0:T(8,128)(2,1)S(1)} %copy-done.7), channel_id=1, source_target_pairs={{0,0},{1,32},{2,64},{3,96},{4,128},{5,160},{6,192},{7,224},{8,8},{... | collective-permute-start | bytes 786440 | tf_op jit(solution)/shard_map/ppermute | solution.py:214
  17.7 5.5 %collective-permute-done = bf16[128,1024]{1,0:T(8,128)(2,1)S(1)} collective-permute-done((bf16[128,1024]{1,0:T(8,128)(2,1)S(1)}, bf16[128,1024]{1,0:T(8,128)(2,1)S(1)}, u32[]{:S(2)}, u32[]{:S(2)}) %collective-permute-start) | collective-permute-done | bytes 262176 | tf_op jit(solution)/shard_map/ppermute | solution.py:214
  23.3 11.0 %all_to_all.50.refs_1_ = bf16[4,64,1024]{2,1,0:T(8,128)(2,1)S(1)} all-to-all(bf16[4,64,1024]{2,1,0:T(8,128)(2,1)S(1)} %broadcast_in_dim.12), channel_id=1, replica_groups=mesh['z'=8,'y'=4,'x'=4,'c'=2] {'y'}, dimensions={0} | all-to-all | bytes 1048576 | tf_op jit(solution)/shard_map/all_to_all | solution.py:27
  35.4 20.2 %all-to-all-start.1 = ((bf16[8,64,1024]{2,1,0:T(8,128)(2,1)}), bf16[8,64,1024]{2,1,0:T(8,128)(2,1)}, u32[]{:S(2)}, u32[]{:S(2)}) async-start(bf16[8,64,1024]{2,1,0:T(8,128)(2,1)} %broadcast_in_dim.13), calls=%async_computation.1 | async-start | bytes 2097152 | tf_op jit(solution)/shard_map/all_to_all | solution.py:27
  58.4 22.8 %all-to-all-done.1.refs_10_ = bf16[8,64,1024]{2,1,0:T(8,128)(2,1)} async-done(((bf16[8,64,1024]{2,1,0:T(8,128)(2,1)}), bf16[8,64,1024]{2,1,0:T(8,128)(2,1)}, u32[]{:S(2)}, u32[]{:S(2)}) %all-to-all-start.1) | async-done | bytes 1048608 | tf_op jit(solution)/shard_map/all_to_all | solution.py:27
  82.6 5.9 %collective-permute-done.2.refs_3_ = bf16[4,64,1024]{2,1,0:T(8,128)(2,1)S(1)} collective-permute-done((bf16[4,64,1024]{2,1,0:T(8,128)(2,1)S(1)}, bf16[4,64,1024]{2,1,0:T(8,128)(2,1)S(1)}, u32[]{:S(2)}, u32[]{:S(2)}) %collective-permute-start.2) | collective-permute-done | bytes 524320 | tf_op jit(solution)/shard_map/ppermute | solution.py:36
  94.5 5.3 %collective-permute-done.4.refs_5_ = bf16[4,64,1024]{2,1,0:T(8,128)(2,1)} collective-permute-done((bf16[4,64,1024]{2,1,0:T(8,128)(2,1)S(1)}, bf16[4,64,1024]{2,1,0:T(8,128)(2,1)}, u32[]{:S(2)}, u32[]{:S(2)}) %collective-permute-start.4) | collective-permute-done | bytes 524320 | tf_op jit(solution)/shard_map/ppermute | solution.py:36
  104.7 9.2 %all-to-all-start.2 = ((f32[8,4,128]{2,1,0:T(4,128)}), f32[8,4,128]{2,1,0:T(4,128)S(1)}, u32[]{:S(2)}, u32[]{:S(2)}) async-start(f32[8,4,128]{2,1,0:T(4,128)} %fusion.3), calls=%async_computation.2 | async-start | bytes 32768 | tf_op jit(solution)/shard_map/all_to_all | solution.py:27
  128.0 3.3 %collective-permute-done.13 = bf16[4,128]{1,0:T(4,128)(2,1)S(1)} collective-permute-done((bf16[4,128]{1,0:T(4,128)(2,1)S(1)}, bf16[4,128]{1,0:T(4,128)(2,1)S(1)}, u32[]{:S(2)}, u32[]{:S(2)}) %collective-permute-start.13) | collective-permute-done | bytes 1056 | tf_op jit(solution)/shard_map/ppermute | solution.py:221
  131.9 13.1 %all-to-all-start.3 = ((bf16[32,4,128]{2,1,0:T(4,128)(2,1)}), bf16[32,4,128]{2,1,0:T(4,128)(2,1)S(1)}, u32[]{:S(2)}, u32[]{:S(2)}) async-start(bf16[32,4,128]{2,1,0:T(4,128)(2,1)} %broadcast_in_dim.14), calls=%async_computation.3 | async-start | bytes 65536 | tf_op jit(solution)/shard_map/all_to_all | solution.py:27
  145.1 8.4 %all-to-all-done.3 = bf16[32,4,128]{2,1,0:T(4,128)(2,1)S(1)} async-done(((bf16[32,4,128]{2,1,0:T(4,128)(2,1)}), bf16[32,4,128]{2,1,0:T(4,128)(2,1)S(1)}, u32[]{:S(2)}, u32[]{:S(2)}) %all-to-all-start.3) | async-done | bytes 32800 | tf_op jit(solution)/shard_map/all_to_all | solution.py:27
  156.0 17.5 %shard_map.103 = (bf16[8,4,128,1024]{3,2,1,0:T(8,128)(2,1)}, bf16[512,512]{1,0:T(8,128)(2,1)}, f32[128,128]{1,0:T(8,128)S(1)}, bf16[4,32,512]{2,1,0:T(8,128)(2,1)S(1)}) custom-call(s32[7]{0:T(128)S(1)} %pad_add_fusion.refs_0_, bf16[4,64,1024]{2,1,0:T(8,128)(2,1)S(1)} %all_to_all.50.refs_1_, bf16[4,64,1024]{2,1,0:T(8,128)(2,1)} %collective-permute-done.1.refs_2_, ...), custom_call_target="tpu_custom_call" | custom-call | flops 8589934592 | bytes 33554432 | tf_op jit(solution)/shard_map/pallas_call | solution.py:130
  174.2 12.5 %all_to_all.51 = bf16[8,4,4,512]{3,2,1,0:T(4,128)(2,1)S(1)} all-to-all(bf16[8,4,4,512]{3,2,1,0:T(4,128)(2,1)S(1)} %bitcast.40), channel_id=1, replica_groups=mesh['z'=8,'y'=4,'x'=4,'c'=2] {'x','c'}, dimensions={0} | all-to-all | bytes 262144 | tf_op jit(solution)/shard_map/all_to_all | solution.py:27
  186.7 3.9 %all-to-all-start.4 = ((f32[32,4,128]{2,1,0:T(4,128)}), f32[32,4,128]{2,1,0:T(4,128)S(1)}, u32[]{:S(2)}, u32[]{:S(2)}) async-start(f32[32,4,128]{2,1,0:T(4,128)} %bitcast.35), calls=%async_computation.4 | async-start | bytes 131072 | tf_op jit(solution)/shard_map/all_to_all | solution.py:27
  191.3 8.2 %all-to-all-done.4 = f32[32,4,128]{2,1,0:T(4,128)S(1)} async-done(((f32[32,4,128]{2,1,0:T(4,128)}), f32[32,4,128]{2,1,0:T(4,128)S(1)}, u32[]{:S(2)}, u32[]{:S(2)}) %all-to-all-start.4) | async-done | bytes 65568 | tf_op jit(solution)/shard_map/all_to_all | solution.py:27
  200.2 3.9 %all-to-all-start.5 = ((bf16[32,4,128]{2,1,0:T(4,128)(2,1)}), bf16[32,4,128]{2,1,0:T(4,128)(2,1)S(1)}, u32[]{:S(2)}, u32[]{:S(2)}) async-start(bf16[32,4,128]{2,1,0:T(4,128)(2,1)} %broadcast_in_dim.17), calls=%async_computation.5 | async-start | bytes 65536 | tf_op jit(solution)/shard_map/all_to_all | solution.py:27
  205.1 7.6 %all-to-all-done.5 = bf16[32,4,128]{2,1,0:T(4,128)(2,1)S(1)} async-done(((bf16[32,4,128]{2,1,0:T(4,128)(2,1)}), bf16[32,4,128]{2,1,0:T(4,128)(2,1)S(1)}, u32[]{:S(2)}, u32[]{:S(2)}) %all-to-all-start.5) | async-done | bytes 32800 | tf_op jit(solution)/shard_map/all_to_all | solution.py:27
  212.6 4.6 %all-to-all-start.8 = ((bf16[32,8,512]{2,1,0:T(8,128)(2,1)}), bf16[32,8,512]{2,1,0:T(8,128)(2,1)}, u32[]{:S(2)}, u32[]{:S(2)}) async-start(bf16[32,8,512]{2,1,0:T(8,128)(2,1)} %reshape.67), calls=%async_computation.8 | async-start | bytes 524288 | tf_op jit(solution)/shard_map/all_to_all | solution.py:27
  217.3 10.5 %all-to-all-done.8 = bf16[32,8,512]{2,1,0:T(8,128)(2,1)} async-done(((bf16[32,8,512]{2,1,0:T(8,128)(2,1)}), bf16[32,8,512]{2,1,0:T(8,128)(2,1)}, u32[]{:S(2)}, u32[]{:S(2)}) %all-to-all-start.8) | async-done | bytes 262176 | tf_op jit(solution)/shard_map/all_to_all | solution.py:27
  227.8 7.6 %all-to-all-start.9 = ((bf16[8,4,8,512]{3,2,1,0:T(8,128)(2,1)}), bf16[8,4,8,512]{3,2,1,0:T(8,128)(2,1)S(1)}, u32[]{:S(2)}, u32[]{:S(2)}) async-start(bf16[8,4,8,512]{3,2,1,0:T(8,128)(2,1)} %bitcast.14), calls=%async_computation.9 | async-start | bytes 524288 | tf_op jit(solution)/shard_map/all_to_all | solution.py:27
  235.6 8.3 %shard_map.104 = bf16[8,64,1024]{2,1,0:T(8,128)(2,1)} custom-call(s32[8]{0:T(128)S(1)} %reshape.70.mine_ref, bf16[128,128]{1,0:T(8,128)(2,1)S(1)} %bitcast.34, bf16[8,4,128,1024]{3,2,1,0:T(8,128)(2,1)} %get-tuple-element.9.rows_ref), custom_call_target="tpu_custom_call" | custom-call | flops 536870912 | bytes 9437184 | tf_op jit(solution)/shard_map/pallas_call | solution.py:174
  243.9 4.8 %all-to-all-start.6 = ((bf16[8,64,1024]{2,1,0:T(8,128)(2,1)}), bf16[8,64,1024]{2,1,0:T(8,128)(2,1)}, u32[]{:S(2)}, u32[]{:S(2)}) async-start(bf16[8,64,1024]{2,1,0:T(8,128)(2,1)} %shard_map.104), calls=%async_computation.6 | async-start | bytes 2097152 | tf_op jit(solution)/shard_map/all_to_all | solution.py:27
  250.5 13.4 %all-to-all-done.6 = bf16[8,64,1024]{2,1,0:T(8,128)(2,1)} async-done(((bf16[8,64,1024]{2,1,0:T(8,128)(2,1)}), bf16[8,64,1024]{2,1,0:T(8,128)(2,1)}, u32[]{:S(2)}, u32[]{:S(2)}) %all-to-all-start.6) | async-done | bytes 1048608 | tf_op jit(solution)/shard_map/all_to_all | solution.py:27
  (86 shorter events, 39.8 us)
Async XLA Ops:
  7.2 96.7 %copy-start = (bf16[32,2,16,1024]{3,2,1,0:T(8,128)(2,1)S(1)}, bf16[32,2,16,1024]{3,2,1,0:T(8,128)(2,1)}, u32[]{:S(2)}) copy-start(bf16[32,2,16,1024]{3,2,1,0:T(8,128)(2,1)} %param.10) | copy-start | bytes 6291460
  7.2 147.0 %all-gather.2.cloned.1.call-start = ((), (), s32[]{:S(2)}) async-start(), calls=%async_computation.10 | async-start | bytes 18874368 | tf_op jit(solution)/shard_map/all_gather | solution.py:212
  12.7 10.4 %collective-permute-start = (bf16[128,1024]{1,0:T(8,128)(2,1)S(1)}, bf16[128,1024]{1,0:T(8,128)(2,1)S(1)}, u32[]{:S(2)}, u32[]{:S(2)}) collective-permute-start(bf16[128,1024]{1,0:T(8,128)(2,1)S(1)} %copy-done.7), channel_id=1, source_target_pairs={{0,0},{1,32},{2,64},{3,96},{4,128},{5,160},{6,192},{7,224},{8,8},{... | collective-permute-start | bytes 786440 | tf_op jit(solution)/shard_map/ppermute | solution.py:214
  35.4 45.7 %all-to-all-start.1 = ((bf16[8,64,1024]{2,1,0:T(8,128)(2,1)}), bf16[8,64,1024]{2,1,0:T(8,128)(2,1)}, u32[]{:S(2)}, u32[]{:S(2)}) async-start(bf16[8,64,1024]{2,1,0:T(8,128)(2,1)} %broadcast_in_dim.13), calls=%async_computation.1 | async-start | bytes 2097152 | tf_op jit(solution)/shard_map/all_to_all | solution.py:27
  55.7 32.8 %collective-permute-start.2 = (bf16[4,64,1024]{2,1,0:T(8,128)(2,1)S(1)}, bf16[4,64,1024]{2,1,0:T(8,128)(2,1)S(1)}, u32[]{:S(2)}, u32[]{:S(2)}) collective-permute-start(bf16[4,64,1024]{2,1,0:T(8,128)(2,1)S(1)} %all_to_all.50.refs_1_), channel_id=1, source_target_pairs={{0,224},{32,0},{64,32},{96,64},{128,96},{160,128},{192,160},{224,1... | collective-permute-start | bytes 1572872 | tf_op jit(solution)/shard_map/ppermute | solution.py:36
  58.4 33.6 %collective-permute-start.1 = (bf16[4,64,1024]{2,1,0:T(8,128)(2,1)S(1)}, bf16[4,64,1024]{2,1,0:T(8,128)(2,1)}, u32[]{:S(2)}, u32[]{:S(2)}) collective-permute-start(bf16[4,64,1024]{2,1,0:T(8,128)(2,1)S(1)} %all_to_all.50.refs_1_), channel_id=1, source_target_pairs={{0,32},{32,64},{64,96},{96,128},{128,160},{160,192},{192,224},{224... | collective-permute-start | bytes 1572872 | tf_op jit(solution)/shard_map/ppermute | solution.py:36
  81.2 32.9 %collective-permute-start.10 = (bf16[8,64,1024]{2,1,0:T(8,128)(2,1)}, bf16[8,64,1024]{2,1,0:T(8,128)(2,1)}, u32[]{:S(2)}, u32[]{:S(2)}) collective-permute-start(bf16[8,64,1024]{2,1,0:T(8,128)(2,1)} %all-to-all-done.1.refs_10_), channel_id=1, source_target_pairs={{0,24},{8,0},{16,8},{24,16},{1,25},{9,1},{17,9},{25,17},{2,26},{10... | collective-permute-start | bytes 3145736 | tf_op jit(solution)/shard_map/ppermute | solution.py:36
  82.1 34.8 %collective-permute-start.9 = (bf16[8,64,1024]{2,1,0:T(8,128)(2,1)}, bf16[8,64,1024]{2,1,0:T(8,128)(2,1)}, u32[]{:S(2)}, u32[]{:S(2)}) collective-permute-start(bf16[8,64,1024]{2,1,0:T(8,128)(2,1)} %all-to-all-done.1.refs_10_), channel_id=1, source_target_pairs={{0,8},{8,16},{16,24},{24,0},{1,9},{9,17},{17,25},{25,1},{2,10},{10... | collective-permute-start | bytes 3145736 | tf_op jit(solution)/shard_map/ppermute | solution.py:36
  88.5 11.3 %collective-permute-start.4 = (bf16[4,64,1024]{2,1,0:T(8,128)(2,1)S(1)}, bf16[4,64,1024]{2,1,0:T(8,128)(2,1)}, u32[]{:S(2)}, u32[]{:S(2)}) collective-permute-start(bf16[4,64,1024]{2,1,0:T(8,128)(2,1)S(1)} %collective-permute-done.2.refs_3_), channel_id=1, source_target_pairs={{0,224},{32,0},{64,32},{96,64},{128,96},{160,128},{192,160},{224,1... | collective-permute-start | bytes 1572872 | tf_op jit(solution)/shard_map/ppermute | solution.py:36
  92.0 11.9 %collective-permute-start.3 = (bf16[4,64,1024]{2,1,0:T(8,128)(2,1)}, bf16[4,64,1024]{2,1,0:T(8,128)(2,1)}, u32[]{:S(2)}, u32[]{:S(2)}) collective-permute-start(bf16[4,64,1024]{2,1,0:T(8,128)(2,1)} %collective-permute-done.1.refs_2_), channel_id=1, source_target_pairs={{0,32},{32,64},{64,96},{96,128},{128,160},{160,192},{192,224},{224... | collective-permute-start | bytes 1572872 | tf_op jit(solution)/shard_map/ppermute | solution.py:36
  99.8 21.3 %collective-permute-start.6 = (bf16[4,64,1024]{2,1,0:T(8,128)(2,1)}, bf16[4,64,1024]{2,1,0:T(8,128)(2,1)S(1)}, u32[]{:S(2)}, u32[]{:S(2)}) collective-permute-start(bf16[4,64,1024]{2,1,0:T(8,128)(2,1)} %collective-permute-done.4.refs_5_), channel_id=1, source_target_pairs={{0,224},{32,0},{64,32},{96,64},{128,96},{160,128},{192,160},{224,1... | collective-permute-start | bytes 1572872 | tf_op jit(solution)/shard_map/ppermute | solution.py:36
  103.9 20.3 %collective-permute-start.5 = (bf16[4,64,1024]{2,1,0:T(8,128)(2,1)}, bf16[4,64,1024]{2,1,0:T(8,128)(2,1)}, u32[]{:S(2)}, u32[]{:S(2)}) collective-permute-start(bf16[4,64,1024]{2,1,0:T(8,128)(2,1)} %collective-permute-done.3.refs_4_), channel_id=1, source_target_pairs={{0,32},{32,64},{64,96},{96,128},{128,160},{160,192},{192,224},{224... | collective-permute-start | bytes 1572872 | tf_op jit(solution)/shard_map/ppermute | solution.py:36
  104.7 21.2 %all-to-all-start.2 = ((f32[8,4,128]{2,1,0:T(4,128)}), f32[8,4,128]{2,1,0:T(4,128)S(1)}, u32[]{:S(2)}, u32[]{:S(2)}) async-start(f32[8,4,128]{2,1,0:T(4,128)} %fusion.3), calls=%async_computation.2 | async-start | bytes 32768 | tf_op jit(solution)/shard_map/all_to_all | solution.py:27
  115.9 38.2 %collective-permute-start.12 = (bf16[4,64,1024]{2,1,0:T(8,128)(2,1)}, bf16[4,64,1024]{2,1,0:T(8,128)(2,1)}, u32[]{:S(2)}, u32[]{:S(2)}) collective-permute-start(bf16[4,64,1024]{2,1,0:T(8,128)(2,1)} %slice.41), channel_id=1, source_target_pairs={{0,24},{8,0},{16,8},{24,16},{1,25},{9,1},{17,9},{25,17},{2,26},{10... | collective-permute-start | bytes 1572872 | tf_op jit(solution)/shard_map/ppermute | solution.py:36
  118.7 35.4 %collective-permute-start.11 = (bf16[4,64,1024]{2,1,0:T(8,128)(2,1)}, bf16[4,64,1024]{2,1,0:T(8,128)(2,1)}, u32[]{:S(2)}, u32[]{:S(2)}) collective-permute-start(bf16[4,64,1024]{2,1,0:T(8,128)(2,1)} %slice.40), channel_id=1, source_target_pairs={{0,8},{8,16},{16,24},{24,0},{1,9},{9,17},{17,25},{25,1},{2,10},{10... | collective-permute-start | bytes 1572872 | tf_op jit(solution)/shard_map/ppermute | solution.py:36
  121.8 32.3 %collective-permute-start.8 = (bf16[2,64,1024]{2,1,0:T(8,128)(2,1)}, bf16[2,64,1024]{2,1,0:T(8,128)(2,1)}, u32[]{:S(2)}, u32[]{:S(2)}) collective-permute-start(bf16[2,64,1024]{2,1,0:T(8,128)(2,1)} %slice.38), channel_id=1, source_target_pairs={{0,224},{32,0},{64,32},{96,64},{128,96},{160,128},{192,160},{224,1... | collective-permute-start | bytes 786440 | tf_op jit(solution)/shard_map/ppermute | solution.py:36
  125.9 28.2 %collective-permute-start.7 = (bf16[2,64,1024]{2,1,0:T(8,128)(2,1)}, bf16[2,64,1024]{2,1,0:T(8,128)(2,1)}, u32[]{:S(2)}, u32[]{:S(2)}) collective-permute-start(bf16[2,64,1024]{2,1,0:T(8,128)(2,1)} %slice.37), channel_id=1, source_target_pairs={{0,32},{32,64},{64,96},{96,128},{128,160},{160,192},{192,224},{224... | collective-permute-start | bytes 786440 | tf_op jit(solution)/shard_map/ppermute | solution.py:36
  125.9 5.4 %collective-permute-start.13 = (bf16[4,128]{1,0:T(4,128)(2,1)S(1)}, bf16[4,128]{1,0:T(4,128)(2,1)S(1)}, u32[]{:S(2)}, u32[]{:S(2)}) collective-permute-start(bf16[4,128]{1,0:T(4,128)(2,1)S(1)} %reduce_sum.27), channel_id=1, source_target_pairs={{0,0},{1,32},{2,64},{3,96},{4,128},{5,160},{6,192},{7,224},{8,8},{... | collective-permute-start | bytes 3080 | tf_op jit(solution)/shard_map/ppermute | solution.py:221
  131.9 21.6 %all-to-all-start.3 = ((bf16[32,4,128]{2,1,0:T(4,128)(2,1)}), bf16[32,4,128]{2,1,0:T(4,128)(2,1)S(1)}, u32[]{:S(2)}, u32[]{:S(2)}) async-start(bf16[32,4,128]{2,1,0:T(4,128)(2,1)} %broadcast_in_dim.14), calls=%async_computation.3 | async-start | bytes 65536 | tf_op jit(solution)/shard_map/all_to_all | solution.py:27
  186.7 12.8 %all-to-all-start.4 = ((f32[32,4,128]{2,1,0:T(4,128)}), f32[32,4,128]{2,1,0:T(4,128)S(1)}, u32[]{:S(2)}, u32[]{:S(2)}) async-start(f32[32,4,128]{2,1,0:T(4,128)} %bitcast.35), calls=%async_computation.4 | async-start | bytes 131072 | tf_op jit(solution)/shard_map/all_to_all | solution.py:27
  200.2 12.5 %all-to-all-start.5 = ((bf16[32,4,128]{2,1,0:T(4,128)(2,1)}), bf16[32,4,128]{2,1,0:T(4,128)(2,1)S(1)}, u32[]{:S(2)}, u32[]{:S(2)}) async-start(bf16[32,4,128]{2,1,0:T(4,128)(2,1)} %broadcast_in_dim.17), calls=%async_computation.5 | async-start | bytes 65536 | tf_op jit(solution)/shard_map/all_to_all | solution.py:27
  212.6 15.2 %all-to-all-start.8 = ((bf16[32,8,512]{2,1,0:T(8,128)(2,1)}), bf16[32,8,512]{2,1,0:T(8,128)(2,1)}, u32[]{:S(2)}, u32[]{:S(2)}) async-start(bf16[32,8,512]{2,1,0:T(8,128)(2,1)} %reshape.67), calls=%async_computation.8 | async-start | bytes 524288 | tf_op jit(solution)/shard_map/all_to_all | solution.py:27
  227.8 16.1 %all-to-all-start.9 = ((bf16[8,4,8,512]{3,2,1,0:T(8,128)(2,1)}), bf16[8,4,8,512]{3,2,1,0:T(8,128)(2,1)S(1)}, u32[]{:S(2)}, u32[]{:S(2)}) async-start(bf16[8,4,8,512]{3,2,1,0:T(8,128)(2,1)} %bitcast.14), calls=%async_computation.9 | async-start | bytes 524288 | tf_op jit(solution)/shard_map/all_to_all | solution.py:27
  243.9 20.0 %all-to-all-start.6 = ((bf16[8,64,1024]{2,1,0:T(8,128)(2,1)}), bf16[8,64,1024]{2,1,0:T(8,128)(2,1)}, u32[]{:S(2)}, u32[]{:S(2)}) async-start(bf16[8,64,1024]{2,1,0:T(8,128)(2,1)} %shard_map.104), calls=%async_computation.6 | async-start | bytes 2097152 | tf_op jit(solution)/shard_map/all_to_all | solution.py:27
  (9 other events, 135.5 us)
Sparse Core Ops, SparseCore 0:
  11.9 92.5 all-gather.1

commit v3 on v2

v3 whole, which is shorter than its diff:
```python
import jax
import jax.numpy as jnp
from jax import lax
from jax.experimental import pallas as pl
from jax.experimental.pallas import tpu as pltpu
from jax.sharding import Mesh, PartitionSpec as P

R = 16
RANKS = 2 * R
BLOCK_ROWS = 128
Z, Y, X, C = 8, 4, 4, 2
N_DP, N_TENSOR = Z * Y, X * C
OWN = 2
SLOTS = OWN * N_DP
DP, TENSOR = ("z", "y"), ("x", "c")
BF16, F32 = jnp.bfloat16, jnp.float32
VMEM_LIMIT = 48 * 2 ** 20


def swap(skew):
    return [((z * Y + y) * N_TENSOR + t, (((t + skew * z) % Z) * Y + y) * N_TENSOR + z)
            for z in range(Z) for y in range(Y) for t in range(N_TENSOR)]


def exchange(x, axes):
    return lax.all_to_all(x, axes, 0, 0, tiled=True)


def spread(x, axis, n):
    return exchange(jnp.broadcast_to(x[None], (n,) + x.shape), axis)


def hop(x, axis, n, step):
    return lax.ppermute(x, axis, [(i, (i + step) % n) for i in range(n)])


def last_hop(up, down, axis, n):
    pairs = []
    for i in range(n):
        for c in range(C):
            pairs.append((i * C + c, ((i + (1 if c == 0 else -1)) % n) * C + c))
    return lax.ppermute(jnp.where(lax.axis_index("c") == 0, up, down), (axis, "c"), pairs)


def block_kernel(where_ref, rows_ref, *refs):
    weights, refs = refs[:N_TENSOR], refs[N_TENSOR:]
    low_ref, out_map_ref, cot_ref, hidden_ref, sent_ref, x_buf, w_buf, acc_ref, x_sem, w_sem = refs
    parts, blocks, _, depth = x_buf.shape
    t = where_ref[0]

    def place(i):
        x, c = lax.div(t, C), lax.rem(t, C)
        step, other = lax.div(i, C), lax.rem(i, C)
        back = jnp.where(step < 2, step, 5 - step)
        feature = lax.rem(x - back + X, X) * C + lax.rem(c + other, C)
        return lax.rem(feature + t, parts)

    def load(i):
        return pltpu.make_async_copy(rows_ref.at[place(i)], x_buf.at[i], x_sem.at[i])

    for i, weight in enumerate(weights):
        load(i).start()
        pltpu.make_async_copy(weight, w_buf.at[i], w_sem.at[i]).start()
    acc_ref[...] = jnp.zeros_like(acc_ref)

    @pl.loop(0, parts)
    def _(i):
        load(i).wait()
        pltpu.make_async_copy(w_buf.at[i], w_buf.at[i], w_sem.at[i]).wait()
        rows = x_buf[i].reshape(blocks * BLOCK_ROWS, depth)
        acc_ref[...] += jnp.dot(rows, w_buf[i], preferred_element_type=F32)

    half = cot_ref.shape[1]
    for b in range(blocks):
        rows = slice(b * BLOCK_ROWS, (b + 1) * BLOCK_ROWS)
        ranks = slice(b * RANKS, (b + 1) * RANKS)
        low = low_ref[ranks, :]
        out_map = out_map_ref[b]
        pre = acc_ref[rows, :] + lax.dot_general(
            low, out_map, (((0,), (0,)), ((), ())), preferred_element_type=F32)
        gate, up = pre[:, :half], pre[:, half:]
        sigma = jax.nn.sigmoid(gate)
        gated = gate * sigma
        hidden_ref[rows, :] = (gated * up).astype(BF16)
        live = lax.broadcasted_iota(jnp.int32, (BLOCK_ROWS, half), 0) < where_ref[1 + b]
        cotan = jnp.where(live, cot_ref[rows, :].astype(F32), 0.0)
        dgate = cotan * up * sigma * (1.0 + gate * (1.0 - sigma))
        dup = cotan * gated
        dpre = jnp.concatenate([dgate, dup], 1).astype(BF16)
        grad = jnp.dot(low, dpre, preferred_element_type=F32)
        sent_ref[:R, b * half:(b + 1) * half] = grad[:R, :half].astype(BF16)
        sent_ref[R:, b * half:(b + 1) * half] = grad[R:, half:].astype(BF16)
        dlow = lax.dot_general(out_map, dpre, (((1,), (1,)), ((), ())), preferred_element_type=F32)
        at = blocks * half + b * BLOCK_ROWS
        sent_ref[:, at:at + BLOCK_ROWS] = dlow.astype(BF16)


def project(where, rows, weights, low, out_map, cotan):
    parts, blocks, _, depth = rows.shape
    n_rows, half = cotan.shape
    any_spec = pl.BlockSpec(memory_space=pl.ANY)
    vmem_spec = pl.BlockSpec(memory_space=pltpu.VMEM)
    return pl.pallas_call(
        block_kernel,
        in_specs=[pl.BlockSpec(memory_space=pltpu.SMEM)] + [any_spec] * (1 + parts) + [vmem_spec] * 3,
        out_specs=[vmem_spec, vmem_spec],
        out_shape=[
            jax.ShapeDtypeStruct((n_rows, half), BF16),
            jax.ShapeDtypeStruct((RANKS, blocks * (half + BLOCK_ROWS)), BF16),
        ],
        scratch_shapes=[
            pltpu.VMEM(rows.shape, BF16),
            pltpu.VMEM((parts,) + weights[0].shape, BF16),
            pltpu.VMEM((n_rows, 2 * half), F32),
            pltpu.SemaphoreType.DMA((parts,)),
            pltpu.SemaphoreType.DMA((parts,)),
        ],
        compiler_params=pltpu.CompilerParams(vmem_limit_bytes=VMEM_LIMIT),
        cost_estimate=pl.CostEstimate(
            flops=4 * parts * n_rows * depth * half,
            bytes_accessed=2 * parts * depth * (n_rows + 2 * half),
            transcendentals=n_rows * half),
    )(where, rows, *weights, low, out_map, cotan)


def slot_kernel(slot_ref, shared_ref, out_ref):
    blocks, _ = slot_ref.shape
    width = shared_ref.shape[1] // blocks
    n_out = OWN * Y * N_DP
    row = lax.broadcasted_iota(jnp.int32, (n_out, N_DP), 0)
    lane = lax.broadcasted_iota(jnp.int32, (n_out, N_DP), 1)
    slot = (row & (N_DP - 1)) * OWN + lax.shift_right_logical(row, 7)
    same = (lax.shift_right_logical(row, 5) & (Y - 1)) == (lane & (Y - 1))
    total = None
    for b in range(blocks):
        pick = jnp.where(same & (slot == slot_ref[b:b + 1, :]), 1.0, 0.0).astype(BF16)
        term = jnp.dot(pick, shared_ref[:, b * width:(b + 1) * width], preferred_element_type=F32)
        total = term if total is None else total + term
    for i in range(OWN * Y):
        out_ref[:, i * width:(i + 1) * width] = total[i * N_DP:(i + 1) * N_DP].astype(BF16)


def in_grad_kernel(mine_ref, dlow_ref, rows_ref, out_ref, buf, acc_ref, sems):
    parts, blocks, _, _ = rows_ref.shape

    def load(b):
        return pltpu.make_async_copy(rows_ref.at[:, b], buf.at[b], sems.at[b])

    def used(b):
        return mine_ref[b] + mine_ref[blocks + b] > 0

    for b in range(blocks):
        @pl.when(used(b))
        def _():
            load(b).start()

    acc_ref[...] = jnp.zeros_like(acc_ref)
    for b in range(blocks):
        @pl.when(used(b))
        def _():
            dlow = dlow_ref[:, b * BLOCK_ROWS:(b + 1) * BLOCK_ROWS].astype(F32)
            left = jnp.concatenate(
                [jnp.where(mine_ref[s * blocks + b] > 0, dlow, 0.0) for s in range(OWN)], 0).astype(BF16)
            load(b).wait()

            @pl.loop(0, parts)
            def _(k):
                feature = lax.rem(k - mine_ref[OWN * blocks] + parts, parts)
                acc_ref[feature] += jnp.dot(left, buf[b, k], preferred_element_type=F32)

    out_ref[...] = acc_ref[...].astype(BF16)


def in_grad(mine, dlow, rows):
    parts, blocks, _, depth = rows.shape
    n_out = OWN * RANKS
    vmem_spec = pl.BlockSpec(memory_space=pltpu.VMEM)
    return pl.pallas_call(
        in_grad_kernel,
        in_specs=[pl.BlockSpec(memory_space=pltpu.SMEM), vmem_spec, pl.BlockSpec(memory_space=pl.ANY)],
        out_specs=vmem_spec,
        out_shape=jax.ShapeDtypeStruct((parts, n_out, depth), BF16),
        scratch_shapes=[
            pltpu.VMEM((blocks, parts, BLOCK_ROWS, depth), BF16),
            pltpu.VMEM((parts, n_out, depth), F32),
            pltpu.SemaphoreType.DMA((blocks,)),
        ],
        compiler_params=pltpu.CompilerParams(vmem_limit_bytes=VMEM_LIMIT),
        cost_estimate=pl.CostEstimate(
            flops=2 * parts * n_out * blocks * BLOCK_ROWS * depth,
            bytes_accessed=2 * parts * depth * blocks * BLOCK_ROWS, transcendentals=0),
    )(mine, dlow, rows)


def out_grad_kernel(got_ref, out_ref):
    width = out_ref.shape[2]
    for s in range(OWN):
        out_ref[s] = got_ref[:, s * width:(s + 1) * width].astype(F32)


def body(tokens, gate_up, adapter_in, adapter_out, d_hidden, block_adapter, block_live, owner_slot):
    dp, tensor = lax.axis_index(DP), lax.axis_index(TENSOR)
    d_part, hidden_part = tokens.shape[1], gate_up.shape[2]
    blocks = d_hidden.shape[0] // BLOCK_ROWS
    lanes = RANKS * blocks
    per = RANKS // N_TENSOR

    join = lax.optimization_barrier

    swapped = lax.ppermute(tokens, DP + TENSOR, swap(1))
    in_map = lax.dynamic_index_in_dim(adapter_in, block_adapter[dp], 0, False).reshape(RANKS, d_part)
    low_part = lax.dot_general(in_map, tokens, (((1,), (1,)), ((), ())), preferred_element_type=F32)
    low_sum = exchange(low_part.reshape(N_TENSOR, per, BLOCK_ROWS), TENSOR).sum(0).astype(BF16)
    swapped, low_sum, flat = join((swapped, low_sum, gate_up.reshape(d_part, 2 * hidden_part)))
    rows = lax.all_gather(swapped, DP, axis=0, tiled=False).reshape(Z, Y, BLOCK_ROWS, d_part)

    left, right = hop(flat, "x", X, 1), hop(flat, "x", X, -1)
    own = hop(flat, "c", C, 1)
    low = spread(lax.ppermute(low_sum, DP + TENSOR, swap(0)), DP, N_DP)
    left, right, own, low = join((left, right, own, low))
    far = last_hop(left, right, "x", X)
    weights = [flat, own, left, hop(left, "c", C, 1), right, hop(right, "c", C, 1), far, hop(far, "c", C, 1)]
    low = low.reshape(Z, Y, per, BLOCK_ROWS).transpose(1, 0, 2, 3).reshape(lanes, BLOCK_ROWS)

    local_ids = lax.dynamic_slice_in_dim(block_adapter, tensor * blocks, blocks, 0)
    local_live = lax.dynamic_slice_in_dim(block_live, tensor * blocks, blocks, 0)
    picked = adapter_out[local_ids]
    out_map = jnp.concatenate([
        jnp.pad(picked[:, 0], ((0, 0), (0, 0), (0, hidden_part))),
        jnp.pad(picked[:, 1], ((0, 0), (0, 0), (hidden_part, 0)))], 1)
    where = jnp.concatenate([tensor.astype(jnp.int32)[None], local_live])
    slot_of = owner_slot[block_adapter]
    local_slot = lax.dynamic_slice_in_dim(slot_of, tensor * blocks, blocks, 0)
    mine = jnp.arange(OWN, dtype=jnp.int32)[:, None] + OWN * dp == local_slot[None, :]
    slot_lane = jnp.repeat(slot_of.reshape(N_TENSOR, blocks).T, Y, axis=1)

    hidden, sent = project(where, rows, weights, low, out_map, d_hidden)

    first = exchange(sent, DP)
    split = blocks * hidden_part
    dlow = spread(first[:, split:].astype(F32).sum(0).astype(BF16), DP, N_DP)
    shared = exchange(first[:, :split], TENSOR)
    merged = pl.pallas_call(
        slot_kernel,
        out_shape=jax.ShapeDtypeStruct((N_DP, OWN * Y * hidden_part), BF16),
    )(slot_lane, shared)
    got = exchange(merged, DP)
    in_part = in_grad(jnp.append(mine.reshape(-1).astype(jnp.int32), tensor.astype(jnp.int32)), dlow, rows)
    grad_in = exchange(in_part, TENSOR).astype(F32).sum(0).reshape(OWN, 2, R, d_part)
    grad_out = pl.pallas_call(
        out_grad_kernel,
        out_shape=jax.ShapeDtypeStruct((OWN, RANKS, Y * hidden_part), F32),
    )(got).reshape(OWN, 2, R, Y * hidden_part)
    return hidden, grad_in, grad_out


def solution(mesh):
    mesh = Mesh(mesh.devices.reshape(Z, Y, X, C), DP + TENSOR)

    return jax.shard_map(
        body,
        mesh=mesh,
        in_specs=(P(DP, TENSOR), P(TENSOR, None, DP), P(None, None, None, TENSOR), P(None, None, None, DP),
                  P(TENSOR, DP), P(), P(), P()),
        out_specs=(P(TENSOR, DP), P(DP, None, None, TENSOR), P(DP, None, None, TENSOR)),
        check_vma=False,
    )
```

time: 274 us -> 238 us (0.87)
  starting transfers between devices: 85.3 us -> 69.5 us
  blocking collectives: 23.5 us -> 14.8 us
  Pallas kernels: 27.6 us -> 19.7 us
  local copies, waits for them, and re-layouts: 22.3 us -> 18.1 us
  waiting for transfers between devices: 94.5 us -> 90.5 us
  other arithmetic: 2.45 us -> 6.02 us
    all_to_all x8 -> x6, waiting for transfers between devices: 70.8 us -> 34.2 us  [exchange(): return lax.all_to_all(x, axes, 0, 0, tiled=True)]
    ppermute x13 -> x8, waiting for transfers between devices: 18.2 us -> 39.9 us  [the longest x1 22.9 us: last_hop(): lax.ppermute(jnp.where(lax.axis_index('c') == 0, up, down), (axis, 'c'),...]
    all_gather x1, waiting for transfers between devices: 0.02 us -> 16.4 us  [body(): lax.all_gather(swapped, DP, axis=0, tiled=False)]
    all_to_all x8 -> x6, starting transfers between devices: 67.3 us -> 51.7 us  [exchange(): return lax.all_to_all(x, axes, 0, 0, tiled=True)]
    all_to_all x2 -> x1, blocking collectives: 23.5 us -> 14.8 us  [exchange(): return lax.all_to_all(x, axes, 0, 0, tiled=True)]
    pallas_call x2 -> x3, Pallas kernels: 25.8 us -> 17.9 us  [the longest x1 14 us: project(): pl.pallas_call(block_kernel, in_specs=[pl.BlockSpec(memory_space=pltpu.SM...]
    unnamed x21 -> x24, local copies, waits for them, and re-layouts: 4.19 us -> 10.6 us
    slice x5 -> x1, local copies, waits for them, and re-layouts: 6.16 us -> 0.01 us  [body(): shared = exchange(first[:, :split], TENSOR)]
  transfers between devices with their start and end apart: 23 -> 16, of which waited for: 12 -> 12; matrix products, arithmetic and copies ran while one was open for 5% -> 8% of each run, Pallas kernels for 4% -> 2%
where the time goes in v3:
time: 238 us; the launch traced here: 237 us
  waiting for transfers between devices  90.5 us (38%)
  starting transfers between devices  69.5 us (29%)
  Pallas kernels  19.7 us (8%)
  local copies, waits for them, and re-layouts  18.1 us (8%)
  between operations  16.2 us (7%)
  blocking collectives  14.8 us (6%)
  other arithmetic  6.02 us (3%)
    all_to_all x6, starting transfers between devices, exchange(): return lax.all_to_all(x, axes, 0, 0, tiled=True)  51.7 us
    all_to_all x6, waiting for transfers between devices, exchange(): return lax.all_to_all(x, axes, 0, 0, tiled=True)  34.2 us
    ppermute x1, waiting for transfers between devices, last_hop(): lax.ppermute(jnp.where(lax.axis_index('c') == 0, up, down), (axis, 'c'),...  22.9 us
    all_gather x1, waiting for transfers between devices, body(): lax.all_gather(swapped, DP, axis=0, tiled=False)  16.4 us
    all_to_all x1, blocking collectives, exchange(): return lax.all_to_all(x, axes, 0, 0, tiled=True)  14.8 us
    ppermute x6, waiting for transfers between devices, hop(): return lax.ppermute(x, axis, [(i, (i + step) % n) for i in range(n)])  14.4 us
    pallas_call x1, Pallas kernels, project(): pl.pallas_call(block_kernel, in_specs=[pl.BlockSpec(memory_space=pltpu.SM...  14 us
    unnamed x24, local copies, waits for them, and re-layouts  10.6 us
  transfers between devices with their start and end apart: 16, of which 12 were waited for; matrix products, arithmetic and copies ran while one was open for 8% of the time, Pallas kernels for 2%

profile of v3, /device:TPU:1, one launch (start us, length us, event | category | flops | bytes accessed | tf_op | source)
XLA Modules:
  0.0 236.6 jit_solution(8703984068409959579)
XLA Ops:
  7.2 5.1 %collective-permute-start = (bf16[128,1024]{1,0:T(8,128)(2,1)}, bf16[128,1024]{1,0:T(8,128)(2,1)S(1)}, u32[]{:S(2)}, u32[]{:S(2)}) collective-permute-start(bf16[128,1024]{1,0:T(8,128)(2,1)} %param.8), channel_id=1, source_target_pairs={{0,0},{1,32},{2,64},{3,96},{4,128},{5,160},{6,192},{7,224},{8,8},{... | collective-permute-start | bytes 786440 | tf_op jit(solution)/shard_map/ppermute | solution.py:210
  17.3 9.9 %all-to-all-start = ((f32[8,4,128]{2,1,0:T(4,128)}), f32[8,4,128]{2,1,0:T(4,128)S(1)}, u32[]{:S(2)}, u32[]{:S(2)}) async-start(f32[8,4,128]{2,1,0:T(4,128)} %fusion.3), calls=%async_computation | async-start | bytes 32768 | tf_op jit(solution)/shard_map/all_to_all | solution.py:26
  27.2 3.5 %copy.36 = bf16[128,8,2,512]{3,1,2,0:T(8,128)(2,1)} copy(bf16[128,8,2,512]{3,2,1,0:T(2,128)(2,1)} %bitcast.46) | data formatting | bytes 4194304
  33.0 2.4 %collective-permute-start.2 = (bf16[1024,1024]{1,0:T(8,128)(2,1)}, bf16[1024,1024]{1,0:T(8,128)(2,1)}, u32[]{:S(2)}, u32[]{:S(2)}) collective-permute-start(bf16[1024,1024]{1,0:T(8,128)(2,1)} %bitcast.38), channel_id=1, source_target_pairs={{0,6},{2,0},{4,2},{6,4},{1,7},{3,1},{5,3},{7,5},{8,14},{10,8},{12,... | collective-permute-start | bytes 6291464 | tf_op jit(solution)/shard_map/ppermute | solution.py:34
  36.6 2.6 %collective-permute-start.4 = (bf16[4,128]{1,0:T(4,128)(2,1)S(1)}, bf16[4,128]{1,0:T(4,128)(2,1)S(1)}, u32[]{:S(2)}, u32[]{:S(2)}) collective-permute-start(bf16[4,128]{1,0:T(4,128)(2,1)S(1)} %reduce_sum.30), channel_id=1, source_target_pairs={{0,0},{1,32},{2,64},{3,96},{4,128},{5,160},{6,192},{7,224},{8,8},{... | collective-permute-start | bytes 3080 | tf_op jit(solution)/shard_map/ppermute | solution.py:219
  39.2 2.6 %collective-permute-done.4 = bf16[4,128]{1,0:T(4,128)(2,1)S(1)} collective-permute-done((bf16[4,128]{1,0:T(4,128)(2,1)S(1)}, bf16[4,128]{1,0:T(4,128)(2,1)S(1)}, u32[]{:S(2)}, u32[]{:S(2)}) %collective-permute-start.4) | collective-permute-done | bytes 1056 | tf_op jit(solution)/shard_map/ppermute | solution.py:219
  42.5 16.9 %all-to-all-start.1 = ((bf16[32,4,128]{2,1,0:T(4,128)(2,1)}), bf16[32,4,128]{2,1,0:T(4,128)(2,1)S(1)}, u32[]{:S(2)}, u32[]{:S(2)}) async-start(bf16[32,4,128]{2,1,0:T(4,128)(2,1)} %broadcast_in_dim.13), calls=%async_computation.1 | async-start | bytes 65536 | tf_op jit(solution)/shard_map/all_to_all | solution.py:26
  59.5 8.9 %all-to-all-done.1 = bf16[32,4,128]{2,1,0:T(4,128)(2,1)S(1)} async-done(((bf16[32,4,128]{2,1,0:T(4,128)(2,1)}), bf16[32,4,128]{2,1,0:T(4,128)(2,1)S(1)}, u32[]{:S(2)}, u32[]{:S(2)}) %all-to-all-start.1) | async-done | bytes 32800 | tf_op jit(solution)/shard_map/all_to_all | solution.py:26
  68.4 12.3 %collective-permute-done.1.refs_2_ = bf16[1024,1024]{1,0:T(8,128)(2,1)} collective-permute-done((bf16[1024,1024]{1,0:T(8,128)(2,1)}, bf16[1024,1024]{1,0:T(8,128)(2,1)}, u32[]{:S(2)}, u32[]{:S(2)}) %collective-permute-start.1) | collective-permute-done | bytes 2097184 | tf_op jit(solution)/shard_map/ppermute | solution.py:34
  82.6 2.4 %collective-permute-start.7 = (bf16[1024,1024]{1,0:T(8,128)(2,1)S(1)}, bf16[1024,1024]{1,0:T(8,128)(2,1)}, u32[]{:S(2)}, u32[]{:S(2)}) collective-permute-start(bf16[1024,1024]{1,0:T(8,128)(2,1)S(1)} %broadcast_select_fusion), channel_id=1, source_target_pairs={{0,2},{1,7},{2,4},{3,1},{4,6},{5,3},{6,0},{7,5},{8,10},{9,15},{10,... | collective-permute-start | bytes 6291464 | tf_op jit(solution)/shard_map/ppermute | solution.py:42
  85.5 22.9 %collective-permute-done.7.refs_6_ = bf16[1024,1024]{1,0:T(8,128)(2,1)} collective-permute-done((bf16[1024,1024]{1,0:T(8,128)(2,1)S(1)}, bf16[1024,1024]{1,0:T(8,128)(2,1)}, u32[]{:S(2)}, u32[]{:S(2)}) %collective-permute-start.7) | collective-permute-done | bytes 2097184 | tf_op jit(solution)/shard_map/ppermute | solution.py:42
  108.4 3.1 %collective-permute-start.8 = (bf16[1024,1024]{1,0:T(8,128)(2,1)}, bf16[1024,1024]{1,0:T(8,128)(2,1)}, u32[]{:S(2)}, u32[]{:S(2)}) collective-permute-start(bf16[1024,1024]{1,0:T(8,128)(2,1)} %collective-permute-done.7.refs_6_), channel_id=1, source_target_pairs={{0,1},{1,0},{2,3},{3,2},{4,5},{5,4},{6,7},{7,6},{8,9},{9,8},{10,11... | collective-permute-start | bytes 6291464 | tf_op jit(solution)/shard_map/ppermute | solution.py:34
  115.6 16.4 %all-gather.3.cloned.1.call-done = bf16[4096,1024]{1,0:T(8,128)(2,1)} async-done(((bf16[128,1024]{1,0:T(8,128)(2,1)}), bf16[4096,1024]{1,0:T(8,128)(2,1)}) %all-gather.3.cloned.1.call-update) | async-done | bytes 8388624 | tf_op jit(solution)/shard_map/all_gather | solution.py:215
  133.7 14.0 %shard_map.103 = (bf16[512,512]{1,0:T(8,128)(2,1)}, bf16[32,2560]{1,0:T(8,128)(2,1)S(1)}) custom-call(s32[5]{0:T(128)S(1)} %pad_add_fusion.where_ref, bf16[8,4,128,1024]{3,2,1,0:T(8,128)(2,1)} %bitcast.44, bf16[1024,1024]{1,0:T(8,128)(2,1)S(1)} %bitcast.40, bf16[1024,1024]{1,0:T(8,128)(2,1)} %collective-permute-done.3.refs_1_, ...), custom_call_target="tpu_custom_call" | custom-call | flops 8589934592 | bytes 25165824 | tf_op jit(solution)/shard_map/pallas_call | solution.py:103
  148.8 14.8 %all_to_all.57 = bf16[32,2,1280]{2,1,0:T(2,128)(2,1)S(1)} all-to-all(bf16[32,2,1280]{2,1,0:T(2,128)(2,1)S(1)} %reshape.92), channel_id=1, replica_groups=mesh['z'=8,'y'=4,'x'=4,'c'=2] {'z','y'}, dimensions={0} | all-to-all | bytes 327680 | tf_op jit(solution)/shard_map/all_to_all | solution.py:26
  164.4 6.8 %all-to-all-start.5 = ((bf16[8,4,2048]{2,1,0:T(4,128)(2,1)}), bf16[8,4,2048]{2,1,0:T(4,128)(2,1)S(1)}, u32[]{:S(2)}, u32[]{:S(2)}) async-start(bf16[8,4,2048]{2,1,0:T(4,128)(2,1)} %all_to_all.44), calls=%async_computation.5 | async-start | bytes 262144 | tf_op jit(solution)/shard_map/all_to_all | solution.py:26
  172.6 3.9 %all-to-all-done.5 = bf16[8,4,2048]{2,1,0:T(4,128)(2,1)S(1)} async-done(((bf16[8,4,2048]{2,1,0:T(4,128)(2,1)}), bf16[8,4,2048]{2,1,0:T(4,128)(2,1)S(1)}, u32[]{:S(2)}, u32[]{:S(2)}) %all-to-all-start.5) | async-done | bytes 131104 | tf_op jit(solution)/shard_map/all_to_all | solution.py:26
  176.5 3.8 %all-to-all-start.3 = ((bf16[32,2,256]{2,1,0:T(2,128)(2,1)}), bf16[32,2,256]{2,1,0:T(2,128)(2,1)S(1)}, u32[]{:S(2)}, u32[]{:S(2)}) async-start(bf16[32,2,256]{2,1,0:T(2,128)(2,1)} %reshape.94), calls=%async_computation.3 | async-start | bytes 65536 | tf_op jit(solution)/shard_map/all_to_all | solution.py:26
  182.6 2.0 shard_map.105
  188.9 7.4 %all-to-all-start.6 = ((bf16[32,2,2048]{2,1,0:T(2,128)(2,1)}), bf16[32,2,2048]{2,1,0:T(2,128)(2,1)S(1)}, u32[]{:S(2)}, u32[]{:S(2)}) async-start(bf16[32,2,2048]{2,1,0:T(2,128)(2,1)} %reshape.96), calls=%async_computation.6 | async-start | bytes 524288 | tf_op jit(solution)/shard_map/all_to_all | solution.py:26
  198.7 8.2 %all-to-all-done.6 = bf16[32,2,2048]{2,1,0:T(2,128)(2,1)S(1)} async-done(((bf16[32,2,2048]{2,1,0:T(2,128)(2,1)}), bf16[32,2,2048]{2,1,0:T(2,128)(2,1)S(1)}, u32[]{:S(2)}, u32[]{:S(2)}) %all-to-all-start.6) | async-done | bytes 262176 | tf_op jit(solution)/shard_map/all_to_all | solution.py:26
  206.9 6.9 %all-to-all-start.4 = ((bf16[8,64,1024]{2,1,0:T(8,128)(2,1)}), bf16[8,64,1024]{2,1,0:T(8,128)(2,1)S(1)}, u32[]{:S(2)}, u32[]{:S(2)}) async-start(bf16[8,64,1024]{2,1,0:T(8,128)(2,1)} %shard_map.104), calls=%async_computation.4 | async-start | bytes 2097152 | tf_op jit(solution)/shard_map/all_to_all | solution.py:26
  214.7 2.0 copy.40
  218.5 10.3 %all-to-all-done.4 = bf16[8,64,1024]{2,1,0:T(8,128)(2,1)S(1)} async-done(((bf16[8,64,1024]{2,1,0:T(8,128)(2,1)}), bf16[8,64,1024]{2,1,0:T(8,128)(2,1)S(1)}, u32[]{:S(2)}, u32[]{:S(2)}) %all-to-all-start.4) | async-done | bytes 1048608 | tf_op jit(solution)/shard_map/all_to_all | solution.py:26
  (76 shorter events, 31.2 us)
Async XLA Ops:
  7.2 8.3 %copy-start = (bf16[32,2,16,1024]{3,2,1,0:T(8,128)(2,1)S(1)}, bf16[32,2,16,1024]{3,2,1,0:T(8,128)(2,1)}, u32[]{:S(2)}) copy-start(bf16[32,2,16,1024]{3,2,1,0:T(8,128)(2,1)} %param.10) | copy-start | bytes 6291460
  7.2 24.7 %collective-permute-start = (bf16[128,1024]{1,0:T(8,128)(2,1)}, bf16[128,1024]{1,0:T(8,128)(2,1)S(1)}, u32[]{:S(2)}, u32[]{:S(2)}) collective-permute-start(bf16[128,1024]{1,0:T(8,128)(2,1)} %param.8), channel_id=1, source_target_pairs={{0,0},{1,32},{2,64},{3,96},{4,128},{5,160},{6,192},{7,224},{8,8},{... | collective-permute-start | bytes 786440 | tf_op jit(solution)/shard_map/ppermute | solution.py:210
  17.3 14.6 %all-to-all-start = ((f32[8,4,128]{2,1,0:T(4,128)}), f32[8,4,128]{2,1,0:T(4,128)S(1)}, u32[]{:S(2)}, u32[]{:S(2)}) async-start(f32[8,4,128]{2,1,0:T(4,128)} %fusion.3), calls=%async_computation | async-start | bytes 32768 | tf_op jit(solution)/shard_map/all_to_all | solution.py:26
  27.2 104.9 %all-gather.3.cloned.1.call-start = ((), (), s32[]{:S(2)}) async-start(), calls=%async_computation.7 | async-start | bytes 8650752 | tf_op jit(solution)/shard_map/all_gather | solution.py:215
  31.9 0.7 copy-start.4
  32.6 48.1 %collective-permute-start.1 = (bf16[1024,1024]{1,0:T(8,128)(2,1)}, bf16[1024,1024]{1,0:T(8,128)(2,1)}, u32[]{:S(2)}, u32[]{:S(2)}) collective-permute-start(bf16[1024,1024]{1,0:T(8,128)(2,1)} %bitcast.37), channel_id=1, source_target_pairs={{0,2},{2,4},{4,6},{6,0},{1,3},{3,5},{5,7},{7,1},{8,10},{10,12},{12... | collective-permute-start | bytes 6291464 | tf_op jit(solution)/shard_map/ppermute | solution.py:34
  33.0 47.8 %collective-permute-start.2 = (bf16[1024,1024]{1,0:T(8,128)(2,1)}, bf16[1024,1024]{1,0:T(8,128)(2,1)}, u32[]{:S(2)}, u32[]{:S(2)}) collective-permute-start(bf16[1024,1024]{1,0:T(8,128)(2,1)} %bitcast.38), channel_id=1, source_target_pairs={{0,6},{2,0},{4,2},{6,4},{1,7},{3,1},{5,3},{7,5},{8,14},{10,8},{12,... | collective-permute-start | bytes 6291464 | tf_op jit(solution)/shard_map/ppermute | solution.py:34
  35.3 45.4 %collective-permute-start.3 = (bf16[1024,1024]{1,0:T(8,128)(2,1)}, bf16[1024,1024]{1,0:T(8,128)(2,1)}, u32[]{:S(2)}, u32[]{:S(2)}) collective-permute-start(bf16[1024,1024]{1,0:T(8,128)(2,1)} %bitcast.39), channel_id=1, source_target_pairs={{0,1},{1,0},{2,3},{3,2},{4,5},{5,4},{6,7},{7,6},{8,9},{9,8},{10,11... | collective-permute-start | bytes 6291464 | tf_op jit(solution)/shard_map/ppermute | solution.py:34
  36.6 5.3 %collective-permute-start.4 = (bf16[4,128]{1,0:T(4,128)(2,1)S(1)}, bf16[4,128]{1,0:T(4,128)(2,1)S(1)}, u32[]{:S(2)}, u32[]{:S(2)}) collective-permute-start(bf16[4,128]{1,0:T(4,128)(2,1)S(1)} %reduce_sum.30), channel_id=1, source_target_pairs={{0,0},{1,32},{2,64},{3,96},{4,128},{5,160},{6,192},{7,224},{8,8},{... | collective-permute-start | bytes 3080 | tf_op jit(solution)/shard_map/ppermute | solution.py:219
  42.5 25.8 %all-to-all-start.1 = ((bf16[32,4,128]{2,1,0:T(4,128)(2,1)}), bf16[32,4,128]{2,1,0:T(4,128)(2,1)S(1)}, u32[]{:S(2)}, u32[]{:S(2)}) async-start(bf16[32,4,128]{2,1,0:T(4,128)(2,1)} %broadcast_in_dim.13), calls=%async_computation.1 | async-start | bytes 65536 | tf_op jit(solution)/shard_map/all_to_all | solution.py:26
  59.4 52.1 %copy-start.5 = (s32[32]{0:T(128)S(1)}, s32[32]{0:T(128)}, u32[]{:S(2)}) copy-start(s32[32]{0:T(128)} %param.14) | copy-start | bytes 388
  59.4 52.1 %copy-start.6 = (s32[32]{0:T(128)S(1)}, s32[32]{0:T(128)}, u32[]{:S(2)}) copy-start(s32[32]{0:T(128)} %param.13) | copy-start | bytes 388
  59.5 72.6 %copy-start.2 = (bf16[512,512]{1,0:T(8,128)(2,1)S(1)}, bf16[512,512]{1,0:T(8,128)(2,1)}, u32[]{:S(2)}) copy-start(bf16[512,512]{1,0:T(8,128)(2,1)} %refs_10_.1) | copy-start | bytes 1572868
  82.6 25.9 %collective-permute-start.7 = (bf16[1024,1024]{1,0:T(8,128)(2,1)S(1)}, bf16[1024,1024]{1,0:T(8,128)(2,1)}, u32[]{:S(2)}, u32[]{:S(2)}) collective-permute-start(bf16[1024,1024]{1,0:T(8,128)(2,1)S(1)} %broadcast_select_fusion), channel_id=1, source_target_pairs={{0,2},{1,7},{2,4},{3,1},{4,6},{5,3},{6,0},{7,5},{8,10},{9,15},{10,... | collective-permute-start | bytes 6291464 | tf_op jit(solution)/shard_map/ppermute | solution.py:42
  84.9 28.7 %collective-permute-start.5 = (bf16[1024,1024]{1,0:T(8,128)(2,1)}, bf16[1024,1024]{1,0:T(8,128)(2,1)}, u32[]{:S(2)}, u32[]{:S(2)}) collective-permute-start(bf16[1024,1024]{1,0:T(8,128)(2,1)} %collective-permute-done.1.refs_2_), channel_id=1, source_target_pairs={{0,1},{1,0},{2,3},{3,2},{4,5},{5,4},{6,7},{7,6},{8,9},{9,8},{10,11... | collective-permute-start | bytes 6291464 | tf_op jit(solution)/shard_map/ppermute | solution.py:34
  85.5 28.1 %collective-permute-start.6 = (bf16[1024,1024]{1,0:T(8,128)(2,1)}, bf16[1024,1024]{1,0:T(8,128)(2,1)}, u32[]{:S(2)}, u32[]{:S(2)}) collective-permute-start(bf16[1024,1024]{1,0:T(8,128)(2,1)} %collective-permute-done.2.refs_4_), channel_id=1, source_target_pairs={{0,1},{1,0},{2,3},{3,2},{4,5},{5,4},{6,7},{7,6},{8,9},{9,8},{10,11... | collective-permute-start | bytes 6291464 | tf_op jit(solution)/shard_map/ppermute | solution.py:34
  108.4 7.2 %collective-permute-start.8 = (bf16[1024,1024]{1,0:T(8,128)(2,1)}, bf16[1024,1024]{1,0:T(8,128)(2,1)}, u32[]{:S(2)}, u32[]{:S(2)}) collective-permute-start(bf16[1024,1024]{1,0:T(8,128)(2,1)} %collective-permute-done.7.refs_6_), channel_id=1, source_target_pairs={{0,1},{1,0},{2,3},{3,2},{4,5},{5,4},{6,7},{7,6},{8,9},{9,8},{10,11... | collective-permute-start | bytes 6291464 | tf_op jit(solution)/shard_map/ppermute | solution.py:34
  132.1 1.6 copy-start.1
  147.6 32.7 %copy-start.3 = (s32[32]{0:T(128)S(1)}, s32[32]{0:T(128)}, u32[]{:S(2)}) copy-start(s32[32]{0:T(128)} %param.15) | copy-start | bytes 388
  164.4 12.1 %all-to-all-start.5 = ((bf16[8,4,2048]{2,1,0:T(4,128)(2,1)}), bf16[8,4,2048]{2,1,0:T(4,128)(2,1)S(1)}, u32[]{:S(2)}, u32[]{:S(2)}) async-start(bf16[8,4,2048]{2,1,0:T(4,128)(2,1)} %all_to_all.44), calls=%async_computation.5 | async-start | bytes 262144 | tf_op jit(solution)/shard_map/all_to_all | solution.py:26
  176.5 12.4 %all-to-all-start.3 = ((bf16[32,2,256]{2,1,0:T(2,128)(2,1)}), bf16[32,2,256]{2,1,0:T(2,128)(2,1)S(1)}, u32[]{:S(2)}, u32[]{:S(2)}) async-start(bf16[32,2,256]{2,1,0:T(2,128)(2,1)} %reshape.94), calls=%async_computation.3 | async-start | bytes 65536 | tf_op jit(solution)/shard_map/all_to_all | solution.py:26
  188.9 17.9 %all-to-all-start.6 = ((bf16[32,2,2048]{2,1,0:T(2,128)(2,1)}), bf16[32,2,2048]{2,1,0:T(2,128)(2,1)S(1)}, u32[]{:S(2)}, u32[]{:S(2)}) async-start(bf16[32,2,2048]{2,1,0:T(2,128)(2,1)} %reshape.96), calls=%async_computation.6 | async-start | bytes 524288 | tf_op jit(solution)/shard_map/all_to_all | solution.py:26
  206.9 22.0 %all-to-all-start.4 = ((bf16[8,64,1024]{2,1,0:T(8,128)(2,1)}), bf16[8,64,1024]{2,1,0:T(8,128)(2,1)S(1)}, u32[]{:S(2)}, u32[]{:S(2)}) async-start(bf16[8,64,1024]{2,1,0:T(8,128)(2,1)} %shard_map.104), calls=%async_computation.4 | async-start | bytes 2097152 | tf_op jit(solution)/shard_map/all_to_all | solution.py:26
Sparse Core Ops, SparseCore 0:
  32.7 99.3 all-gather.2

commit v4 on v3

--- a/solution.py
+++ b/solution.py
@@ -63,7 +63,7 @@
         pltpu.make_async_copy(weight, w_buf.at[i], w_sem.at[i]).start()
     acc_ref[...] = jnp.zeros_like(acc_ref)
 
-    @pl.loop(0, parts)
+    @pl.loop(0, parts, unroll=True)
     def _(i):
         load(i).wait()
         pltpu.make_async_copy(w_buf.at[i], w_buf.at[i], w_sem.at[i]).wait()
@@ -123,9 +123,9 @@
     )(where, rows, *weights, low, out_map, cotan)
 
 
-def slot_kernel(slot_ref, shared_ref, out_ref):
+def slot_kernel(slot_ref, shared_ref, first_ref, out_ref):
     blocks, _ = slot_ref.shape
-    width = shared_ref.shape[1] // blocks
+    width = shared_ref.shape[1] // blocks - BLOCK_ROWS
     n_out = OWN * Y * N_DP
     row = lax.broadcasted_iota(jnp.int32, (n_out, N_DP), 0)
     lane = lax.broadcasted_iota(jnp.int32, (n_out, N_DP), 1)
@@ -138,10 +138,13 @@
         total = term if total is None else total + term
     for i in range(OWN * Y):
         out_ref[:, i * width:(i + 1) * width] = total[i * N_DP:(i + 1) * N_DP].astype(BF16)
-
-
-def in_grad_kernel(mine_ref, dlow_ref, rows_ref, out_ref, buf, acc_ref, sems):
+    dlow = jnp.sum(first_ref[:, blocks * width:].astype(F32), axis=0, keepdims=True)
+    out_ref[:, OWN * Y * width:] = jnp.broadcast_to(dlow, (N_DP, dlow.shape[1])).astype(BF16)
+
+
+def in_grad_kernel(mine_ref, got_ref, rows_ref, out_ref, buf, acc_ref, sems):
     parts, blocks, _, _ = rows_ref.shape
+    start = got_ref.shape[1] - blocks * BLOCK_ROWS
 
     def load(b):
         return pltpu.make_async_copy(rows_ref.at[:, b], buf.at[b], sems.at[b])
@@ -158,7 +161,7 @@
     for b in range(blocks):
         @pl.when(used(b))
         def _():
-            dlow = dlow_ref[:, b * BLOCK_ROWS:(b + 1) * BLOCK_ROWS].astype(F32)
+            dlow = got_ref[:, start + b * BLOCK_ROWS:start + (b + 1) * BLOCK_ROWS].astype(F32)
             left = jnp.concatenate(
                 [jnp.where(mine_ref[s * blocks + b] > 0, dlow, 0.0) for s in range(OWN)], 0).astype(BF16)
             load(b).wait()
@@ -171,7 +174,7 @@
     out_ref[...] = acc_ref[...].astype(BF16)
 
 
-def in_grad(mine, dlow, rows):
+def in_grad(mine, got, rows):
     parts, blocks, _, depth = rows.shape
     n_out = OWN * RANKS
     vmem_spec = pl.BlockSpec(memory_space=pltpu.VMEM)
@@ -189,7 +192,7 @@
         cost_estimate=pl.CostEstimate(
             flops=2 * parts * n_out * blocks * BLOCK_ROWS * depth,
             bytes_accessed=2 * parts * depth * blocks * BLOCK_ROWS, transcendentals=0),
-    )(mine, dlow, rows)
+    )(mine, got, rows)
 
 
 def out_grad_kernel(got_ref, out_ref):
@@ -211,9 +214,10 @@
     in_map = lax.dynamic_index_in_dim(adapter_in, block_adapter[dp], 0, False).reshape(RANKS, d_part)
     low_part = lax.dot_general(in_map, tokens, (((1,), (1,)), ((), ())), preferred_element_type=F32)
     low_sum = exchange(low_part.reshape(N_TENSOR, per, BLOCK_ROWS), TENSOR).sum(0).astype(BF16)
-    swapped, low_sum, flat = join((swapped, low_sum, gate_up.reshape(d_part, 2 * hidden_part)))
+    swapped, low_sum, gate_up = join((swapped, low_sum, gate_up))
     rows = lax.all_gather(swapped, DP, axis=0, tiled=False).reshape(Z, Y, BLOCK_ROWS, d_part)
 
+    flat = gate_up.reshape(d_part, 2 * hidden_part)
     left, right = hop(flat, "x", X, 1), hop(flat, "x", X, -1)
     own = hop(flat, "c", C, 1)
     low = spread(lax.ppermute(low_sum, DP + TENSOR, swap(0)), DP, N_DP)
@@ -237,15 +241,13 @@
     hidden, sent = project(where, rows, weights, low, out_map, d_hidden)
 
     first = exchange(sent, DP)
-    split = blocks * hidden_part
-    dlow = spread(first[:, split:].astype(F32).sum(0).astype(BF16), DP, N_DP)
-    shared = exchange(first[:, :split], TENSOR)
+    shared = exchange(first, TENSOR)
     merged = pl.pallas_call(
         slot_kernel,
-        out_shape=jax.ShapeDtypeStruct((N_DP, OWN * Y * hidden_part), BF16),
-    )(slot_lane, shared)
+        out_shape=jax.ShapeDtypeStruct((N_DP, OWN * Y * hidden_part + blocks * BLOCK_ROWS), BF16),
+    )(slot_lane, shared, first)
     got = exchange(merged, DP)
-    in_part = in_grad(jnp.append(mine.reshape(-1).astype(jnp.int32), tensor.astype(jnp.int32)), dlow, rows)
+    in_part = in_grad(jnp.append(mine.reshape(-1).astype(jnp.int32), tensor.astype(jnp.int32)), got, rows)
     grad_in = exchange(in_part, TENSOR).astype(F32).sum(0).reshape(OWN, 2, R, d_part)
     grad_out = pl.pallas_call(
         out_grad_kernel,

time: 238 us -> 230 us (0.966)
  starting transfers between devices: 69.5 us -> 51.8 us
  blocking collectives: 14.8 us -> 29.1 us
  local copies, waits for them, and re-layouts: 18.1 us -> 13.8 us
    all_to_all x6 -> x4, starting transfers between devices: 51.7 us -> 34.6 us  [exchange(): return lax.all_to_all(x, axes, 0, 0, tiled=True)]
    all_to_all x1 -> x2, blocking collectives: 14.8 us -> 29.1 us  [exchange(): return lax.all_to_all(x, axes, 0, 0, tiled=True)]
    unnamed x24 -> x21, local copies, waits for them, and re-layouts: 10.6 us -> 6.19 us
    all_gather x1, waiting for transfers between devices: 16.4 us -> 12.5 us  [body(): lax.all_gather(swapped, DP, axis=0, tiled=False)]
    all_to_all x6 -> x4, waiting for transfers between devices: 34.2 us -> 37.6 us  [exchange(): return lax.all_to_all(x, axes, 0, 0, tiled=True)]
  transfers between devices with their start and end apart: 16 -> 14, of which waited for: 12 -> 10; matrix products, arithmetic and copies ran while one was open for 8% -> 6% of each run, Pallas kernels for 2% -> 1%
where the time goes in v4:
time: 230 us; the launch traced here: 228 us
  waiting for transfers between devices  89.9 us (39%)
  starting transfers between devices  51.8 us (23%)
  blocking collectives  29.1 us (13%)
  Pallas kernels  19.7 us (9%)
  between operations  16.2 us (7%)
  local copies, waits for them, and re-layouts  13.8 us (6%)
  other arithmetic  6.4 us (3%)
    all_to_all x4, waiting for transfers between devices, exchange(): return lax.all_to_all(x, axes, 0, 0, tiled=True)  37.6 us
    all_to_all x4, starting transfers between devices, exchange(): return lax.all_to_all(x, axes, 0, 0, tiled=True)  34.6 us
    all_to_all x2, blocking collectives, exchange(): return lax.all_to_all(x, axes, 0, 0, tiled=True)  29.1 us
    ppermute x1, waiting for transfers between devices, last_hop(): lax.ppermute(jnp.where(lax.axis_index('c') == 0, up, down), (axis, 'c'),...  23.2 us
    ppermute x6, waiting for transfers between devices, hop(): return lax.ppermute(x, axis, [(i, (i + step) % n) for i in range(n)])  14.7 us
    pallas_call x1, Pallas kernels, project(): pl.pallas_call(block_kernel, in_specs=[pl.BlockSpec(memory_space=pltpu.SM...  13.8 us
    all_gather x1, waiting for transfers between devices, body(): lax.all_gather(swapped, DP, axis=0, tiled=False)  12.5 us
    ppermute x6, starting transfers between devices, hop(): return lax.ppermute(x, axis, [(i, (i + step) % n) for i in range(n)])  7.9 us
  transfers between devices with their start and end apart: 14, of which 10 were waited for; matrix products, arithmetic and copies ran while one was open for 6% of the time, Pallas kernels for 1%

profile of v4, /device:TPU:1, one launch (start us, length us, event | category | flops | bytes accessed | tf_op | source)
XLA Modules:
  0.0 228.1 jit_solution(11899430322924319444)
XLA Ops:
  7.2 5.1 %collective-permute-start = (bf16[128,1024]{1,0:T(8,128)(2,1)}, bf16[128,1024]{1,0:T(8,128)(2,1)S(1)}, u32[]{:S(2)}, u32[]{:S(2)}) collective-permute-start(bf16[128,1024]{1,0:T(8,128)(2,1)} %param.8), channel_id=1, source_target_pairs={{0,0},{1,32},{2,64},{3,96},{4,128},{5,160},{6,192},{7,224},{8,8},{... | collective-permute-start | bytes 786440 | tf_op jit(solution)/shard_map/ppermute | solution.py:213
  16.7 14.4 %all_to_all.48 = f32[8,4,128]{2,1,0:T(4,128)S(1)} all-to-all(f32[8,4,128]{2,1,0:T(4,128)S(1)} %fusion.3), channel_id=1, replica_groups=mesh['z'=8,'y'=4,'x'=4,'c'=2] {'x','c'}, dimensions={0} | all-to-all | bytes 32768 | tf_op jit(solution)/shard_map/all_to_all | solution.py:26
  31.8 3.5 %copy.36 = bf16[128,8,2,512]{3,1,2,0:T(8,128)(2,1)} copy(bf16[128,8,2,512]{3,2,1,0:T(2,128)(2,1)} %bitcast.40) | data formatting | bytes 4194304
  35.6 2.4 %collective-permute-start.2 = (bf16[1024,1024]{1,0:T(8,128)(2,1)}, bf16[1024,1024]{1,0:T(8,128)(2,1)}, u32[]{:S(2)}, u32[]{:S(2)}) collective-permute-start(bf16[1024,1024]{1,0:T(8,128)(2,1)} %bitcast.23.refs_0_), channel_id=1, source_target_pairs={{0,6},{2,0},{4,2},{6,4},{1,7},{3,1},{5,3},{7,5},{8,14},{10,8},{12,... | collective-permute-start | bytes 6291464 | tf_op jit(solution)/shard_map/ppermute | solution.py:34
  39.3 3.3 %collective-permute-start.4 = (bf16[4,128]{1,0:T(4,128)(2,1)S(1)}, bf16[4,128]{1,0:T(4,128)(2,1)S(1)}, u32[]{:S(2)}, u32[]{:S(2)}) collective-permute-start(bf16[4,128]{1,0:T(4,128)(2,1)S(1)} %reduce_sum.18), channel_id=1, source_target_pairs={{0,0},{1,32},{2,64},{3,96},{4,128},{5,160},{6,192},{7,224},{8,8},{... | collective-permute-start | bytes 3080 | tf_op jit(solution)/shard_map/ppermute | solution.py:223
  42.7 1.9 collective-permute-done.4
  45.2 17.6 %all-to-all-start.1 = ((bf16[32,4,128]{2,1,0:T(4,128)(2,1)}), bf16[32,4,128]{2,1,0:T(4,128)(2,1)S(1)}, u32[]{:S(2)}, u32[]{:S(2)}) async-start(bf16[32,4,128]{2,1,0:T(4,128)(2,1)} %broadcast_in_dim.21), calls=%async_computation.1 | async-start | bytes 65536 | tf_op jit(solution)/shard_map/all_to_all | solution.py:26
  62.9 9.4 %all-to-all-done.1 = bf16[32,4,128]{2,1,0:T(4,128)(2,1)S(1)} async-done(((bf16[32,4,128]{2,1,0:T(4,128)(2,1)}), bf16[32,4,128]{2,1,0:T(4,128)(2,1)S(1)}, u32[]{:S(2)}, u32[]{:S(2)}) %all-to-all-start.1) | async-done | bytes 32800 | tf_op jit(solution)/shard_map/all_to_all | solution.py:26
  72.3 11.0 %collective-permute-done.1.refs_2_ = bf16[1024,1024]{1,0:T(8,128)(2,1)} collective-permute-done((bf16[1024,1024]{1,0:T(8,128)(2,1)}, bf16[1024,1024]{1,0:T(8,128)(2,1)}, u32[]{:S(2)}, u32[]{:S(2)}) %collective-permute-start.1) | collective-permute-done | bytes 2097184 | tf_op jit(solution)/shard_map/ppermute | solution.py:34
  85.0 1.8 broadcast_select_fusion
  89.1 23.2 %collective-permute-done.7.refs_6_ = bf16[1024,1024]{1,0:T(8,128)(2,1)} collective-permute-done((bf16[1024,1024]{1,0:T(8,128)(2,1)S(1)}, bf16[1024,1024]{1,0:T(8,128)(2,1)}, u32[]{:S(2)}, u32[]{:S(2)}) %collective-permute-start.7) | collective-permute-done | bytes 2097184 | tf_op jit(solution)/shard_map/ppermute | solution.py:42
  112.2 2.6 %collective-permute-start.8 = (bf16[1024,1024]{1,0:T(8,128)(2,1)}, bf16[1024,1024]{1,0:T(8,128)(2,1)}, u32[]{:S(2)}, u32[]{:S(2)}) collective-permute-start(bf16[1024,1024]{1,0:T(8,128)(2,1)} %collective-permute-done.7.refs_6_), channel_id=1, source_target_pairs={{0,1},{1,0},{2,3},{3,2},{4,5},{5,4},{6,7},{7,6},{8,9},{9,8},{10,11... | collective-permute-start | bytes 6291464 | tf_op jit(solution)/shard_map/ppermute | solution.py:34
  116.9 2.0 collective-permute-done.8.refs_7_
  118.9 12.5 %all-gather.3.cloned.1.call-done = bf16[4096,1024]{1,0:T(8,128)(2,1)} async-done(((bf16[128,1024]{1,0:T(8,128)(2,1)}), bf16[4096,1024]{1,0:T(8,128)(2,1)}) %all-gather.3.cloned.1.call-update) | async-done | bytes 8388624 | tf_op jit(solution)/shard_map/all_gather | solution.py:218
  131.5 13.8 %shard_map.103 = (bf16[512,512]{1,0:T(8,128)(2,1)}, bf16[32,2560]{1,0:T(8,128)(2,1)S(1)}) custom-call(s32[5]{0:T(128)S(1)} %pad_add_fusion.where_ref, bf16[8,4,128,1024]{3,2,1,0:T(8,128)(2,1)} %bitcast.38, bf16[1024,1024]{1,0:T(8,128)(2,1)} %bitcast.23.refs_0_, bf16[1024,1024]{1,0:T(8,128)(2,1)} %collective-permute-done.3.refs_1_, ...), custom_call_target="tpu_custom_call" | custom-call | flops 8589934592 | bytes 25165824 | tf_op jit(solution)/shard_map/pallas_call | solution.py:103
  146.6 14.8 %all_to_all.49 = bf16[32,2,1280]{2,1,0:T(2,128)(2,1)S(1)} all-to-all(bf16[32,2,1280]{2,1,0:T(2,128)(2,1)S(1)} %reshape.88), channel_id=1, replica_groups=mesh['z'=8,'y'=4,'x'=4,'c'=2] {'z','y'}, dimensions={0} | all-to-all | bytes 327680 | tf_op jit(solution)/shard_map/all_to_all | solution.py:26
  163.2 6.8 %all-to-all-start.3 = ((bf16[8,4,2560]{2,1,0:T(4,128)(2,1)}), bf16[8,4,2560]{2,1,0:T(4,128)(2,1)S(1)}, u32[]{:S(2)}, u32[]{:S(2)}) async-start(bf16[8,4,2560]{2,1,0:T(4,128)(2,1)} %all_to_all.34), calls=%async_computation.3 | async-start | bytes 327680 | tf_op jit(solution)/shard_map/all_to_all | solution.py:26
  172.3 3.2 %all-to-all-done.3 = bf16[8,4,2560]{2,1,0:T(4,128)(2,1)S(1)} async-done(((bf16[8,4,2560]{2,1,0:T(4,128)(2,1)}), bf16[8,4,2560]{2,1,0:T(4,128)(2,1)S(1)}, u32[]{:S(2)}, u32[]{:S(2)}) %all-to-all-start.3) | async-done | bytes 163872 | tf_op jit(solution)/shard_map/all_to_all | solution.py:26
  176.3 2.1 shard_map.104
  180.9 3.9 %all-to-all-start.4 = ((bf16[32,2,2304]{2,1,0:T(2,128)(2,1)}), bf16[32,2,2304]{2,1,0:T(2,128)(2,1)S(1)}, u32[]{:S(2)}, u32[]{:S(2)}) async-start(bf16[32,2,2304]{2,1,0:T(2,128)(2,1)} %reshape.90), calls=%async_computation.4 | async-start | bytes 589824 | tf_op jit(solution)/shard_map/all_to_all | solution.py:26
  185.1 11.6 %all-to-all-done.4 = bf16[32,2,2304]{2,1,0:T(2,128)(2,1)S(1)} async-done(((bf16[32,2,2304]{2,1,0:T(2,128)(2,1)}), bf16[32,2,2304]{2,1,0:T(2,128)(2,1)S(1)}, u32[]{:S(2)}, u32[]{:S(2)}) %all-to-all-start.4) | async-done | bytes 294944 | tf_op jit(solution)/shard_map/all_to_all | solution.py:26
  197.0 1.9 shard_map.105
  198.9 6.3 %all-to-all-start.5 = ((bf16[8,64,1024]{2,1,0:T(8,128)(2,1)}), bf16[8,64,1024]{2,1,0:T(8,128)(2,1)S(1)}, u32[]{:S(2)}, u32[]{:S(2)}) async-start(bf16[8,64,1024]{2,1,0:T(8,128)(2,1)} %shard_map.105), calls=%async_computation.5 | async-start | bytes 2097152 | tf_op jit(solution)/shard_map/all_to_all | solution.py:26
  207.0 13.3 %all-to-all-done.5 = bf16[8,64,1024]{2,1,0:T(8,128)(2,1)S(1)} async-done(((bf16[8,64,1024]{2,1,0:T(8,128)(2,1)}), bf16[8,64,1024]{2,1,0:T(8,128)(2,1)S(1)}, u32[]{:S(2)}, u32[]{:S(2)}) %all-to-all-start.5) | async-done | bytes 1048608 | tf_op jit(solution)/shard_map/all_to_all | solution.py:26
  (67 shorter events, 23.3 us)
Async XLA Ops:
  7.2 8.3 %copy-start = (bf16[32,2,16,1024]{3,2,1,0:T(8,128)(2,1)S(1)}, bf16[32,2,16,1024]{3,2,1,0:T(8,128)(2,1)}, u32[]{:S(2)}) copy-start(bf16[32,2,16,1024]{3,2,1,0:T(8,128)(2,1)} %param.10) | copy-start | bytes 6291460
  7.2 124.3 %all-gather.3.cloned.1.call-start = ((), (), s32[]{:S(2)}) async-start(), calls=%async_computation.6 | async-start | bytes 8650752 | tf_op jit(solution)/shard_map/all_gather | solution.py:218
  7.2 23.9 %collective-permute-start = (bf16[128,1024]{1,0:T(8,128)(2,1)}, bf16[128,1024]{1,0:T(8,128)(2,1)S(1)}, u32[]{:S(2)}, u32[]{:S(2)}) collective-permute-start(bf16[128,1024]{1,0:T(8,128)(2,1)} %param.8), channel_id=1, source_target_pairs={{0,0},{1,32},{2,64},{3,96},{4,128},{5,160},{6,192},{7,224},{8,8},{... | collective-permute-start | bytes 786440 | tf_op jit(solution)/shard_map/ppermute | solution.py:213
  31.1 0.7 copy-start.4
  35.4 48.0 %collective-permute-start.1 = (bf16[1024,1024]{1,0:T(8,128)(2,1)}, bf16[1024,1024]{1,0:T(8,128)(2,1)}, u32[]{:S(2)}, u32[]{:S(2)}) collective-permute-start(bf16[1024,1024]{1,0:T(8,128)(2,1)} %bitcast.23.refs_0_), channel_id=1, source_target_pairs={{0,2},{2,4},{4,6},{6,0},{1,3},{3,5},{5,7},{7,1},{8,10},{10,12},{12... | collective-permute-start | bytes 6291464 | tf_op jit(solution)/shard_map/ppermute | solution.py:34
  35.6 49.4 %collective-permute-start.2 = (bf16[1024,1024]{1,0:T(8,128)(2,1)}, bf16[1024,1024]{1,0:T(8,128)(2,1)}, u32[]{:S(2)}, u32[]{:S(2)}) collective-permute-start(bf16[1024,1024]{1,0:T(8,128)(2,1)} %bitcast.23.refs_0_), channel_id=1, source_target_pairs={{0,6},{2,0},{4,2},{6,4},{1,7},{3,1},{5,3},{7,5},{8,14},{10,8},{12,... | collective-permute-start | bytes 6291464 | tf_op jit(solution)/shard_map/ppermute | solution.py:34
  38.0 47.0 %collective-permute-start.3 = (bf16[1024,1024]{1,0:T(8,128)(2,1)}, bf16[1024,1024]{1,0:T(8,128)(2,1)}, u32[]{:S(2)}, u32[]{:S(2)}) collective-permute-start(bf16[1024,1024]{1,0:T(8,128)(2,1)} %bitcast.23.refs_0_), channel_id=1, source_target_pairs={{0,1},{1,0},{2,3},{3,2},{4,5},{5,4},{6,7},{7,6},{8,9},{9,8},{10,11... | collective-permute-start | bytes 6291464 | tf_op jit(solution)/shard_map/ppermute | solution.py:34
  39.3 5.3 %collective-permute-start.4 = (bf16[4,128]{1,0:T(4,128)(2,1)S(1)}, bf16[4,128]{1,0:T(4,128)(2,1)S(1)}, u32[]{:S(2)}, u32[]{:S(2)}) collective-permute-start(bf16[4,128]{1,0:T(4,128)(2,1)S(1)} %reduce_sum.18), channel_id=1, source_target_pairs={{0,0},{1,32},{2,64},{3,96},{4,128},{5,160},{6,192},{7,224},{8,8},{... | collective-permute-start | bytes 3080 | tf_op jit(solution)/shard_map/ppermute | solution.py:223
  45.2 27.1 %all-to-all-start.1 = ((bf16[32,4,128]{2,1,0:T(4,128)(2,1)}), bf16[32,4,128]{2,1,0:T(4,128)(2,1)S(1)}, u32[]{:S(2)}, u32[]{:S(2)}) async-start(bf16[32,4,128]{2,1,0:T(4,128)(2,1)} %broadcast_in_dim.21), calls=%async_computation.1 | async-start | bytes 65536 | tf_op jit(solution)/shard_map/all_to_all | solution.py:26
  62.9 51.9 %copy-start.5 = (s32[32]{0:T(128)S(1)}, s32[32]{0:T(128)}, u32[]{:S(2)}) copy-start(s32[32]{0:T(128)} %param.14) | copy-start | bytes 388
  62.9 52.0 %copy-start.6 = (s32[32]{0:T(128)S(1)}, s32[32]{0:T(128)}, u32[]{:S(2)}) copy-start(s32[32]{0:T(128)} %param.13) | copy-start | bytes 388
  62.9 68.6 %copy-start.2 = (bf16[512,512]{1,0:T(8,128)(2,1)S(1)}, bf16[512,512]{1,0:T(8,128)(2,1)}, u32[]{:S(2)}) copy-start(bf16[512,512]{1,0:T(8,128)(2,1)} %refs_10_.1) | copy-start | bytes 1572868
  86.9 25.4 %collective-permute-start.7 = (bf16[1024,1024]{1,0:T(8,128)(2,1)S(1)}, bf16[1024,1024]{1,0:T(8,128)(2,1)}, u32[]{:S(2)}, u32[]{:S(2)}) collective-permute-start(bf16[1024,1024]{1,0:T(8,128)(2,1)S(1)} %broadcast_select_fusion), channel_id=1, source_target_pairs={{0,2},{1,7},{2,4},{3,1},{4,6},{5,3},{6,0},{7,5},{8,10},{9,15},{10,... | collective-permute-start | bytes 6291464 | tf_op jit(solution)/shard_map/ppermute | solution.py:42
  87.7 29.2 %collective-permute-start.5 = (bf16[1024,1024]{1,0:T(8,128)(2,1)}, bf16[1024,1024]{1,0:T(8,128)(2,1)}, u32[]{:S(2)}, u32[]{:S(2)}) collective-permute-start(bf16[1024,1024]{1,0:T(8,128)(2,1)} %collective-permute-done.1.refs_2_), channel_id=1, source_target_pairs={{0,1},{1,0},{2,3},{3,2},{4,5},{5,4},{6,7},{7,6},{8,9},{9,8},{10,11... | collective-permute-start | bytes 6291464 | tf_op jit(solution)/shard_map/ppermute | solution.py:34
  89.0 27.9 %collective-permute-start.6 = (bf16[1024,1024]{1,0:T(8,128)(2,1)}, bf16[1024,1024]{1,0:T(8,128)(2,1)}, u32[]{:S(2)}, u32[]{:S(2)}) collective-permute-start(bf16[1024,1024]{1,0:T(8,128)(2,1)} %collective-permute-done.2.refs_4_), channel_id=1, source_target_pairs={{0,1},{1,0},{2,3},{3,2},{4,5},{5,4},{6,7},{7,6},{8,9},{9,8},{10,11... | collective-permute-start | bytes 6291464 | tf_op jit(solution)/shard_map/ppermute | solution.py:34
  112.2 6.7 %collective-permute-start.8 = (bf16[1024,1024]{1,0:T(8,128)(2,1)}, bf16[1024,1024]{1,0:T(8,128)(2,1)}, u32[]{:S(2)}, u32[]{:S(2)}) collective-permute-start(bf16[1024,1024]{1,0:T(8,128)(2,1)} %collective-permute-done.7.refs_6_), channel_id=1, source_target_pairs={{0,1},{1,0},{2,3},{3,2},{4,5},{5,4},{6,7},{7,6},{8,9},{9,8},{10,11... | collective-permute-start | bytes 6291464 | tf_op jit(solution)/shard_map/ppermute | solution.py:34
  145.3 24.7 %copy-start.3 = (s32[32]{0:T(128)S(1)}, s32[32]{0:T(128)}, u32[]{:S(2)}) copy-start(s32[32]{0:T(128)} %param.15) | copy-start | bytes 388
  163.2 12.4 %all-to-all-start.3 = ((bf16[8,4,2560]{2,1,0:T(4,128)(2,1)}), bf16[8,4,2560]{2,1,0:T(4,128)(2,1)S(1)}, u32[]{:S(2)}, u32[]{:S(2)}) async-start(bf16[8,4,2560]{2,1,0:T(4,128)(2,1)} %all_to_all.34), calls=%async_computation.3 | async-start | bytes 327680 | tf_op jit(solution)/shard_map/all_to_all | solution.py:26
  180.9 15.8 %all-to-all-start.4 = ((bf16[32,2,2304]{2,1,0:T(2,128)(2,1)}), bf16[32,2,2304]{2,1,0:T(2,128)(2,1)S(1)}, u32[]{:S(2)}, u32[]{:S(2)}) async-start(bf16[32,2,2304]{2,1,0:T(2,128)(2,1)} %reshape.90), calls=%async_computation.4 | async-start | bytes 589824 | tf_op jit(solution)/shard_map/all_to_all | solution.py:26
  197.0 1.9 copy-start.1
  198.9 21.4 %all-to-all-start.5 = ((bf16[8,64,1024]{2,1,0:T(8,128)(2,1)}), bf16[8,64,1024]{2,1,0:T(8,128)(2,1)S(1)}, u32[]{:S(2)}, u32[]{:S(2)}) async-start(bf16[8,64,1024]{2,1,0:T(8,128)(2,1)} %shard_map.105), calls=%async_computation.5 | async-start | bytes 2097152 | tf_op jit(solution)/shard_map/all_to_all | solution.py:26
Sparse Core Ops, SparseCore 0:
  31.9 99.4 all-gather.2

commit v5 on v4

--- a/solution.py
+++ b/solution.py
@@ -17,8 +17,11 @@
 VMEM_LIMIT = 48 * 2 ** 20
 
 
-def swap(skew):
-    return [((z * Y + y) * N_TENSOR + t, (((t + skew * z) % Z) * Y + y) * N_TENSOR + z)
+STEPS = (1, -1, 2, -2, 3, -3, 0, 4)
+
+
+def swap(place):
+    return [((z * Y + y) * N_TENSOR + t, (place(z, t) * Y + y) * N_TENSOR + z)
             for z in range(Z) for y in range(Y) for t in range(N_TENSOR)]
 
 
@@ -49,26 +52,24 @@
     t = where_ref[0]
 
     def place(i):
-        x, c = lax.div(t, C), lax.rem(t, C)
-        step, other = lax.div(i, C), lax.rem(i, C)
-        back = jnp.where(step < 2, step, 5 - step)
-        feature = lax.rem(x - back + X, X) * C + lax.rem(c + other, C)
-        return lax.rem(feature + t, parts)
+        x, c = lax.rem(lax.div(t, C) - (0, 1, 3, 2)[i // C] + X, X), lax.rem(t + i % C, C)
+        step = jnp.where(c == 0, x + 1, -x - 1)
+        step = jnp.where(x == X - 1, jnp.where(c == 0, 0, 4), step)
+        return lax.rem(t + step + parts, parts)
 
     def load(i):
-        return pltpu.make_async_copy(rows_ref.at[place(i)], x_buf.at[i], x_sem.at[i])
+        return pltpu.make_async_copy(rows_ref.at[:, place(i)], x_buf.at[i], x_sem.at[i])
 
     for i, weight in enumerate(weights):
         load(i).start()
         pltpu.make_async_copy(weight, w_buf.at[i], w_sem.at[i]).start()
-    acc_ref[...] = jnp.zeros_like(acc_ref)
-
-    @pl.loop(0, parts, unroll=True)
-    def _(i):
+
+    for i, weight in enumerate(weights):
         load(i).wait()
-        pltpu.make_async_copy(w_buf.at[i], w_buf.at[i], w_sem.at[i]).wait()
+        pltpu.make_async_copy(weight, w_buf.at[i], w_sem.at[i]).wait()
         rows = x_buf[i].reshape(blocks * BLOCK_ROWS, depth)
-        acc_ref[...] += jnp.dot(rows, w_buf[i], preferred_element_type=F32)
+        part = jnp.dot(rows, w_buf[i], preferred_element_type=F32)
+        acc_ref[...] = part if i == 0 else acc_ref[...] + part
 
     half = cot_ref.shape[1]
     for b in range(blocks):
@@ -96,7 +97,7 @@
 
 
 def project(where, rows, weights, low, out_map, cotan):
-    parts, blocks, _, depth = rows.shape
+    blocks, parts, _, depth = rows.shape
     n_rows, half = cotan.shape
     any_spec = pl.BlockSpec(memory_space=pl.ANY)
     vmem_spec = pl.BlockSpec(memory_space=pltpu.VMEM)
@@ -109,7 +110,7 @@
             jax.ShapeDtypeStruct((RANKS, blocks * (half + BLOCK_ROWS)), BF16),
         ],
         scratch_shapes=[
-            pltpu.VMEM(rows.shape, BF16),
+            pltpu.VMEM((parts, blocks, BLOCK_ROWS, depth), BF16),
             pltpu.VMEM((parts,) + weights[0].shape, BF16),
             pltpu.VMEM((n_rows, 2 * half), F32),
             pltpu.SemaphoreType.DMA((parts,)),
@@ -143,11 +144,11 @@
 
 
 def in_grad_kernel(mine_ref, got_ref, rows_ref, out_ref, buf, acc_ref, sems):
-    parts, blocks, _, _ = rows_ref.shape
+    blocks, parts, _, _ = rows_ref.shape
     start = got_ref.shape[1] - blocks * BLOCK_ROWS
 
     def load(b):
-        return pltpu.make_async_copy(rows_ref.at[:, b], buf.at[b], sems.at[b])
+        return pltpu.make_async_copy(rows_ref.at[b], buf.at[b], sems.at[b])
 
     def used(b):
         return mine_ref[b] + mine_ref[blocks + b] > 0
@@ -166,16 +167,15 @@
                 [jnp.where(mine_ref[s * blocks + b] > 0, dlow, 0.0) for s in range(OWN)], 0).astype(BF16)
             load(b).wait()
 
-            @pl.loop(0, parts)
-            def _(k):
-                feature = lax.rem(k - mine_ref[OWN * blocks] + parts, parts)
-                acc_ref[feature] += jnp.dot(left, buf[b, k], preferred_element_type=F32)
+            for feature, step in enumerate(STEPS):
+                place = lax.rem(mine_ref[OWN * blocks] + step + parts, parts)
+                acc_ref[feature] += jnp.dot(left, buf[b, place], preferred_element_type=F32)
 
     out_ref[...] = acc_ref[...].astype(BF16)
 
 
 def in_grad(mine, got, rows):
-    parts, blocks, _, depth = rows.shape
+    blocks, parts, _, depth = rows.shape
     n_out = OWN * RANKS
     vmem_spec = pl.BlockSpec(memory_space=pltpu.VMEM)
     return pl.pallas_call(
@@ -210,17 +210,17 @@
 
     join = lax.optimization_barrier
 
-    swapped = lax.ppermute(tokens, DP + TENSOR, swap(1))
+    swapped = lax.ppermute(tokens, DP + TENSOR, swap(lambda z, t: (z + STEPS[t]) % Z))
     in_map = lax.dynamic_index_in_dim(adapter_in, block_adapter[dp], 0, False).reshape(RANKS, d_part)
     low_part = lax.dot_general(in_map, tokens, (((1,), (1,)), ((), ())), preferred_element_type=F32)
     low_sum = exchange(low_part.reshape(N_TENSOR, per, BLOCK_ROWS), TENSOR).sum(0).astype(BF16)
-    swapped, low_sum, gate_up = join((swapped, low_sum, gate_up))
-    rows = lax.all_gather(swapped, DP, axis=0, tiled=False).reshape(Z, Y, BLOCK_ROWS, d_part)
+    rows = lax.all_gather(swapped, ("y", "z"), axis=0, tiled=False).reshape(Y, Z, BLOCK_ROWS, d_part)
+    low_sum, gate_up, _ = join((low_sum, gate_up, swapped))
 
     flat = gate_up.reshape(d_part, 2 * hidden_part)
     left, right = hop(flat, "x", X, 1), hop(flat, "x", X, -1)
     own = hop(flat, "c", C, 1)
-    low = spread(lax.ppermute(low_sum, DP + TENSOR, swap(0)), DP, N_DP)
+    low = spread(lax.ppermute(low_sum, DP + TENSOR, swap(lambda z, t: t)), DP, N_DP)
     left, right, own, low = join((left, right, own, low))
     far = last_hop(left, right, "x", X)
     weights = [flat, own, left, hop(left, "c", C, 1), right, hop(right, "c", C, 1), far, hop(far, "c", C, 1)]

time: 230 us -> 228 us (level)
  waiting for transfers between devices: 89.9 us -> 81 us
  blocking collectives: 29.1 us -> 35.1 us
    all_gather x1, waiting for transfers between devices: 12.5 us -> 0.01 us  [body(): lax.all_gather(swapped, ('y', 'z'), axis=0, tiled=False)]
    all_to_all x2, blocking collectives: 29.1 us -> 35.1 us  [exchange(): return lax.all_to_all(x, axes, 0, 0, tiled=True)]
    ppermute x2, waiting for transfers between devices: 1.93 us -> 5.95 us  [the longest x1 3.61 us: body(): lax.ppermute(tokens, DP + TENSOR, swap(lambda z, t: (z + STEPS[t]) % Z))]
    ppermute x2, starting transfers between devices: 8.41 us -> 11.9 us  [the longest x1 9.01 us: body(): lax.ppermute(tokens, DP + TENSOR, swap(lambda z, t: (z + STEPS[t]) % Z))]
    all_to_all x4, starting transfers between devices: 34.6 us -> 31.4 us  [exchange(): return lax.all_to_all(x, axes, 0, 0, tiled=True)]
  transfers between devices with their start and end apart: 14 -> 14, of which waited for: 10 -> 9; matrix products, arithmetic and copies ran while one was open for 6% -> 6% of each run, Pallas kernels for 1% -> 1%
where the time goes in v5:
time: 228 us; the launch traced here: 227 us
  waiting for transfers between devices  81 us (36%)
  starting transfers between devices  53.9 us (24%)
  blocking collectives  35.1 us (15%)
  Pallas kernels  19.7 us (9%)
  between operations  16.2 us (7%)
  local copies, waits for them, and re-layouts  13.8 us (6%)
  other arithmetic  6.41 us (3%)
    all_to_all x4, waiting for transfers between devices, exchange(): return lax.all_to_all(x, axes, 0, 0, tiled=True)  36.8 us
    all_to_all x2, blocking collectives, exchange(): return lax.all_to_all(x, axes, 0, 0, tiled=True)  35.1 us
    all_to_all x4, starting transfers between devices, exchange(): return lax.all_to_all(x, axes, 0, 0, tiled=True)  31.4 us
    ppermute x1, waiting for transfers between devices, last_hop(): lax.ppermute(jnp.where(lax.axis_index('c') == 0, up, down), (axis, 'c'),...  22.5 us
    ppermute x6, waiting for transfers between devices, hop(): return lax.ppermute(x, axis, [(i, (i + step) % n) for i in range(n)])  15.7 us
    pallas_call x1, Pallas kernels, project(): pl.pallas_call(block_kernel, in_specs=[pl.BlockSpec(memory_space=pltpu.SM...  13.8 us
    ppermute x1, starting transfers between devices, body(): lax.ppermute(tokens, DP + TENSOR, swap(lambda z, t: (z + STEPS[t]) % Z))  9.01 us
    ppermute x6, starting transfers between devices, hop(): return lax.ppermute(x, axis, [(i, (i + step) % n) for i in range(n)])  8.04 us
  transfers between devices with their start and end apart: 14, of which 9 were waited for; matrix products, arithmetic and copies ran while one was open for 6% of the time, Pallas kernels for 1%

profile of v5, /device:TPU:1, one launch (start us, length us, event | category | flops | bytes accessed | tf_op | source)
XLA Modules:
  0.0 227.3 jit_solution(42700625925195616)
XLA Ops:
  7.2 9.0 %collective-permute-start = (bf16[128,1024]{1,0:T(8,128)(2,1)}, bf16[128,1024]{1,0:T(8,128)(2,1)S(1)}, u32[]{:S(2)}, u32[]{:S(2)}) collective-permute-start(bf16[128,1024]{1,0:T(8,128)(2,1)} %param.8), channel_id=1, source_target_pairs={{0,32},{1,224},{2,64},{3,192},{4,96},{5,160},{6,0},{7,128},{8,40},... | collective-permute-start | bytes 786440 | tf_op jit(solution)/shard_map/ppermute | solution.py:213
  16.2 3.6 %collective-permute-done = bf16[128,1024]{1,0:T(8,128)(2,1)S(1)} collective-permute-done((bf16[128,1024]{1,0:T(8,128)(2,1)}, bf16[128,1024]{1,0:T(8,128)(2,1)S(1)}, u32[]{:S(2)}, u32[]{:S(2)}) %collective-permute-start) | collective-permute-done | bytes 262176 | tf_op jit(solution)/shard_map/ppermute | solution.py:213
  25.0 15.2 %all_to_all.48 = f32[8,4,128]{2,1,0:T(4,128)S(1)} all-to-all(f32[8,4,128]{2,1,0:T(4,128)S(1)} %fusion.3), channel_id=1, replica_groups=mesh['z'=8,'y'=4,'x'=4,'c'=2] {'x','c'}, dimensions={0} | all-to-all | bytes 32768 | tf_op jit(solution)/shard_map/all_to_all | solution.py:29
  40.2 3.6 %copy.36 = bf16[128,8,2,512]{3,1,2,0:T(8,128)(2,1)} copy(bf16[128,8,2,512]{3,2,1,0:T(2,128)(2,1)} %bitcast.40) | data formatting | bytes 4194304
  44.1 2.4 %collective-permute-start.2 = (bf16[1024,1024]{1,0:T(8,128)(2,1)}, bf16[1024,1024]{1,0:T(8,128)(2,1)}, u32[]{:S(2)}, u32[]{:S(2)}) collective-permute-start(bf16[1024,1024]{1,0:T(8,128)(2,1)} %bitcast.23.refs_0_), channel_id=1, source_target_pairs={{0,6},{2,0},{4,2},{6,4},{1,7},{3,1},{5,3},{7,5},{8,14},{10,8},{12,... | collective-permute-start | bytes 6291464 | tf_op jit(solution)/shard_map/ppermute | solution.py:37
  47.8 2.9 %collective-permute-start.4 = (bf16[4,128]{1,0:T(4,128)(2,1)S(1)}, bf16[4,128]{1,0:T(4,128)(2,1)S(1)}, u32[]{:S(2)}, u32[]{:S(2)}) collective-permute-start(bf16[4,128]{1,0:T(4,128)(2,1)S(1)} %reduce_sum.18), channel_id=1, source_target_pairs={{0,0},{1,32},{2,64},{3,96},{4,128},{5,160},{6,192},{7,224},{8,8},{... | collective-permute-start | bytes 3080 | tf_op jit(solution)/shard_map/ppermute | solution.py:223
  50.7 2.3 %collective-permute-done.4 = bf16[4,128]{1,0:T(4,128)(2,1)S(1)} collective-permute-done((bf16[4,128]{1,0:T(4,128)(2,1)S(1)}, bf16[4,128]{1,0:T(4,128)(2,1)S(1)}, u32[]{:S(2)}, u32[]{:S(2)}) %collective-permute-start.4) | collective-permute-done | bytes 1056 | tf_op jit(solution)/shard_map/ppermute | solution.py:223
  53.7 15.7 %all-to-all-start.1 = ((bf16[32,4,128]{2,1,0:T(4,128)(2,1)}), bf16[32,4,128]{2,1,0:T(4,128)(2,1)S(1)}, u32[]{:S(2)}, u32[]{:S(2)}) async-start(bf16[32,4,128]{2,1,0:T(4,128)(2,1)} %broadcast_in_dim.21), calls=%async_computation.1 | async-start | bytes 65536 | tf_op jit(solution)/shard_map/all_to_all | solution.py:29
  69.4 8.7 %all-to-all-done.1 = bf16[32,4,128]{2,1,0:T(4,128)(2,1)S(1)} async-done(((bf16[32,4,128]{2,1,0:T(4,128)(2,1)}), bf16[32,4,128]{2,1,0:T(4,128)(2,1)S(1)}, u32[]{:S(2)}, u32[]{:S(2)}) %all-to-all-start.1) | async-done | bytes 32800 | tf_op jit(solution)/shard_map/all_to_all | solution.py:29
  78.1 13.7 %collective-permute-done.1.refs_2_ = bf16[1024,1024]{1,0:T(8,128)(2,1)} collective-permute-done((bf16[1024,1024]{1,0:T(8,128)(2,1)}, bf16[1024,1024]{1,0:T(8,128)(2,1)}, u32[]{:S(2)}, u32[]{:S(2)}) %collective-permute-start.1) | collective-permute-done | bytes 2097184 | tf_op jit(solution)/shard_map/ppermute | solution.py:37
  93.6 2.5 %collective-permute-start.7 = (bf16[1024,1024]{1,0:T(8,128)(2,1)S(1)}, bf16[1024,1024]{1,0:T(8,128)(2,1)}, u32[]{:S(2)}, u32[]{:S(2)}) collective-permute-start(bf16[1024,1024]{1,0:T(8,128)(2,1)S(1)} %broadcast_select_fusion), channel_id=1, source_target_pairs={{0,2},{1,7},{2,4},{3,1},{4,6},{5,3},{6,0},{7,5},{8,10},{9,15},{10,... | collective-permute-start | bytes 6291464 | tf_op jit(solution)/shard_map/ppermute | solution.py:45
  96.6 22.5 %collective-permute-done.7.refs_6_ = bf16[1024,1024]{1,0:T(8,128)(2,1)} collective-permute-done((bf16[1024,1024]{1,0:T(8,128)(2,1)S(1)}, bf16[1024,1024]{1,0:T(8,128)(2,1)}, u32[]{:S(2)}, u32[]{:S(2)}) %collective-permute-start.7) | collective-permute-done | bytes 2097184 | tf_op jit(solution)/shard_map/ppermute | solution.py:45
  119.1 3.6 %collective-permute-start.8 = (bf16[1024,1024]{1,0:T(8,128)(2,1)}, bf16[1024,1024]{1,0:T(8,128)(2,1)}, u32[]{:S(2)}, u32[]{:S(2)}) collective-permute-start(bf16[1024,1024]{1,0:T(8,128)(2,1)} %collective-permute-done.7.refs_6_), channel_id=1, source_target_pairs={{0,1},{1,0},{2,3},{3,2},{4,5},{5,4},{6,7},{7,6},{8,9},{9,8},{10,11... | collective-permute-start | bytes 6291464 | tf_op jit(solution)/shard_map/ppermute | solution.py:37
  124.8 2.0 collective-permute-done.8.refs_7_
  126.8 13.8 %shard_map.103 = (bf16[512,512]{1,0:T(8,128)(2,1)}, bf16[32,2560]{1,0:T(8,128)(2,1)S(1)}) custom-call(s32[5]{0:T(128)S(1)} %pad_add_fusion.where_ref, bf16[4,8,128,1024]{3,2,1,0:T(8,128)(2,1)} %bitcast.38, bf16[1024,1024]{1,0:T(8,128)(2,1)} %bitcast.23.refs_0_, bf16[1024,1024]{1,0:T(8,128)(2,1)} %collective-permute-done.3.refs_1_, ...), custom_call_target="tpu_custom_call" | custom-call | flops 8589934592 | bytes 25165824 | tf_op jit(solution)/shard_map/pallas_call | solution.py:104
  141.9 19.9 %all_to_all.49 = bf16[32,2,1280]{2,1,0:T(2,128)(2,1)S(1)} all-to-all(bf16[32,2,1280]{2,1,0:T(2,128)(2,1)S(1)} %reshape.88), channel_id=1, replica_groups=mesh['z'=8,'y'=4,'x'=4,'c'=2] {'z','y'}, dimensions={0} | all-to-all | bytes 327680 | tf_op jit(solution)/shard_map/all_to_all | solution.py:29
  163.6 5.6 %all-to-all-start.3 = ((bf16[8,4,2560]{2,1,0:T(4,128)(2,1)}), bf16[8,4,2560]{2,1,0:T(4,128)(2,1)S(1)}, u32[]{:S(2)}, u32[]{:S(2)}) async-start(bf16[8,4,2560]{2,1,0:T(4,128)(2,1)} %all_to_all.34), calls=%async_computation.3 | async-start | bytes 327680 | tf_op jit(solution)/shard_map/all_to_all | solution.py:29
  171.5 3.3 %all-to-all-done.3 = bf16[8,4,2560]{2,1,0:T(4,128)(2,1)S(1)} async-done(((bf16[8,4,2560]{2,1,0:T(4,128)(2,1)}), bf16[8,4,2560]{2,1,0:T(4,128)(2,1)S(1)}, u32[]{:S(2)}, u32[]{:S(2)}) %all-to-all-start.3) | async-done | bytes 163872 | tf_op jit(solution)/shard_map/all_to_all | solution.py:29
  175.5 2.1 shard_map.104
  180.1 3.9 %all-to-all-start.4 = ((bf16[32,2,2304]{2,1,0:T(2,128)(2,1)}), bf16[32,2,2304]{2,1,0:T(2,128)(2,1)S(1)}, u32[]{:S(2)}, u32[]{:S(2)}) async-start(bf16[32,2,2304]{2,1,0:T(2,128)(2,1)} %reshape.90), calls=%async_computation.4 | async-start | bytes 589824 | tf_op jit(solution)/shard_map/all_to_all | solution.py:29
  184.3 11.6 %all-to-all-done.4 = bf16[32,2,2304]{2,1,0:T(2,128)(2,1)S(1)} async-done(((bf16[32,2,2304]{2,1,0:T(2,128)(2,1)}), bf16[32,2,2304]{2,1,0:T(2,128)(2,1)S(1)}, u32[]{:S(2)}, u32[]{:S(2)}) %all-to-all-start.4) | async-done | bytes 294944 | tf_op jit(solution)/shard_map/all_to_all | solution.py:29
  196.2 1.9 shard_map.105
  198.2 6.3 %all-to-all-start.5 = ((bf16[8,64,1024]{2,1,0:T(8,128)(2,1)}), bf16[8,64,1024]{2,1,0:T(8,128)(2,1)S(1)}, u32[]{:S(2)}, u32[]{:S(2)}) async-start(bf16[8,64,1024]{2,1,0:T(8,128)(2,1)} %shard_map.105), calls=%async_computation.5 | async-start | bytes 2097152 | tf_op jit(solution)/shard_map/all_to_all | solution.py:29
  206.2 13.3 %all-to-all-done.5 = bf16[8,64,1024]{2,1,0:T(8,128)(2,1)S(1)} async-done(((bf16[8,64,1024]{2,1,0:T(8,128)(2,1)}), bf16[8,64,1024]{2,1,0:T(8,128)(2,1)S(1)}, u32[]{:S(2)}, u32[]{:S(2)}) %all-to-all-start.5) | async-done | bytes 1048608 | tf_op jit(solution)/shard_map/all_to_all | solution.py:29
  (67 shorter events, 21.7 us)
Async XLA Ops:
  7.2 16.6 %copy-start = (bf16[32,2,16,1024]{3,2,1,0:T(8,128)(2,1)S(1)}, bf16[32,2,16,1024]{3,2,1,0:T(8,128)(2,1)}, u32[]{:S(2)}) copy-start(bf16[32,2,16,1024]{3,2,1,0:T(8,128)(2,1)} %param.10) | copy-start | bytes 6291460
  7.2 119.6 %all-gather.3.cloned.1.call-start = ((), (), s32[]{:S(2)}) async-start(), calls=%async_computation.6 | async-start | bytes 8650752 | tf_op jit(solution)/shard_map/all_gather | solution.py:217
  7.2 12.6 %collective-permute-start = (bf16[128,1024]{1,0:T(8,128)(2,1)}, bf16[128,1024]{1,0:T(8,128)(2,1)S(1)}, u32[]{:S(2)}, u32[]{:S(2)}) collective-permute-start(bf16[128,1024]{1,0:T(8,128)(2,1)} %param.8), channel_id=1, source_target_pairs={{0,32},{1,224},{2,64},{3,192},{4,96},{5,160},{6,0},{7,128},{8,40},... | collective-permute-start | bytes 786440 | tf_op jit(solution)/shard_map/ppermute | solution.py:213
  19.9 0.7 copy-start.4
  43.8 48.0 %collective-permute-start.1 = (bf16[1024,1024]{1,0:T(8,128)(2,1)}, bf16[1024,1024]{1,0:T(8,128)(2,1)}, u32[]{:S(2)}, u32[]{:S(2)}) collective-permute-start(bf16[1024,1024]{1,0:T(8,128)(2,1)} %bitcast.23.refs_0_), channel_id=1, source_target_pairs={{0,2},{2,4},{4,6},{6,0},{1,3},{3,5},{5,7},{7,1},{8,10},{10,12},{12... | collective-permute-start | bytes 6291464 | tf_op jit(solution)/shard_map/ppermute | solution.py:37
  44.1 47.7 %collective-permute-start.2 = (bf16[1024,1024]{1,0:T(8,128)(2,1)}, bf16[1024,1024]{1,0:T(8,128)(2,1)}, u32[]{:S(2)}, u32[]{:S(2)}) collective-permute-start(bf16[1024,1024]{1,0:T(8,128)(2,1)} %bitcast.23.refs_0_), channel_id=1, source_target_pairs={{0,6},{2,0},{4,2},{6,4},{1,7},{3,1},{5,3},{7,5},{8,14},{10,8},{12,... | collective-permute-start | bytes 6291464 | tf_op jit(solution)/shard_map/ppermute | solution.py:37
  46.5 45.3 %collective-permute-start.3 = (bf16[1024,1024]{1,0:T(8,128)(2,1)}, bf16[1024,1024]{1,0:T(8,128)(2,1)}, u32[]{:S(2)}, u32[]{:S(2)}) collective-permute-start(bf16[1024,1024]{1,0:T(8,128)(2,1)} %bitcast.23.refs_0_), channel_id=1, source_target_pairs={{0,1},{1,0},{2,3},{3,2},{4,5},{5,4},{6,7},{7,6},{8,9},{9,8},{10,11... | collective-permute-start | bytes 6291464 | tf_op jit(solution)/shard_map/ppermute | solution.py:37
  47.8 5.3 %collective-permute-start.4 = (bf16[4,128]{1,0:T(4,128)(2,1)S(1)}, bf16[4,128]{1,0:T(4,128)(2,1)S(1)}, u32[]{:S(2)}, u32[]{:S(2)}) collective-permute-start(bf16[4,128]{1,0:T(4,128)(2,1)S(1)} %reduce_sum.18), channel_id=1, source_target_pairs={{0,0},{1,32},{2,64},{3,96},{4,128},{5,160},{6,192},{7,224},{8,8},{... | collective-permute-start | bytes 3080 | tf_op jit(solution)/shard_map/ppermute | solution.py:223
  53.7 24.4 %all-to-all-start.1 = ((bf16[32,4,128]{2,1,0:T(4,128)(2,1)}), bf16[32,4,128]{2,1,0:T(4,128)(2,1)S(1)}, u32[]{:S(2)}, u32[]{:S(2)}) async-start(bf16[32,4,128]{2,1,0:T(4,128)(2,1)} %broadcast_in_dim.21), calls=%async_computation.1 | async-start | bytes 65536 | tf_op jit(solution)/shard_map/all_to_all | solution.py:29
  69.4 53.3 %copy-start.5 = (s32[32]{0:T(128)S(1)}, s32[32]{0:T(128)}, u32[]{:S(2)}) copy-start(s32[32]{0:T(128)} %param.14) | copy-start | bytes 388
  69.4 53.3 %copy-start.6 = (s32[32]{0:T(128)S(1)}, s32[32]{0:T(128)}, u32[]{:S(2)}) copy-start(s32[32]{0:T(128)} %param.13) | copy-start | bytes 388
  69.4 57.4 %copy-start.2 = (bf16[512,512]{1,0:T(8,128)(2,1)S(1)}, bf16[512,512]{1,0:T(8,128)(2,1)}, u32[]{:S(2)}) copy-start(bf16[512,512]{1,0:T(8,128)(2,1)} %refs_10_.1) | copy-start | bytes 1572868
  93.6 25.4 %collective-permute-start.7 = (bf16[1024,1024]{1,0:T(8,128)(2,1)S(1)}, bf16[1024,1024]{1,0:T(8,128)(2,1)}, u32[]{:S(2)}, u32[]{:S(2)}) collective-permute-start(bf16[1024,1024]{1,0:T(8,128)(2,1)S(1)} %broadcast_select_fusion), channel_id=1, source_target_pairs={{0,2},{1,7},{2,4},{3,1},{4,6},{5,3},{6,0},{7,5},{8,10},{9,15},{10,... | collective-permute-start | bytes 6291464 | tf_op jit(solution)/shard_map/ppermute | solution.py:45
  96.1 28.7 %collective-permute-start.5 = (bf16[1024,1024]{1,0:T(8,128)(2,1)}, bf16[1024,1024]{1,0:T(8,128)(2,1)}, u32[]{:S(2)}, u32[]{:S(2)}) collective-permute-start(bf16[1024,1024]{1,0:T(8,128)(2,1)} %collective-permute-done.1.refs_2_), channel_id=1, source_target_pairs={{0,1},{1,0},{2,3},{3,2},{4,5},{5,4},{6,7},{7,6},{8,9},{9,8},{10,11... | collective-permute-start | bytes 6291464 | tf_op jit(solution)/shard_map/ppermute | solution.py:37
  96.1 28.7 %collective-permute-start.6 = (bf16[1024,1024]{1,0:T(8,128)(2,1)}, bf16[1024,1024]{1,0:T(8,128)(2,1)}, u32[]{:S(2)}, u32[]{:S(2)}) collective-permute-start(bf16[1024,1024]{1,0:T(8,128)(2,1)} %collective-permute-done.2.refs_4_), channel_id=1, source_target_pairs={{0,1},{1,0},{2,3},{3,2},{4,5},{5,4},{6,7},{7,6},{8,9},{9,8},{10,11... | collective-permute-start | bytes 6291464 | tf_op jit(solution)/shard_map/ppermute | solution.py:37
  119.1 7.7 %collective-permute-start.8 = (bf16[1024,1024]{1,0:T(8,128)(2,1)}, bf16[1024,1024]{1,0:T(8,128)(2,1)}, u32[]{:S(2)}, u32[]{:S(2)}) collective-permute-start(bf16[1024,1024]{1,0:T(8,128)(2,1)} %collective-permute-done.7.refs_6_), channel_id=1, source_target_pairs={{0,1},{1,0},{2,3},{3,2},{4,5},{5,4},{6,7},{7,6},{8,9},{9,8},{10,11... | collective-permute-start | bytes 6291464 | tf_op jit(solution)/shard_map/ppermute | solution.py:37
  140.6 28.6 %copy-start.3 = (s32[32]{0:T(128)S(1)}, s32[32]{0:T(128)}, u32[]{:S(2)}) copy-start(s32[32]{0:T(128)} %param.15) | copy-start | bytes 388
  163.6 11.2 %all-to-all-start.3 = ((bf16[8,4,2560]{2,1,0:T(4,128)(2,1)}), bf16[8,4,2560]{2,1,0:T(4,128)(2,1)S(1)}, u32[]{:S(2)}, u32[]{:S(2)}) async-start(bf16[8,4,2560]{2,1,0:T(4,128)(2,1)} %all_to_all.34), calls=%async_computation.3 | async-start | bytes 327680 | tf_op jit(solution)/shard_map/all_to_all | solution.py:29
  180.1 15.8 %all-to-all-start.4 = ((bf16[32,2,2304]{2,1,0:T(2,128)(2,1)}), bf16[32,2,2304]{2,1,0:T(2,128)(2,1)S(1)}, u32[]{:S(2)}, u32[]{:S(2)}) async-start(bf16[32,2,2304]{2,1,0:T(2,128)(2,1)} %reshape.90), calls=%async_computation.4 | async-start | bytes 589824 | tf_op jit(solution)/shard_map/all_to_all | solution.py:29
  196.2 1.9 copy-start.1
  198.2 21.4 %all-to-all-start.5 = ((bf16[8,64,1024]{2,1,0:T(8,128)(2,1)}), bf16[8,64,1024]{2,1,0:T(8,128)(2,1)S(1)}, u32[]{:S(2)}, u32[]{:S(2)}) async-start(bf16[8,64,1024]{2,1,0:T(8,128)(2,1)} %shard_map.105), calls=%async_computation.5 | async-start | bytes 2097152 | tf_op jit(solution)/shard_map/all_to_all | solution.py:29
Sparse Core Ops, SparseCore 0:
  20.7 105.1 all-gather.2

commit v6 on v5

--- a/solution.py
+++ b/solution.py
@@ -124,7 +124,7 @@
     )(where, rows, *weights, low, out_map, cotan)
 
 
-def slot_kernel(slot_ref, shared_ref, first_ref, out_ref):
+def slot_kernel(slot_ref, shared_ref, out_ref):
     blocks, _ = slot_ref.shape
     width = shared_ref.shape[1] // blocks - BLOCK_ROWS
     n_out = OWN * Y * N_DP
@@ -139,13 +139,10 @@
         total = term if total is None else total + term
     for i in range(OWN * Y):
         out_ref[:, i * width:(i + 1) * width] = total[i * N_DP:(i + 1) * N_DP].astype(BF16)
-    dlow = jnp.sum(first_ref[:, blocks * width:].astype(F32), axis=0, keepdims=True)
-    out_ref[:, OWN * Y * width:] = jnp.broadcast_to(dlow, (N_DP, dlow.shape[1])).astype(BF16)
-
-
-def in_grad_kernel(mine_ref, got_ref, rows_ref, out_ref, buf, acc_ref, sems):
+
+
+def in_grad_kernel(mine_ref, dlow_ref, rows_ref, acc_ref, buf, sems):
     blocks, parts, _, _ = rows_ref.shape
-    start = got_ref.shape[1] - blocks * BLOCK_ROWS
 
     def load(b):
         return pltpu.make_async_copy(rows_ref.at[b], buf.at[b], sems.at[b])
@@ -162,7 +159,7 @@
     for b in range(blocks):
         @pl.when(used(b))
         def _():
-            dlow = got_ref[:, start + b * BLOCK_ROWS:start + (b + 1) * BLOCK_ROWS].astype(F32)
+            dlow = dlow_ref[:, b * BLOCK_ROWS:(b + 1) * BLOCK_ROWS].astype(F32)
             left = jnp.concatenate(
                 [jnp.where(mine_ref[s * blocks + b] > 0, dlow, 0.0) for s in range(OWN)], 0).astype(BF16)
             load(b).wait()
@@ -171,10 +168,8 @@
                 place = lax.rem(mine_ref[OWN * blocks] + step + parts, parts)
                 acc_ref[feature] += jnp.dot(left, buf[b, place], preferred_element_type=F32)
 
-    out_ref[...] = acc_ref[...].astype(BF16)
-
-
-def in_grad(mine, got, rows):
+
+def in_grad(mine, dlow, rows):
     blocks, parts, _, depth = rows.shape
     n_out = OWN * RANKS
     vmem_spec = pl.BlockSpec(memory_space=pltpu.VMEM)
@@ -182,17 +177,16 @@
         in_grad_kernel,
         in_specs=[pl.BlockSpec(memory_space=pltpu.SMEM), vmem_spec, pl.BlockSpec(memory_space=pl.ANY)],
         out_specs=vmem_spec,
-        out_shape=jax.ShapeDtypeStruct((parts, n_out, depth), BF16),
+        out_shape=jax.ShapeDtypeStruct((parts, n_out, depth), F32),
         scratch_shapes=[
             pltpu.VMEM((blocks, parts, BLOCK_ROWS, depth), BF16),
-            pltpu.VMEM((parts, n_out, depth), F32),
             pltpu.SemaphoreType.DMA((blocks,)),
         ],
         compiler_params=pltpu.CompilerParams(vmem_limit_bytes=VMEM_LIMIT),
         cost_estimate=pl.CostEstimate(
             flops=2 * parts * n_out * blocks * BLOCK_ROWS * depth,
             bytes_accessed=2 * parts * depth * blocks * BLOCK_ROWS, transcendentals=0),
-    )(mine, got, rows)
+    )(mine, dlow, rows)
 
 
 def out_grad_kernel(got_ref, out_ref):
@@ -241,14 +235,16 @@
     hidden, sent = project(where, rows, weights, low, out_map, d_hidden)
 
     first = exchange(sent, DP)
+    dlow = spread(first[:, blocks * hidden_part:].astype(F32).sum(0).astype(BF16), DP, N_DP)
+    in_part = in_grad(jnp.append(mine.reshape(-1).astype(jnp.int32), tensor.astype(jnp.int32)), dlow, rows)
+    in_part, first = join((in_part, first))
+    grad_in = lax.psum_scatter(in_part, TENSOR, scatter_dimension=0, tiled=True).reshape(OWN, 2, R, d_part)
     shared = exchange(first, TENSOR)
     merged = pl.pallas_call(
         slot_kernel,
-        out_shape=jax.ShapeDtypeStruct((N_DP, OWN * Y * hidden_part + blocks * BLOCK_ROWS), BF16),
-    )(slot_lane, shared, first)
+        out_shape=jax.ShapeDtypeStruct((N_DP, OWN * Y * hidden_part), BF16),
+    )(slot_lane, shared)
     got = exchange(merged, DP)
-    in_part = in_grad(jnp.append(mine.reshape(-1).astype(jnp.int32), tensor.astype(jnp.int32)), got, rows)
-    grad_in = exchange(in_part, TENSOR).astype(F32).sum(0).reshape(OWN, 2, R, d_part)
     grad_out = pl.pallas_call(
         out_grad_kernel,
         out_shape=jax.ShapeDtypeStruct((OWN, RANKS, Y * hidden_part), F32),

time: 228 us -> 223 us (0.978)
  waiting for transfers between devices: 81 us -> 75.2 us
  starting transfers between devices: 53.9 us -> 59.1 us
  blocking collectives: 35.1 us -> 31 us
  local copies, waits for them, and re-layouts: 13.8 us -> 16.2 us
    all_to_all x4, starting transfers between devices: 31.4 us -> 36.6 us  [exchange(): return lax.all_to_all(x, axes, 0, 0, tiled=True)]
    all_to_all x4, waiting for transfers between devices: 36.8 us -> 31.8 us  [exchange(): return lax.all_to_all(x, axes, 0, 0, tiled=True)]
    all_to_all x2, blocking collectives: 35.1 us -> 31 us  [exchange(): return lax.all_to_all(x, axes, 0, 0, tiled=True)]
    unnamed x21 -> x24, local copies, waits for them, and re-layouts: 6.25 us -> 8.63 us
  transfers between devices with their start and end apart: 14 -> 15, of which waited for: 9 -> 9; matrix products, arithmetic and copies ran while one was open for 6% -> 7% of each run, Pallas kernels for 1% -> 2%
where the time goes in v6:
time: 223 us; the launch traced here: 222 us
  waiting for transfers between devices  75.2 us (34%)
  starting transfers between devices  59.1 us (27%)
  blocking collectives  31 us (14%)
  Pallas kernels  18.4 us (8%)
  between operations  16.3 us (7%)
  local copies, waits for them, and re-layouts  16.2 us (7%)
  other arithmetic  5.2 us (2%)
    all_to_all x4, starting transfers between devices, exchange(): return lax.all_to_all(x, axes, 0, 0, tiled=True)  36.6 us
    all_to_all x4, waiting for transfers between devices, exchange(): return lax.all_to_all(x, axes, 0, 0, tiled=True)  31.8 us
    all_to_all x2, blocking collectives, exchange(): return lax.all_to_all(x, axes, 0, 0, tiled=True)  31 us
    ppermute x1, waiting for transfers between devices, last_hop(): lax.ppermute(jnp.where(lax.axis_index('c') == 0, up, down), (axis, 'c'),...  22.5 us
    ppermute x6, waiting for transfers between devices, hop(): return lax.ppermute(x, axis, [(i, (i + step) % n) for i in range(n)])  14.9 us
    pallas_call x1, Pallas kernels, project(): pl.pallas_call(block_kernel, in_specs=[pl.BlockSpec(memory_space=pltpu.SM...  13.8 us
    ppermute x1, starting transfers between devices, body(): lax.ppermute(tokens, DP + TENSOR, swap(lambda z, t: (z + STEPS[t]) % Z))  9.01 us
    unnamed x24, local copies, waits for them, and re-layouts  8.63 us
  transfers between devices with their start and end apart: 15, of which 9 were waited for; matrix products, arithmetic and copies ran while one was open for 7% of the time, Pallas kernels for 2%

profile of v6, /device:TPU:1, one launch (start us, length us, event | category | flops | bytes accessed | tf_op | source)
XLA Modules:
  0.0 222.4 jit_solution(2490864764391488008)
XLA Ops:
  7.2 9.0 %collective-permute-start = (bf16[128,1024]{1,0:T(8,128)(2,1)}, bf16[128,1024]{1,0:T(8,128)(2,1)S(1)}, u32[]{:S(2)}, u32[]{:S(2)}) collective-permute-start(bf16[128,1024]{1,0:T(8,128)(2,1)} %param.8), channel_id=1, source_target_pairs={{0,32},{1,224},{2,64},{3,192},{4,96},{5,160},{6,0},{7,128},{8,40},... | collective-permute-start | bytes 786440 | tf_op jit(solution)/shard_map/ppermute | solution.py:207
  16.2 3.6 %collective-permute-done = bf16[128,1024]{1,0:T(8,128)(2,1)S(1)} collective-permute-done((bf16[128,1024]{1,0:T(8,128)(2,1)}, bf16[128,1024]{1,0:T(8,128)(2,1)S(1)}, u32[]{:S(2)}, u32[]{:S(2)}) %collective-permute-start) | collective-permute-done | bytes 262176 | tf_op jit(solution)/shard_map/ppermute | solution.py:207
  25.0 15.2 %all_to_all.52 = f32[8,4,128]{2,1,0:T(4,128)S(1)} all-to-all(f32[8,4,128]{2,1,0:T(4,128)S(1)} %fusion.3), channel_id=1, replica_groups=mesh['z'=8,'y'=4,'x'=4,'c'=2] {'x','c'}, dimensions={0} | all-to-all | bytes 32768 | tf_op jit(solution)/shard_map/all_to_all | solution.py:29
  40.2 3.6 %copy.36 = bf16[128,8,2,512]{3,1,2,0:T(8,128)(2,1)} copy(bf16[128,8,2,512]{3,2,1,0:T(2,128)(2,1)} %bitcast.42) | data formatting | bytes 4194304
  44.1 2.4 %collective-permute-start.2 = (bf16[1024,1024]{1,0:T(8,128)(2,1)}, bf16[1024,1024]{1,0:T(8,128)(2,1)}, u32[]{:S(2)}, u32[]{:S(2)}) collective-permute-start(bf16[1024,1024]{1,0:T(8,128)(2,1)} %bitcast.24.refs_0_), channel_id=1, source_target_pairs={{0,6},{2,0},{4,2},{6,4},{1,7},{3,1},{5,3},{7,5},{8,14},{10,8},{12,... | collective-permute-start | bytes 6291464 | tf_op jit(solution)/shard_map/ppermute | solution.py:37
  47.8 2.9 %collective-permute-start.4 = (bf16[4,128]{1,0:T(4,128)(2,1)S(1)}, bf16[4,128]{1,0:T(4,128)(2,1)S(1)}, u32[]{:S(2)}, u32[]{:S(2)}) collective-permute-start(bf16[4,128]{1,0:T(4,128)(2,1)S(1)} %reduce_sum.21), channel_id=1, source_target_pairs={{0,0},{1,32},{2,64},{3,96},{4,128},{5,160},{6,192},{7,224},{8,8},{... | collective-permute-start | bytes 3080 | tf_op jit(solution)/shard_map/ppermute | solution.py:217
  50.7 2.3 %collective-permute-done.4 = bf16[4,128]{1,0:T(4,128)(2,1)S(1)} collective-permute-done((bf16[4,128]{1,0:T(4,128)(2,1)S(1)}, bf16[4,128]{1,0:T(4,128)(2,1)S(1)}, u32[]{:S(2)}, u32[]{:S(2)}) %collective-permute-start.4) | collective-permute-done | bytes 1056 | tf_op jit(solution)/shard_map/ppermute | solution.py:217
  53.7 15.7 %all-to-all-start.1 = ((bf16[32,4,128]{2,1,0:T(4,128)(2,1)}), bf16[32,4,128]{2,1,0:T(4,128)(2,1)S(1)}, u32[]{:S(2)}, u32[]{:S(2)}) async-start(bf16[32,4,128]{2,1,0:T(4,128)(2,1)} %broadcast_in_dim.13), calls=%async_computation.1 | async-start | bytes 65536 | tf_op jit(solution)/shard_map/all_to_all | solution.py:29
  69.4 8.6 %all-to-all-done.1 = bf16[32,4,128]{2,1,0:T(4,128)(2,1)S(1)} async-done(((bf16[32,4,128]{2,1,0:T(4,128)(2,1)}), bf16[32,4,128]{2,1,0:T(4,128)(2,1)S(1)}, u32[]{:S(2)}, u32[]{:S(2)}) %all-to-all-start.1) | async-done | bytes 32800 | tf_op jit(solution)/shard_map/all_to_all | solution.py:29
  78.1 13.7 %collective-permute-done.1.refs_2_ = bf16[1024,1024]{1,0:T(8,128)(2,1)} collective-permute-done((bf16[1024,1024]{1,0:T(8,128)(2,1)}, bf16[1024,1024]{1,0:T(8,128)(2,1)}, u32[]{:S(2)}, u32[]{:S(2)}) %collective-permute-start.1) | collective-permute-done | bytes 2097184 | tf_op jit(solution)/shard_map/ppermute | solution.py:37
  91.8 1.8 broadcast_select_fusion
  93.6 2.5 %collective-permute-start.7 = (bf16[1024,1024]{1,0:T(8,128)(2,1)S(1)}, bf16[1024,1024]{1,0:T(8,128)(2,1)}, u32[]{:S(2)}, u32[]{:S(2)}) collective-permute-start(bf16[1024,1024]{1,0:T(8,128)(2,1)S(1)} %broadcast_select_fusion), channel_id=1, source_target_pairs={{0,2},{1,7},{2,4},{3,1},{4,6},{5,3},{6,0},{7,5},{8,10},{9,15},{10,... | collective-permute-start | bytes 6291464 | tf_op jit(solution)/shard_map/ppermute | solution.py:45
  96.6 22.5 %collective-permute-done.7.refs_6_ = bf16[1024,1024]{1,0:T(8,128)(2,1)} collective-permute-done((bf16[1024,1024]{1,0:T(8,128)(2,1)S(1)}, bf16[1024,1024]{1,0:T(8,128)(2,1)}, u32[]{:S(2)}, u32[]{:S(2)}) %collective-permute-start.7) | collective-permute-done | bytes 2097184 | tf_op jit(solution)/shard_map/ppermute | solution.py:45
  119.1 3.6 %collective-permute-start.8 = (bf16[1024,1024]{1,0:T(8,128)(2,1)}, bf16[1024,1024]{1,0:T(8,128)(2,1)}, u32[]{:S(2)}, u32[]{:S(2)}) collective-permute-start(bf16[1024,1024]{1,0:T(8,128)(2,1)} %collective-permute-done.7.refs_6_), channel_id=1, source_target_pairs={{0,1},{1,0},{2,3},{3,2},{4,5},{5,4},{6,7},{7,6},{8,9},{9,8},{10,11... | collective-permute-start | bytes 6291464 | tf_op jit(solution)/shard_map/ppermute | solution.py:37
  123.6 1.8 gather_fusion
  126.8 13.8 %shard_map.103 = (bf16[512,512]{1,0:T(8,128)(2,1)}, bf16[32,2560]{1,0:T(8,128)(2,1)S(1)}) custom-call(s32[5]{0:T(128)S(1)} %pad_add_fusion.where_ref, bf16[4,8,128,1024]{3,2,1,0:T(8,128)(2,1)} %bitcast.40, bf16[1024,1024]{1,0:T(8,128)(2,1)} %bitcast.24.refs_0_, bf16[1024,1024]{1,0:T(8,128)(2,1)} %collective-permute-done.3.refs_1_, ...), custom_call_target="tpu_custom_call" | custom-call | flops 8589934592 | bytes 25165824 | tf_op jit(solution)/shard_map/pallas_call | solution.py:104
  142.4 10.4 %all-to-all-start.2 = ((bf16[32,2,1280]{2,1,0:T(2,128)(2,1)}), bf16[32,2,1280]{2,1,0:T(2,128)(2,1)S(1)}, u32[]{:S(2)}, u32[]{:S(2)}) async-start(bf16[32,2,1280]{2,1,0:T(2,128)(2,1)} %reshape.92), calls=%async_computation.2 | async-start | bytes 327680 | tf_op jit(solution)/shard_map/all_to_all | solution.py:29
  153.0 9.5 %all-to-all-done.2 = bf16[32,2,1280]{2,1,0:T(2,128)(2,1)S(1)} async-done(((bf16[32,2,1280]{2,1,0:T(2,128)(2,1)}), bf16[32,2,1280]{2,1,0:T(2,128)(2,1)S(1)}, u32[]{:S(2)}, u32[]{:S(2)}) %all-to-all-start.2) | async-done | bytes 163872 | tf_op jit(solution)/shard_map/all_to_all | solution.py:29
  164.1 4.3 %all-to-all-start.3 = ((bf16[32,2,256]{2,1,0:T(2,128)(2,1)}), bf16[32,2,256]{2,1,0:T(2,128)(2,1)S(1)}, u32[]{:S(2)}, u32[]{:S(2)}) async-start(bf16[32,2,256]{2,1,0:T(2,128)(2,1)} %reshape.94), calls=%async_computation.3 | async-start | bytes 65536 | tf_op jit(solution)/shard_map/all_to_all | solution.py:29
  168.5 8.6 %all-to-all-done.3 = bf16[32,2,256]{2,1,0:T(2,128)(2,1)S(1)} async-done(((bf16[32,2,256]{2,1,0:T(2,128)(2,1)}), bf16[32,2,256]{2,1,0:T(2,128)(2,1)S(1)}, u32[]{:S(2)}, u32[]{:S(2)}) %all-to-all-start.3) | async-done | bytes 32800 | tf_op jit(solution)/shard_map/all_to_all | solution.py:29
  180.0 6.3 %all-to-all-start.4 = ((bf16[8,4,2560]{2,1,0:T(4,128)(2,1)}), bf16[8,4,2560]{2,1,0:T(4,128)(2,1)S(1)}, u32[]{:S(2)}, u32[]{:S(2)}) async-start(bf16[8,4,2560]{2,1,0:T(4,128)(2,1)} %all_to_all.40), calls=%async_computation.5 | async-start | bytes 327680 | tf_op jit(solution)/shard_map/all_to_all | solution.py:29
  187.1 5.0 %all-to-all-done.4 = bf16[8,4,2560]{2,1,0:T(4,128)(2,1)S(1)} async-done(((bf16[8,4,2560]{2,1,0:T(4,128)(2,1)}), bf16[8,4,2560]{2,1,0:T(4,128)(2,1)S(1)}, u32[]{:S(2)}, u32[]{:S(2)}) %all-to-all-start.4) | async-done | bytes 163872 | tf_op jit(solution)/shard_map/all_to_all | solution.py:29
  192.9 2.0 shard_map.105
  196.7 15.8 %all_to_all.53 = bf16[32,2,2048]{2,1,0:T(2,128)(2,1)S(1)} all-to-all(bf16[32,2,2048]{2,1,0:T(2,128)(2,1)S(1)} %reshape.96), channel_id=1, replica_groups=mesh['z'=8,'y'=4,'x'=4,'c'=2] {'z','y'}, dimensions={0} | all-to-all | bytes 524288 | tf_op jit(solution)/shard_map/all_to_all | solution.py:29
  (74 shorter events, 21.3 us)
Async XLA Ops:
  7.2 16.6 %copy-start = (bf16[32,2,16,1024]{3,2,1,0:T(8,128)(2,1)S(1)}, bf16[32,2,16,1024]{3,2,1,0:T(8,128)(2,1)}, u32[]{:S(2)}) copy-start(bf16[32,2,16,1024]{3,2,1,0:T(8,128)(2,1)} %param.10) | copy-start | bytes 6291460
  7.2 119.6 %all-gather.3.cloned.1.call-start = ((), (), s32[]{:S(2)}) async-start(), calls=%async_computation.8 | async-start | bytes 8650752 | tf_op jit(solution)/shard_map/all_gather | solution.py:211
  7.2 12.6 %collective-permute-start = (bf16[128,1024]{1,0:T(8,128)(2,1)}, bf16[128,1024]{1,0:T(8,128)(2,1)S(1)}, u32[]{:S(2)}, u32[]{:S(2)}) collective-permute-start(bf16[128,1024]{1,0:T(8,128)(2,1)} %param.8), channel_id=1, source_target_pairs={{0,32},{1,224},{2,64},{3,192},{4,96},{5,160},{6,0},{7,128},{8,40},... | collective-permute-start | bytes 786440 | tf_op jit(solution)/shard_map/ppermute | solution.py:207
  19.9 0.7 copy-start.4
  43.8 48.0 %collective-permute-start.1 = (bf16[1024,1024]{1,0:T(8,128)(2,1)}, bf16[1024,1024]{1,0:T(8,128)(2,1)}, u32[]{:S(2)}, u32[]{:S(2)}) collective-permute-start(bf16[1024,1024]{1,0:T(8,128)(2,1)} %bitcast.24.refs_0_), channel_id=1, source_target_pairs={{0,2},{2,4},{4,6},{6,0},{1,3},{3,5},{5,7},{7,1},{8,10},{10,12},{12... | collective-permute-start | bytes 6291464 | tf_op jit(solution)/shard_map/ppermute | solution.py:37
  44.1 47.7 %collective-permute-start.2 = (bf16[1024,1024]{1,0:T(8,128)(2,1)}, bf16[1024,1024]{1,0:T(8,128)(2,1)}, u32[]{:S(2)}, u32[]{:S(2)}) collective-permute-start(bf16[1024,1024]{1,0:T(8,128)(2,1)} %bitcast.24.refs_0_), channel_id=1, source_target_pairs={{0,6},{2,0},{4,2},{6,4},{1,7},{3,1},{5,3},{7,5},{8,14},{10,8},{12,... | collective-permute-start | bytes 6291464 | tf_op jit(solution)/shard_map/ppermute | solution.py:37
  46.5 45.3 %collective-permute-start.3 = (bf16[1024,1024]{1,0:T(8,128)(2,1)}, bf16[1024,1024]{1,0:T(8,128)(2,1)}, u32[]{:S(2)}, u32[]{:S(2)}) collective-permute-start(bf16[1024,1024]{1,0:T(8,128)(2,1)} %bitcast.24.refs_0_), channel_id=1, source_target_pairs={{0,1},{1,0},{2,3},{3,2},{4,5},{5,4},{6,7},{7,6},{8,9},{9,8},{10,11... | collective-permute-start | bytes 6291464 | tf_op jit(solution)/shard_map/ppermute | solution.py:37
  47.8 5.3 %collective-permute-start.4 = (bf16[4,128]{1,0:T(4,128)(2,1)S(1)}, bf16[4,128]{1,0:T(4,128)(2,1)S(1)}, u32[]{:S(2)}, u32[]{:S(2)}) collective-permute-start(bf16[4,128]{1,0:T(4,128)(2,1)S(1)} %reduce_sum.21), channel_id=1, source_target_pairs={{0,0},{1,32},{2,64},{3,96},{4,128},{5,160},{6,192},{7,224},{8,8},{... | collective-permute-start | bytes 3080 | tf_op jit(solution)/shard_map/ppermute | solution.py:217
  53.7 24.4 %all-to-all-start.1 = ((bf16[32,4,128]{2,1,0:T(4,128)(2,1)}), bf16[32,4,128]{2,1,0:T(4,128)(2,1)S(1)}, u32[]{:S(2)}, u32[]{:S(2)}) async-start(bf16[32,4,128]{2,1,0:T(4,128)(2,1)} %broadcast_in_dim.13), calls=%async_computation.1 | async-start | bytes 65536 | tf_op jit(solution)/shard_map/all_to_all | solution.py:29
  69.4 53.3 %copy-start.5 = (s32[32]{0:T(128)S(1)}, s32[32]{0:T(128)}, u32[]{:S(2)}) copy-start(s32[32]{0:T(128)} %param.14) | copy-start | bytes 388
  69.4 53.3 %copy-start.6 = (s32[32]{0:T(128)S(1)}, s32[32]{0:T(128)}, u32[]{:S(2)}) copy-start(s32[32]{0:T(128)} %param.13) | copy-start | bytes 388
  69.4 53.3 %copy-start.3 = (s32[32]{0:T(128)S(1)}, s32[32]{0:T(128)}, u32[]{:S(2)}) copy-start(s32[32]{0:T(128)} %param.15) | copy-start | bytes 388
  69.4 57.4 %copy-start.2 = (bf16[512,512]{1,0:T(8,128)(2,1)S(1)}, bf16[512,512]{1,0:T(8,128)(2,1)}, u32[]{:S(2)}) copy-start(bf16[512,512]{1,0:T(8,128)(2,1)} %refs_10_.1) | copy-start | bytes 1572868
  93.6 25.4 %collective-permute-start.7 = (bf16[1024,1024]{1,0:T(8,128)(2,1)S(1)}, bf16[1024,1024]{1,0:T(8,128)(2,1)}, u32[]{:S(2)}, u32[]{:S(2)}) collective-permute-start(bf16[1024,1024]{1,0:T(8,128)(2,1)S(1)} %broadcast_select_fusion), channel_id=1, source_target_pairs={{0,2},{1,7},{2,4},{3,1},{4,6},{5,3},{6,0},{7,5},{8,10},{9,15},{10,... | collective-permute-start | bytes 6291464 | tf_op jit(solution)/shard_map/ppermute | solution.py:45
  96.1 29.5 %collective-permute-start.5 = (bf16[1024,1024]{1,0:T(8,128)(2,1)}, bf16[1024,1024]{1,0:T(8,128)(2,1)}, u32[]{:S(2)}, u32[]{:S(2)}) collective-permute-start(bf16[1024,1024]{1,0:T(8,128)(2,1)} %collective-permute-done.1.refs_2_), channel_id=1, source_target_pairs={{0,1},{1,0},{2,3},{3,2},{4,5},{5,4},{6,7},{7,6},{8,9},{9,8},{10,11... | collective-permute-start | bytes 6291464 | tf_op jit(solution)/shard_map/ppermute | solution.py:37
  96.1 29.5 %collective-permute-start.6 = (bf16[1024,1024]{1,0:T(8,128)(2,1)}, bf16[1024,1024]{1,0:T(8,128)(2,1)}, u32[]{:S(2)}, u32[]{:S(2)}) collective-permute-start(bf16[1024,1024]{1,0:T(8,128)(2,1)} %collective-permute-done.2.refs_4_), channel_id=1, source_target_pairs={{0,1},{1,0},{2,3},{3,2},{4,5},{5,4},{6,7},{7,6},{8,9},{9,8},{10,11... | collective-permute-start | bytes 6291464 | tf_op jit(solution)/shard_map/ppermute | solution.py:37
  119.1 7.7 %collective-permute-start.8 = (bf16[1024,1024]{1,0:T(8,128)(2,1)}, bf16[1024,1024]{1,0:T(8,128)(2,1)}, u32[]{:S(2)}, u32[]{:S(2)}) collective-permute-start(bf16[1024,1024]{1,0:T(8,128)(2,1)} %collective-permute-done.7.refs_6_), channel_id=1, source_target_pairs={{0,1},{1,0},{2,3},{3,2},{4,5},{5,4},{6,7},{7,6},{8,9},{9,8},{10,11... | collective-permute-start | bytes 6291464 | tf_op jit(solution)/shard_map/ppermute | solution.py:37
  142.4 20.1 %all-to-all-start.2 = ((bf16[32,2,1280]{2,1,0:T(2,128)(2,1)}), bf16[32,2,1280]{2,1,0:T(2,128)(2,1)S(1)}, u32[]{:S(2)}, u32[]{:S(2)}) async-start(bf16[32,2,1280]{2,1,0:T(2,128)(2,1)} %reshape.92), calls=%async_computation.2 | async-start | bytes 327680 | tf_op jit(solution)/shard_map/all_to_all | solution.py:29
  164.1 13.0 %all-to-all-start.3 = ((bf16[32,2,256]{2,1,0:T(2,128)(2,1)}), bf16[32,2,256]{2,1,0:T(2,128)(2,1)S(1)}, u32[]{:S(2)}, u32[]{:S(2)}) async-start(bf16[32,2,256]{2,1,0:T(2,128)(2,1)} %reshape.94), calls=%async_computation.3 | async-start | bytes 65536 | tf_op jit(solution)/shard_map/all_to_all | solution.py:29
  168.4 47.2 %reduce-scatter.2.cloned.1.call-start = ((), (), s32[]{:S(2)}) async-start(), calls=%async_computation.7 | async-start | bytes 2359296 | tf_op jit(solution)/shard_map/reduce_scatter | solution.py:241
  177.9 1.3 copy-start.1
  180.0 12.2 %all-to-all-start.4 = ((bf16[8,4,2560]{2,1,0:T(4,128)(2,1)}), bf16[8,4,2560]{2,1,0:T(4,128)(2,1)S(1)}, u32[]{:S(2)}, u32[]{:S(2)}) async-start(bf16[8,4,2560]{2,1,0:T(4,128)(2,1)} %all_to_all.40), calls=%async_computation.5 | async-start | bytes 327680 | tf_op jit(solution)/shard_map/all_to_all | solution.py:29
Sparse Core Ops, SparseCore 0:
  20.7 105.1 all-gather.2
  179.4 31.7 reduce-scatter.1

commit v7 on v6

--- a/solution.py
+++ b/solution.py
@@ -127,17 +127,18 @@
 def slot_kernel(slot_ref, shared_ref, out_ref):
     blocks, _ = slot_ref.shape
     width = shared_ref.shape[1] // blocks - BLOCK_ROWS
-    n_out = OWN * Y * N_DP
+    per = RANKS // Z
+    n_out = OWN * per * N_DP
     row = lax.broadcasted_iota(jnp.int32, (n_out, N_DP), 0)
     lane = lax.broadcasted_iota(jnp.int32, (n_out, N_DP), 1)
     slot = (row & (N_DP - 1)) * OWN + lax.shift_right_logical(row, 7)
-    same = (lax.shift_right_logical(row, 5) & (Y - 1)) == (lane & (Y - 1))
+    same = (lax.shift_right_logical(row, 5) & (per - 1)) == (lane & (per - 1))
     total = None
     for b in range(blocks):
         pick = jnp.where(same & (slot == slot_ref[b:b + 1, :]), 1.0, 0.0).astype(BF16)
         term = jnp.dot(pick, shared_ref[:, b * width:(b + 1) * width], preferred_element_type=F32)
         total = term if total is None else total + term
-    for i in range(OWN * Y):
+    for i in range(OWN * per):
         out_ref[:, i * width:(i + 1) * width] = total[i * N_DP:(i + 1) * N_DP].astype(BF16)
 
 
@@ -189,10 +190,27 @@
     )(mine, dlow, rows)
 
 
+def by_rank(k, y):
+    per = RANKS // Z
+    rank = lax.broadcasted_iota(jnp.int32, (RANKS, N_DP), 0)
+    source = lax.broadcasted_iota(jnp.int32, (RANKS, N_DP), 1)
+    hit = (lax.shift_right_logical(rank, 2) == lax.shift_right_logical(source, 2)) & ((rank & (per - 1)) == k)
+    hit = hit & ((source & (Y - 1)) == y)
+    return jnp.where(hit, 1.0, 0.0).astype(BF16)
+
+
 def out_grad_kernel(got_ref, out_ref):
-    width = out_ref.shape[2]
-    for s in range(OWN):
-        out_ref[s] = got_ref[:, s * width:(s + 1) * width].astype(F32)
+    per = RANKS // Z
+    width = out_ref.shape[2] // Y
+    for y in range(Y):
+        picks = [by_rank(k, y) for k in range(per)]
+        for s in range(OWN):
+            total = None
+            for k in range(per):
+                at = (s * per + k) * width
+                term = jnp.dot(picks[k], got_ref[:, at:at + width], preferred_element_type=F32)
+                total = term if total is None else total + term
+            out_ref[s, :, y * width:(y + 1) * width] = total
 
 
 def body(tokens, gate_up, adapter_in, adapter_out, d_hidden, block_adapter, block_live, owner_slot):
@@ -230,19 +248,20 @@
     slot_of = owner_slot[block_adapter]
     local_slot = lax.dynamic_slice_in_dim(slot_of, tensor * blocks, blocks, 0)
     mine = jnp.arange(OWN, dtype=jnp.int32)[:, None] + OWN * dp == local_slot[None, :]
-    slot_lane = jnp.repeat(slot_of.reshape(N_TENSOR, blocks).T, Y, axis=1)
+    slot_lane = jnp.repeat(slot_of.reshape(N_TENSOR, blocks).T, RANKS // Z, axis=1)
 
     hidden, sent = project(where, rows, weights, low, out_map, d_hidden)
 
-    first = exchange(sent, DP)
-    dlow = spread(first[:, blocks * hidden_part:].astype(F32).sum(0).astype(BF16), DP, N_DP)
+    first = exchange(sent, "z")
+    dlow = first[:, blocks * hidden_part:].astype(F32).reshape(Z, RANKS // Z, -1).sum(0).astype(BF16)
+    dlow = spread(dlow, DP, N_DP).astype(F32).reshape(Z, Y, RANKS // Z, -1).sum(1).reshape(RANKS, -1)
     in_part = in_grad(jnp.append(mine.reshape(-1).astype(jnp.int32), tensor.astype(jnp.int32)), dlow, rows)
     in_part, first = join((in_part, first))
     grad_in = lax.psum_scatter(in_part, TENSOR, scatter_dimension=0, tiled=True).reshape(OWN, 2, R, d_part)
     shared = exchange(first, TENSOR)
     merged = pl.pallas_call(
         slot_kernel,
-        out_shape=jax.ShapeDtypeStruct((N_DP, OWN * Y * hidden_part), BF16),
+        out_shape=jax.ShapeDtypeStruct((N_DP, OWN * (RANKS // Z) * hidden_part), BF16),
     )(slot_lane, shared)
     got = exchange(merged, DP)
     grad_out = pl.pallas_call(

time: 223 us -> 220 us (0.987)
    unnamed x24 -> x18, local copies, waits for them, and re-layouts: 8.63 us -> 7.12 us
where the time goes in v7:
time: 220 us; the launch traced here: 219 us
  waiting for transfers between devices  74.4 us (34%)
  starting transfers between devices  57 us (26%)
  blocking collectives  31.3 us (14%)
  Pallas kernels  18.8 us (9%)
  local copies, waits for them, and re-layouts  16.2 us (7%)
  between operations  16.2 us (7%)
  other arithmetic  4.05 us (2%)
    all_to_all x4, starting transfers between devices, exchange(): return lax.all_to_all(x, axes, 0, 0, tiled=True)  34.5 us
    all_to_all x2, blocking collectives, exchange(): return lax.all_to_all(x, axes, 0, 0, tiled=True)  31.3 us
    all_to_all x4, waiting for transfers between devices, exchange(): return lax.all_to_all(x, axes, 0, 0, tiled=True)  30.2 us
    ppermute x1, waiting for transfers between devices, last_hop(): lax.ppermute(jnp.where(lax.axis_index('c') == 0, up, down), (axis, 'c'),...  22.5 us
    ppermute x6, waiting for transfers between devices, hop(): return lax.ppermute(x, axis, [(i, (i + step) % n) for i in range(n)])  15.7 us
    pallas_call x1, Pallas kernels, project(): pl.pallas_call(block_kernel, in_specs=[pl.BlockSpec(memory_space=pltpu.SM...  13.8 us
    ppermute x1, starting transfers between devices, body(): lax.ppermute(tokens, DP + TENSOR, swap(lambda z, t: (z + STEPS[t]) % Z))  9.01 us
    ppermute x6, starting transfers between devices, hop(): return lax.ppermute(x, axis, [(i, (i + step) % n) for i in range(n)])  8.04 us
  transfers between devices with their start and end apart: 15, of which 9 were waited for; matrix products, arithmetic and copies ran while one was open for 7% of the time, Pallas kernels for 2%

profile of v7, /device:TPU:1, one launch (start us, length us, event | category | flops | bytes accessed | tf_op | source)
XLA Modules:
  0.0 219.1 jit_solution(8411656042464225028)
XLA Ops:
  7.2 9.0 %collective-permute-start = (bf16[128,1024]{1,0:T(8,128)(2,1)}, bf16[128,1024]{1,0:T(8,128)(2,1)S(1)}, u32[]{:S(2)}, u32[]{:S(2)}) collective-permute-start(bf16[128,1024]{1,0:T(8,128)(2,1)} %param.8), channel_id=1, source_target_pairs={{0,32},{1,224},{2,64},{3,192},{4,96},{5,160},{6,0},{7,128},{8,40},... | collective-permute-start | bytes 786440 | tf_op jit(solution)/shard_map/ppermute | solution.py:225
  16.2 3.6 %collective-permute-done = bf16[128,1024]{1,0:T(8,128)(2,1)S(1)} collective-permute-done((bf16[128,1024]{1,0:T(8,128)(2,1)}, bf16[128,1024]{1,0:T(8,128)(2,1)S(1)}, u32[]{:S(2)}, u32[]{:S(2)}) %collective-permute-start) | collective-permute-done | bytes 262176 | tf_op jit(solution)/shard_map/ppermute | solution.py:225
  25.0 15.2 %all_to_all.49 = f32[8,4,128]{2,1,0:T(4,128)S(1)} all-to-all(f32[8,4,128]{2,1,0:T(4,128)S(1)} %fusion.3), channel_id=1, replica_groups=mesh['z'=8,'y'=4,'x'=4,'c'=2] {'x','c'}, dimensions={0} | all-to-all | bytes 32768 | tf_op jit(solution)/shard_map/all_to_all | solution.py:29
  40.2 3.6 %copy.48 = bf16[128,8,2,512]{3,1,2,0:T(8,128)(2,1)} copy(bf16[128,8,2,512]{3,2,1,0:T(2,128)(2,1)} %bitcast.36) | data formatting | bytes 4194304
  44.1 2.4 %collective-permute-start.2 = (bf16[1024,1024]{1,0:T(8,128)(2,1)}, bf16[1024,1024]{1,0:T(8,128)(2,1)}, u32[]{:S(2)}, u32[]{:S(2)}) collective-permute-start(bf16[1024,1024]{1,0:T(8,128)(2,1)} %bitcast.23.refs_0_), channel_id=1, source_target_pairs={{0,6},{2,0},{4,2},{6,4},{1,7},{3,1},{5,3},{7,5},{8,14},{10,8},{12,... | collective-permute-start | bytes 6291464 | tf_op jit(solution)/shard_map/ppermute | solution.py:37
  47.8 2.9 %collective-permute-start.4 = (bf16[4,128]{1,0:T(4,128)(2,1)S(1)}, bf16[4,128]{1,0:T(4,128)(2,1)S(1)}, u32[]{:S(2)}, u32[]{:S(2)}) collective-permute-start(bf16[4,128]{1,0:T(4,128)(2,1)S(1)} %reduce_sum.27), channel_id=1, source_target_pairs={{0,0},{1,32},{2,64},{3,96},{4,128},{5,160},{6,192},{7,224},{8,8},{... | collective-permute-start | bytes 3080 | tf_op jit(solution)/shard_map/ppermute | solution.py:235
  50.7 2.3 %collective-permute-done.4 = bf16[4,128]{1,0:T(4,128)(2,1)S(1)} collective-permute-done((bf16[4,128]{1,0:T(4,128)(2,1)S(1)}, bf16[4,128]{1,0:T(4,128)(2,1)S(1)}, u32[]{:S(2)}, u32[]{:S(2)}) %collective-permute-start.4) | collective-permute-done | bytes 1056 | tf_op jit(solution)/shard_map/ppermute | solution.py:235
  53.7 15.7 %all-to-all-start.1 = ((bf16[32,4,128]{2,1,0:T(4,128)(2,1)}), bf16[32,4,128]{2,1,0:T(4,128)(2,1)S(1)}, u32[]{:S(2)}, u32[]{:S(2)}) async-start(bf16[32,4,128]{2,1,0:T(4,128)(2,1)} %broadcast_in_dim.13), calls=%async_computation.1 | async-start | bytes 65536 | tf_op jit(solution)/shard_map/all_to_all | solution.py:29
  69.4 8.7 %all-to-all-done.1 = bf16[32,4,128]{2,1,0:T(4,128)(2,1)S(1)} async-done(((bf16[32,4,128]{2,1,0:T(4,128)(2,1)}), bf16[32,4,128]{2,1,0:T(4,128)(2,1)S(1)}, u32[]{:S(2)}, u32[]{:S(2)}) %all-to-all-start.1) | async-done | bytes 32800 | tf_op jit(solution)/shard_map/all_to_all | solution.py:29
  78.1 13.7 %collective-permute-done.1.refs_2_ = bf16[1024,1024]{1,0:T(8,128)(2,1)} collective-permute-done((bf16[1024,1024]{1,0:T(8,128)(2,1)}, bf16[1024,1024]{1,0:T(8,128)(2,1)}, u32[]{:S(2)}, u32[]{:S(2)}) %collective-permute-start.1) | collective-permute-done | bytes 2097184 | tf_op jit(solution)/shard_map/ppermute | solution.py:37
  93.6 2.5 %collective-permute-start.7 = (bf16[1024,1024]{1,0:T(8,128)(2,1)S(1)}, bf16[1024,1024]{1,0:T(8,128)(2,1)}, u32[]{:S(2)}, u32[]{:S(2)}) collective-permute-start(bf16[1024,1024]{1,0:T(8,128)(2,1)S(1)} %broadcast_select_fusion), channel_id=1, source_target_pairs={{0,2},{1,7},{2,4},{3,1},{4,6},{5,3},{6,0},{7,5},{8,10},{9,15},{10,... | collective-permute-start | bytes 6291464 | tf_op jit(solution)/shard_map/ppermute | solution.py:45
  96.6 22.5 %collective-permute-done.7.refs_6_ = bf16[1024,1024]{1,0:T(8,128)(2,1)} collective-permute-done((bf16[1024,1024]{1,0:T(8,128)(2,1)S(1)}, bf16[1024,1024]{1,0:T(8,128)(2,1)}, u32[]{:S(2)}, u32[]{:S(2)}) %collective-permute-start.7) | collective-permute-done | bytes 2097184 | tf_op jit(solution)/shard_map/ppermute | solution.py:45
  119.1 3.6 %collective-permute-start.8 = (bf16[1024,1024]{1,0:T(8,128)(2,1)}, bf16[1024,1024]{1,0:T(8,128)(2,1)}, u32[]{:S(2)}, u32[]{:S(2)}) collective-permute-start(bf16[1024,1024]{1,0:T(8,128)(2,1)} %collective-permute-done.7.refs_6_), channel_id=1, source_target_pairs={{0,1},{1,0},{2,3},{3,2},{4,5},{5,4},{6,7},{7,6},{8,9},{9,8},{10,11... | collective-permute-start | bytes 6291464 | tf_op jit(solution)/shard_map/ppermute | solution.py:37
  124.8 2.0 collective-permute-done.8.refs_7_
  126.8 13.8 %shard_map.103 = (bf16[512,512]{1,0:T(8,128)(2,1)}, bf16[32,2560]{1,0:T(8,128)(2,1)S(1)}) custom-call(s32[5]{0:T(128)S(1)} %pad_add_fusion.where_ref, bf16[4,8,128,1024]{3,2,1,0:T(8,128)(2,1)} %bitcast.34, bf16[1024,1024]{1,0:T(8,128)(2,1)} %bitcast.23.refs_0_, bf16[1024,1024]{1,0:T(8,128)(2,1)} %collective-permute-done.3.refs_1_, ...), custom_call_target="tpu_custom_call" | custom-call | flops 8589934592 | bytes 25165824 | tf_op jit(solution)/shard_map/pallas_call | solution.py:104
  141.3 7.5 %all-to-all-start.2 = ((bf16[8,4,2560]{2,1,0:T(4,128)(2,1)}), bf16[8,4,2560]{2,1,0:T(4,128)(2,1)S(1)}, u32[]{:S(2)}, u32[]{:S(2)}) async-start(bf16[8,4,2560]{2,1,0:T(4,128)(2,1)} %all_to_all.33), calls=%async_computation.2 | async-start | bytes 327680 | tf_op jit(solution)/shard_map/all_to_all | solution.py:29
  149.6 7.8 %all-to-all-done.2 = bf16[8,4,2560]{2,1,0:T(4,128)(2,1)S(1)} async-done(((bf16[8,4,2560]{2,1,0:T(4,128)(2,1)}), bf16[8,4,2560]{2,1,0:T(4,128)(2,1)S(1)}, u32[]{:S(2)}, u32[]{:S(2)}) %all-to-all-start.2) | async-done | bytes 163872 | tf_op jit(solution)/shard_map/all_to_all | solution.py:29
  158.2 5.5 %all-to-all-start.3 = ((bf16[32,4,512]{2,1,0:T(4,128)(2,1)}), bf16[32,4,512]{2,1,0:T(4,128)(2,1)S(1)}, u32[]{:S(2)}, u32[]{:S(2)}) async-start(bf16[32,4,512]{2,1,0:T(4,128)(2,1)} %broadcast_in_dim.30), calls=%async_computation.3 | async-start | bytes 262144 | tf_op jit(solution)/shard_map/all_to_all | solution.py:29
  164.0 9.1 %all-to-all-done.3 = bf16[32,4,512]{2,1,0:T(4,128)(2,1)S(1)} async-done(((bf16[32,4,512]{2,1,0:T(4,128)(2,1)}), bf16[32,4,512]{2,1,0:T(4,128)(2,1)S(1)}, u32[]{:S(2)}, u32[]{:S(2)}) %all-to-all-start.3) | async-done | bytes 131104 | tf_op jit(solution)/shard_map/all_to_all | solution.py:29
  176.0 5.8 %all-to-all-start.4 = ((bf16[8,4,2560]{2,1,0:T(4,128)(2,1)}), bf16[8,4,2560]{2,1,0:T(4,128)(2,1)S(1)}, u32[]{:S(2)}, u32[]{:S(2)}) async-start(bf16[8,4,2560]{2,1,0:T(4,128)(2,1)} %all_to_all.37), calls=%async_computation.5 | async-start | bytes 327680 | tf_op jit(solution)/shard_map/all_to_all | solution.py:29
  182.7 4.7 %all-to-all-done.4 = bf16[8,4,2560]{2,1,0:T(4,128)(2,1)S(1)} async-done(((bf16[8,4,2560]{2,1,0:T(4,128)(2,1)}), bf16[8,4,2560]{2,1,0:T(4,128)(2,1)S(1)}, u32[]{:S(2)}, u32[]{:S(2)}) %all-to-all-start.4) | async-done | bytes 163872 | tf_op jit(solution)/shard_map/all_to_all | solution.py:29
  188.1 2.0 shard_map.105
  192.7 16.1 %all_to_all.50 = bf16[32,2,2048]{2,1,0:T(2,128)(2,1)S(1)} all-to-all(bf16[32,2,2048]{2,1,0:T(2,128)(2,1)S(1)} %reshape.111), channel_id=1, replica_groups=mesh['z'=8,'y'=4,'x'=4,'c'=2] {'z','y'}, dimensions={0} | all-to-all | bytes 524288 | tf_op jit(solution)/shard_map/all_to_all | solution.py:29
  210.1 2.2 shard_map.106
  (72 shorter events, 20.7 us)
Async XLA Ops:
  7.2 16.6 %copy-start = (bf16[32,2,16,1024]{3,2,1,0:T(8,128)(2,1)S(1)}, bf16[32,2,16,1024]{3,2,1,0:T(8,128)(2,1)}, u32[]{:S(2)}) copy-start(bf16[32,2,16,1024]{3,2,1,0:T(8,128)(2,1)} %param.10) | copy-start | bytes 6291460
  7.2 119.6 %all-gather.3.cloned.1.call-start = ((), (), s32[]{:S(2)}) async-start(), calls=%async_computation.8 | async-start | bytes 8650752 | tf_op jit(solution)/shard_map/all_gather | solution.py:229
  7.2 12.6 %collective-permute-start = (bf16[128,1024]{1,0:T(8,128)(2,1)}, bf16[128,1024]{1,0:T(8,128)(2,1)S(1)}, u32[]{:S(2)}, u32[]{:S(2)}) collective-permute-start(bf16[128,1024]{1,0:T(8,128)(2,1)} %param.8), channel_id=1, source_target_pairs={{0,32},{1,224},{2,64},{3,192},{4,96},{5,160},{6,0},{7,128},{8,40},... | collective-permute-start | bytes 786440 | tf_op jit(solution)/shard_map/ppermute | solution.py:225
  19.9 0.7 copy-start.4
  43.8 48.0 %collective-permute-start.1 = (bf16[1024,1024]{1,0:T(8,128)(2,1)}, bf16[1024,1024]{1,0:T(8,128)(2,1)}, u32[]{:S(2)}, u32[]{:S(2)}) collective-permute-start(bf16[1024,1024]{1,0:T(8,128)(2,1)} %bitcast.23.refs_0_), channel_id=1, source_target_pairs={{0,2},{2,4},{4,6},{6,0},{1,3},{3,5},{5,7},{7,1},{8,10},{10,12},{12... | collective-permute-start | bytes 6291464 | tf_op jit(solution)/shard_map/ppermute | solution.py:37
  44.1 47.7 %collective-permute-start.2 = (bf16[1024,1024]{1,0:T(8,128)(2,1)}, bf16[1024,1024]{1,0:T(8,128)(2,1)}, u32[]{:S(2)}, u32[]{:S(2)}) collective-permute-start(bf16[1024,1024]{1,0:T(8,128)(2,1)} %bitcast.23.refs_0_), channel_id=1, source_target_pairs={{0,6},{2,0},{4,2},{6,4},{1,7},{3,1},{5,3},{7,5},{8,14},{10,8},{12,... | collective-permute-start | bytes 6291464 | tf_op jit(solution)/shard_map/ppermute | solution.py:37
  46.5 45.3 %collective-permute-start.3 = (bf16[1024,1024]{1,0:T(8,128)(2,1)}, bf16[1024,1024]{1,0:T(8,128)(2,1)}, u32[]{:S(2)}, u32[]{:S(2)}) collective-permute-start(bf16[1024,1024]{1,0:T(8,128)(2,1)} %bitcast.23.refs_0_), channel_id=1, source_target_pairs={{0,1},{1,0},{2,3},{3,2},{4,5},{5,4},{6,7},{7,6},{8,9},{9,8},{10,11... | collective-permute-start | bytes 6291464 | tf_op jit(solution)/shard_map/ppermute | solution.py:37
  47.8 5.3 %collective-permute-start.4 = (bf16[4,128]{1,0:T(4,128)(2,1)S(1)}, bf16[4,128]{1,0:T(4,128)(2,1)S(1)}, u32[]{:S(2)}, u32[]{:S(2)}) collective-permute-start(bf16[4,128]{1,0:T(4,128)(2,1)S(1)} %reduce_sum.27), channel_id=1, source_target_pairs={{0,0},{1,32},{2,64},{3,96},{4,128},{5,160},{6,192},{7,224},{8,8},{... | collective-permute-start | bytes 3080 | tf_op jit(solution)/shard_map/ppermute | solution.py:235
  53.7 24.4 %all-to-all-start.1 = ((bf16[32,4,128]{2,1,0:T(4,128)(2,1)}), bf16[32,4,128]{2,1,0:T(4,128)(2,1)S(1)}, u32[]{:S(2)}, u32[]{:S(2)}) async-start(bf16[32,4,128]{2,1,0:T(4,128)(2,1)} %broadcast_in_dim.13), calls=%async_computation.1 | async-start | bytes 65536 | tf_op jit(solution)/shard_map/all_to_all | solution.py:29
  69.4 53.3 %copy-start.5 = (s32[32]{0:T(128)S(1)}, s32[32]{0:T(128)}, u32[]{:S(2)}) copy-start(s32[32]{0:T(128)} %param.14) | copy-start | bytes 388
  69.4 53.3 %copy-start.6 = (s32[32]{0:T(128)S(1)}, s32[32]{0:T(128)}, u32[]{:S(2)}) copy-start(s32[32]{0:T(128)} %param.13) | copy-start | bytes 388
  69.4 57.4 %copy-start.2 = (bf16[512,512]{1,0:T(8,128)(2,1)S(1)}, bf16[512,512]{1,0:T(8,128)(2,1)}, u32[]{:S(2)}) copy-start(bf16[512,512]{1,0:T(8,128)(2,1)} %refs_10_.1) | copy-start | bytes 1572868
  93.6 25.4 %collective-permute-start.7 = (bf16[1024,1024]{1,0:T(8,128)(2,1)S(1)}, bf16[1024,1024]{1,0:T(8,128)(2,1)}, u32[]{:S(2)}, u32[]{:S(2)}) collective-permute-start(bf16[1024,1024]{1,0:T(8,128)(2,1)S(1)} %broadcast_select_fusion), channel_id=1, source_target_pairs={{0,2},{1,7},{2,4},{3,1},{4,6},{5,3},{6,0},{7,5},{8,10},{9,15},{10,... | collective-permute-start | bytes 6291464 | tf_op jit(solution)/shard_map/ppermute | solution.py:45
  96.1 28.7 %collective-permute-start.5 = (bf16[1024,1024]{1,0:T(8,128)(2,1)}, bf16[1024,1024]{1,0:T(8,128)(2,1)}, u32[]{:S(2)}, u32[]{:S(2)}) collective-permute-start(bf16[1024,1024]{1,0:T(8,128)(2,1)} %collective-permute-done.1.refs_2_), channel_id=1, source_target_pairs={{0,1},{1,0},{2,3},{3,2},{4,5},{5,4},{6,7},{7,6},{8,9},{9,8},{10,11... | collective-permute-start | bytes 6291464 | tf_op jit(solution)/shard_map/ppermute | solution.py:37
  96.1 28.7 %collective-permute-start.6 = (bf16[1024,1024]{1,0:T(8,128)(2,1)}, bf16[1024,1024]{1,0:T(8,128)(2,1)}, u32[]{:S(2)}, u32[]{:S(2)}) collective-permute-start(bf16[1024,1024]{1,0:T(8,128)(2,1)} %collective-permute-done.2.refs_4_), channel_id=1, source_target_pairs={{0,1},{1,0},{2,3},{3,2},{4,5},{5,4},{6,7},{7,6},{8,9},{9,8},{10,11... | collective-permute-start | bytes 6291464 | tf_op jit(solution)/shard_map/ppermute | solution.py:37
  119.1 7.7 %collective-permute-start.8 = (bf16[1024,1024]{1,0:T(8,128)(2,1)}, bf16[1024,1024]{1,0:T(8,128)(2,1)}, u32[]{:S(2)}, u32[]{:S(2)}) collective-permute-start(bf16[1024,1024]{1,0:T(8,128)(2,1)} %collective-permute-done.7.refs_6_), channel_id=1, source_target_pairs={{0,1},{1,0},{2,3},{3,2},{4,5},{5,4},{6,7},{7,6},{8,9},{9,8},{10,11... | collective-permute-start | bytes 6291464 | tf_op jit(solution)/shard_map/ppermute | solution.py:37
  126.8 22.0 %copy-start.3 = (s32[32]{0:T(128)S(1)}, s32[32]{0:T(128)}, u32[]{:S(2)}) copy-start(s32[32]{0:T(128)} %param.15) | copy-start | bytes 388
  141.3 16.0 %all-to-all-start.2 = ((bf16[8,4,2560]{2,1,0:T(4,128)(2,1)}), bf16[8,4,2560]{2,1,0:T(4,128)(2,1)S(1)}, u32[]{:S(2)}, u32[]{:S(2)}) async-start(bf16[8,4,2560]{2,1,0:T(4,128)(2,1)} %all_to_all.33), calls=%async_computation.2 | async-start | bytes 327680 | tf_op jit(solution)/shard_map/all_to_all | solution.py:29
  158.2 14.9 %all-to-all-start.3 = ((bf16[32,4,512]{2,1,0:T(4,128)(2,1)}), bf16[32,4,512]{2,1,0:T(4,128)(2,1)S(1)}, u32[]{:S(2)}, u32[]{:S(2)}) async-start(bf16[32,4,512]{2,1,0:T(4,128)(2,1)} %broadcast_in_dim.30), calls=%async_computation.3 | async-start | bytes 262144 | tf_op jit(solution)/shard_map/all_to_all | solution.py:29
  163.7 48.5 %reduce-scatter.2.cloned.1.call-start = ((), (), s32[]{:S(2)}) async-start(), calls=%async_computation.7 | async-start | bytes 2359296 | tf_op jit(solution)/shard_map/reduce_scatter | solution.py:260
  173.9 1.3 copy-start.1
  176.0 11.4 %all-to-all-start.4 = ((bf16[8,4,2560]{2,1,0:T(4,128)(2,1)}), bf16[8,4,2560]{2,1,0:T(4,128)(2,1)S(1)}, u32[]{:S(2)}, u32[]{:S(2)}) async-start(bf16[8,4,2560]{2,1,0:T(4,128)(2,1)} %all_to_all.37), calls=%async_computation.5 | async-start | bytes 327680 | tf_op jit(solution)/shard_map/all_to_all | solution.py:29
Sparse Core Ops, SparseCore 0:
  20.7 105.1 all-gather.2
  175.4 31.5 reduce-scatter.1

commit v8 on v6

--- a/solution.py
+++ b/solution.py
@@ -126,19 +126,18 @@
 
 def slot_kernel(slot_ref, shared_ref, out_ref):
     blocks, _ = slot_ref.shape
-    width = shared_ref.shape[1] // blocks - BLOCK_ROWS
-    n_out = OWN * Y * N_DP
-    row = lax.broadcasted_iota(jnp.int32, (n_out, N_DP), 0)
-    lane = lax.broadcasted_iota(jnp.int32, (n_out, N_DP), 1)
-    slot = (row & (N_DP - 1)) * OWN + lax.shift_right_logical(row, 7)
-    same = (lax.shift_right_logical(row, 5) & (Y - 1)) == (lane & (Y - 1))
+    width = out_ref.shape[1]
+    per = RANKS // Z
+    row = lax.broadcasted_iota(jnp.int32, (SLOTS * per, N_DP), 0)
+    lane = lax.broadcasted_iota(jnp.int32, (SLOTS * per, N_DP), 1)
+    slot = lax.shift_right_logical(row, 2)
+    same = (row & (per - 1)) == (lane & (per - 1))
     total = None
     for b in range(blocks):
         pick = jnp.where(same & (slot == slot_ref[b:b + 1, :]), 1.0, 0.0).astype(BF16)
         term = jnp.dot(pick, shared_ref[:, b * width:(b + 1) * width], preferred_element_type=F32)
         total = term if total is None else total + term
-    for i in range(OWN * Y):
-        out_ref[:, i * width:(i + 1) * width] = total[i * N_DP:(i + 1) * N_DP].astype(BF16)
+    out_ref[...] = total.astype(BF16)
 
 
 def in_grad_kernel(mine_ref, dlow_ref, rows_ref, acc_ref, buf, sems):
@@ -190,9 +189,17 @@
 
 
 def out_grad_kernel(got_ref, out_ref):
-    width = out_ref.shape[2]
+    rows, width = got_ref.shape
+    to = lax.broadcasted_iota(jnp.int32, (rows, rows), 0)
+    source = lax.broadcasted_iota(jnp.int32, (rows, rows), 1)
+    shift = lax.shift_right_logical
+    hit = (shift(to & 31, 2) == shift(source, 5)) & ((shift(to, 5) & 3) == (shift(source, 3) & 3))
+    hit = hit & (shift(to, 7) == (shift(source, 2) & 1)) & ((to & 3) == (source & 3))
+    total = jnp.dot(jnp.where(hit, 1.0, 0.0).astype(BF16), got_ref[...], preferred_element_type=F32)
     for s in range(OWN):
-        out_ref[s] = got_ref[:, s * width:(s + 1) * width].astype(F32)
+        for y in range(Y):
+            at = (s * Y + y) * RANKS
+            out_ref[s, :, y * width:(y + 1) * width] = total[at:at + RANKS]
 
 
 def body(tokens, gate_up, adapter_in, adapter_out, d_hidden, block_adapter, block_live, owner_slot):
@@ -230,19 +237,20 @@
     slot_of = owner_slot[block_adapter]
     local_slot = lax.dynamic_slice_in_dim(slot_of, tensor * blocks, blocks, 0)
     mine = jnp.arange(OWN, dtype=jnp.int32)[:, None] + OWN * dp == local_slot[None, :]
-    slot_lane = jnp.repeat(slot_of.reshape(N_TENSOR, blocks).T, Y, axis=1)
+    slot_lane = jnp.repeat(slot_of.reshape(N_TENSOR, blocks).T, RANKS // Z, axis=1)
 
     hidden, sent = project(where, rows, weights, low, out_map, d_hidden)
 
-    first = exchange(sent, DP)
-    dlow = spread(first[:, blocks * hidden_part:].astype(F32).sum(0).astype(BF16), DP, N_DP)
+    first = exchange(sent, "z")
+    dlow = first[:, blocks * hidden_part:].astype(F32).reshape(Z, RANKS // Z, -1).sum(0).astype(BF16)
+    dlow = spread(dlow, DP, N_DP).astype(F32).reshape(Z, Y, RANKS // Z, -1).sum(1).reshape(RANKS, -1)
     in_part = in_grad(jnp.append(mine.reshape(-1).astype(jnp.int32), tensor.astype(jnp.int32)), dlow, rows)
     in_part, first = join((in_part, first))
     grad_in = lax.psum_scatter(in_part, TENSOR, scatter_dimension=0, tiled=True).reshape(OWN, 2, R, d_part)
     shared = exchange(first, TENSOR)
     merged = pl.pallas_call(
         slot_kernel,
-        out_shape=jax.ShapeDtypeStruct((N_DP, OWN * Y * hidden_part), BF16),
+        out_shape=jax.ShapeDtypeStruct((SLOTS * (RANKS // Z), hidden_part), BF16),
     )(slot_lane, shared)
     got = exchange(merged, DP)
     grad_out = pl.pallas_call(

time: 223 us -> 217 us (0.973)
  other arithmetic: 5.2 us -> 2.27 us
  starting transfers between devices: 59.1 us -> 56.8 us
    unnamed x24 -> x15, local copies, waits for them, and re-layouts: 8.63 us -> 5.67 us
    all_to_all x2 -> x0, other arithmetic: 2.25 us -> none  [exchange(): return lax.all_to_all(x, axes, 0, 0, tiled=True)]
  transfers between devices with their start and end apart: 15 -> 15, of which waited for: 9 -> 9; matrix products, arithmetic and copies ran while one was open for 7% -> 6% of each run, Pallas kernels for 2% -> 2%
where the time goes in v8:
time: 217 us
  waiting for transfers between devices  75 us (35%)
  starting transfers between devices  56.8 us (26%)
  blocking collectives  30.8 us (14%)
  Pallas kernels  20.5 us (9%)
  between operations  16.2 us (7%)
  local copies, waits for them, and re-layouts  14.1 us (6%)
  other arithmetic  2.27 us (1%)
    all_to_all x4, starting transfers between devices, exchange(): return lax.all_to_all(x, axes, 0, 0, tiled=True)  34.3 us
    all_to_all x4, waiting for transfers between devices, exchange(): return lax.all_to_all(x, axes, 0, 0, tiled=True)  30.8 us
    all_to_all x2, blocking collectives, exchange(): return lax.all_to_all(x, axes, 0, 0, tiled=True)  30.8 us
    ppermute x1, waiting for transfers between devices, last_hop(): lax.ppermute(jnp.where(lax.axis_index('c') == 0, up, down), (axis, 'c'),...  22.5 us
    ppermute x6, waiting for transfers between devices, hop(): return lax.ppermute(x, axis, [(i, (i + step) % n) for i in range(n)])  15.7 us
    pallas_call x1, Pallas kernels, project(): pl.pallas_call(block_kernel, in_specs=[pl.BlockSpec(memory_space=pltpu.SM...  13.8 us
    ppermute x1, starting transfers between devices, body(): lax.ppermute(tokens, DP + TENSOR, swap(lambda z, t: (z + STEPS[t]) % Z))  9.01 us
    ppermute x6, starting transfers between devices, hop(): return lax.ppermute(x, axis, [(i, (i + step) % n) for i in range(n)])  8.04 us
  transfers between devices with their start and end apart: 15, of which 9 were waited for; matrix products, arithmetic and copies ran while one was open for 6% of the time, Pallas kernels for 2%

profile of v8, /device:TPU:1, one launch (start us, length us, event | category | flops | bytes accessed | tf_op | source)
XLA Modules:
  0.0 216.9 jit_solution(2197267128838800814)
XLA Ops:
  7.2 9.0 %collective-permute-start = (bf16[128,1024]{1,0:T(8,128)(2,1)}, bf16[128,1024]{1,0:T(8,128)(2,1)S(1)}, u32[]{:S(2)}, u32[]{:S(2)}) collective-permute-start(bf16[128,1024]{1,0:T(8,128)(2,1)} %param.8), channel_id=1, source_target_pairs={{0,32},{1,224},{2,64},{3,192},{4,96},{5,160},{6,0},{7,128},{8,40},... | collective-permute-start | bytes 786440 | tf_op jit(solution)/shard_map/ppermute | solution.py:214
  16.2 3.6 %collective-permute-done = bf16[128,1024]{1,0:T(8,128)(2,1)S(1)} collective-permute-done((bf16[128,1024]{1,0:T(8,128)(2,1)}, bf16[128,1024]{1,0:T(8,128)(2,1)S(1)}, u32[]{:S(2)}, u32[]{:S(2)}) %collective-permute-start) | collective-permute-done | bytes 262176 | tf_op jit(solution)/shard_map/ppermute | solution.py:214
  25.0 15.2 %all_to_all.49 = f32[8,4,128]{2,1,0:T(4,128)S(1)} all-to-all(f32[8,4,128]{2,1,0:T(4,128)S(1)} %fusion.3), channel_id=1, replica_groups=mesh['z'=8,'y'=4,'x'=4,'c'=2] {'x','c'}, dimensions={0} | all-to-all | bytes 32768 | tf_op jit(solution)/shard_map/all_to_all | solution.py:29
  40.2 3.6 %copy.38 = bf16[128,8,2,512]{3,1,2,0:T(8,128)(2,1)} copy(bf16[128,8,2,512]{3,2,1,0:T(2,128)(2,1)} %bitcast.34) | data formatting | bytes 4194304
  44.1 2.4 %collective-permute-start.2 = (bf16[1024,1024]{1,0:T(8,128)(2,1)}, bf16[1024,1024]{1,0:T(8,128)(2,1)}, u32[]{:S(2)}, u32[]{:S(2)}) collective-permute-start(bf16[1024,1024]{1,0:T(8,128)(2,1)} %bitcast.23.refs_0_), channel_id=1, source_target_pairs={{0,6},{2,0},{4,2},{6,4},{1,7},{3,1},{5,3},{7,5},{8,14},{10,8},{12,... | collective-permute-start | bytes 6291464 | tf_op jit(solution)/shard_map/ppermute | solution.py:37
  47.8 2.9 %collective-permute-start.4 = (bf16[4,128]{1,0:T(4,128)(2,1)S(1)}, bf16[4,128]{1,0:T(4,128)(2,1)S(1)}, u32[]{:S(2)}, u32[]{:S(2)}) collective-permute-start(bf16[4,128]{1,0:T(4,128)(2,1)S(1)} %reduce_sum.27), channel_id=1, source_target_pairs={{0,0},{1,32},{2,64},{3,96},{4,128},{5,160},{6,192},{7,224},{8,8},{... | collective-permute-start | bytes 3080 | tf_op jit(solution)/shard_map/ppermute | solution.py:224
  50.7 2.3 %collective-permute-done.4 = bf16[4,128]{1,0:T(4,128)(2,1)S(1)} collective-permute-done((bf16[4,128]{1,0:T(4,128)(2,1)S(1)}, bf16[4,128]{1,0:T(4,128)(2,1)S(1)}, u32[]{:S(2)}, u32[]{:S(2)}) %collective-permute-start.4) | collective-permute-done | bytes 1056 | tf_op jit(solution)/shard_map/ppermute | solution.py:224
  53.7 15.7 %all-to-all-start.1 = ((bf16[32,4,128]{2,1,0:T(4,128)(2,1)}), bf16[32,4,128]{2,1,0:T(4,128)(2,1)S(1)}, u32[]{:S(2)}, u32[]{:S(2)}) async-start(bf16[32,4,128]{2,1,0:T(4,128)(2,1)} %broadcast_in_dim.13), calls=%async_computation.1 | async-start | bytes 65536 | tf_op jit(solution)/shard_map/all_to_all | solution.py:29
  69.4 8.7 %all-to-all-done.1 = bf16[32,4,128]{2,1,0:T(4,128)(2,1)S(1)} async-done(((bf16[32,4,128]{2,1,0:T(4,128)(2,1)}), bf16[32,4,128]{2,1,0:T(4,128)(2,1)S(1)}, u32[]{:S(2)}, u32[]{:S(2)}) %all-to-all-start.1) | async-done | bytes 32800 | tf_op jit(solution)/shard_map/all_to_all | solution.py:29
  78.1 13.7 %collective-permute-done.1.refs_2_ = bf16[1024,1024]{1,0:T(8,128)(2,1)} collective-permute-done((bf16[1024,1024]{1,0:T(8,128)(2,1)}, bf16[1024,1024]{1,0:T(8,128)(2,1)}, u32[]{:S(2)}, u32[]{:S(2)}) %collective-permute-start.1) | collective-permute-done | bytes 2097184 | tf_op jit(solution)/shard_map/ppermute | solution.py:37
  93.6 2.5 %collective-permute-start.7 = (bf16[1024,1024]{1,0:T(8,128)(2,1)S(1)}, bf16[1024,1024]{1,0:T(8,128)(2,1)}, u32[]{:S(2)}, u32[]{:S(2)}) collective-permute-start(bf16[1024,1024]{1,0:T(8,128)(2,1)S(1)} %broadcast_select_fusion), channel_id=1, source_target_pairs={{0,2},{1,7},{2,4},{3,1},{4,6},{5,3},{6,0},{7,5},{8,10},{9,15},{10,... | collective-permute-start | bytes 6291464 | tf_op jit(solution)/shard_map/ppermute | solution.py:45
  96.6 22.5 %collective-permute-done.7.refs_6_ = bf16[1024,1024]{1,0:T(8,128)(2,1)} collective-permute-done((bf16[1024,1024]{1,0:T(8,128)(2,1)S(1)}, bf16[1024,1024]{1,0:T(8,128)(2,1)}, u32[]{:S(2)}, u32[]{:S(2)}) %collective-permute-start.7) | collective-permute-done | bytes 2097184 | tf_op jit(solution)/shard_map/ppermute | solution.py:45
  119.1 3.6 %collective-permute-start.8 = (bf16[1024,1024]{1,0:T(8,128)(2,1)}, bf16[1024,1024]{1,0:T(8,128)(2,1)}, u32[]{:S(2)}, u32[]{:S(2)}) collective-permute-start(bf16[1024,1024]{1,0:T(8,128)(2,1)} %collective-permute-done.7.refs_6_), channel_id=1, source_target_pairs={{0,1},{1,0},{2,3},{3,2},{4,5},{5,4},{6,7},{7,6},{8,9},{9,8},{10,11... | collective-permute-start | bytes 6291464 | tf_op jit(solution)/shard_map/ppermute | solution.py:37
  124.8 2.0 collective-permute-done.8.refs_7_
  126.8 13.8 %shard_map.103 = (bf16[512,512]{1,0:T(8,128)(2,1)}, bf16[32,2560]{1,0:T(8,128)(2,1)S(1)}) custom-call(s32[5]{0:T(128)S(1)} %pad_add_fusion.where_ref, bf16[4,8,128,1024]{3,2,1,0:T(8,128)(2,1)} %bitcast.32, bf16[1024,1024]{1,0:T(8,128)(2,1)} %bitcast.23.refs_0_, bf16[1024,1024]{1,0:T(8,128)(2,1)} %collective-permute-done.3.refs_1_, ...), custom_call_target="tpu_custom_call" | custom-call | flops 8589934592 | bytes 25165824 | tf_op jit(solution)/shard_map/pallas_call | solution.py:104
  141.3 7.5 %all-to-all-start.2 = ((bf16[8,4,2560]{2,1,0:T(4,128)(2,1)}), bf16[8,4,2560]{2,1,0:T(4,128)(2,1)S(1)}, u32[]{:S(2)}, u32[]{:S(2)}) async-start(bf16[8,4,2560]{2,1,0:T(4,128)(2,1)} %all_to_all.33), calls=%async_computation.2 | async-start | bytes 327680 | tf_op jit(solution)/shard_map/all_to_all | solution.py:29
  149.6 7.8 %all-to-all-done.2 = bf16[8,4,2560]{2,1,0:T(4,128)(2,1)S(1)} async-done(((bf16[8,4,2560]{2,1,0:T(4,128)(2,1)}), bf16[8,4,2560]{2,1,0:T(4,128)(2,1)S(1)}, u32[]{:S(2)}, u32[]{:S(2)}) %all-to-all-start.2) | async-done | bytes 163872 | tf_op jit(solution)/shard_map/all_to_all | solution.py:29
  158.2 5.5 %all-to-all-start.3 = ((bf16[32,4,512]{2,1,0:T(4,128)(2,1)}), bf16[32,4,512]{2,1,0:T(4,128)(2,1)S(1)}, u32[]{:S(2)}, u32[]{:S(2)}) async-start(bf16[32,4,512]{2,1,0:T(4,128)(2,1)} %broadcast_in_dim.30), calls=%async_computation.3 | async-start | bytes 262144 | tf_op jit(solution)/shard_map/all_to_all | solution.py:29
  164.0 9.1 %all-to-all-done.3 = bf16[32,4,512]{2,1,0:T(4,128)(2,1)S(1)} async-done(((bf16[32,4,512]{2,1,0:T(4,128)(2,1)}), bf16[32,4,512]{2,1,0:T(4,128)(2,1)S(1)}, u32[]{:S(2)}, u32[]{:S(2)}) %all-to-all-start.3) | async-done | bytes 131104 | tf_op jit(solution)/shard_map/all_to_all | solution.py:29
  173.2 2.6 %shard_map.104 = f32[8,64,1024]{2,1,0:T(8,128)S(1)} custom-call(s32[9]{0:T(128)S(1)} %pad_add_fusion.1.mine_ref, f32[32,512]{1,0:T(8,128)S(1)} %reshape.82.dlow_ref, bf16[4,8,128,1024]{3,2,1,0:T(8,128)(2,1)} %bitcast.33), custom_call_target="tpu_custom_call" | custom-call | flops 536870912 | bytes 8388608 | tf_op jit(solution)/shard_map/pallas_call | solution.py:175
  177.9 5.7 %all-to-all-start.4 = ((bf16[8,4,2560]{2,1,0:T(4,128)(2,1)}), bf16[8,4,2560]{2,1,0:T(4,128)(2,1)S(1)}, u32[]{:S(2)}, u32[]{:S(2)}) async-start(bf16[8,4,2560]{2,1,0:T(4,128)(2,1)} %all_to_all.37), calls=%async_computation.5 | async-start | bytes 327680 | tf_op jit(solution)/shard_map/all_to_all | solution.py:29
  184.5 5.3 %all-to-all-done.4 = bf16[8,4,2560]{2,1,0:T(4,128)(2,1)S(1)} async-done(((bf16[8,4,2560]{2,1,0:T(4,128)(2,1)}), bf16[8,4,2560]{2,1,0:T(4,128)(2,1)S(1)}, u32[]{:S(2)}, u32[]{:S(2)}) %all-to-all-start.4) | async-done | bytes 163872 | tf_op jit(solution)/shard_map/all_to_all | solution.py:29
  190.5 2.0 shard_map.105
  192.5 15.6 %all_to_all.50 = bf16[32,8,512]{2,1,0:T(8,128)(2,1)} all-to-all(bf16[32,8,512]{2,1,0:T(8,128)(2,1)} %bitcast.36), channel_id=1, replica_groups=mesh['z'=8,'y'=4,'x'=4,'c'=2] {'z','y'}, dimensions={0} | all-to-all | bytes 524288 | tf_op jit(solution)/shard_map/all_to_all | solution.py:29
  (67 shorter events, 18.2 us)
Async XLA Ops:
  7.2 16.6 %copy-start = (bf16[32,2,16,1024]{3,2,1,0:T(8,128)(2,1)S(1)}, bf16[32,2,16,1024]{3,2,1,0:T(8,128)(2,1)}, u32[]{:S(2)}) copy-start(bf16[32,2,16,1024]{3,2,1,0:T(8,128)(2,1)} %param.10) | copy-start | bytes 6291460
  7.2 119.6 %all-gather.3.cloned.1.call-start = ((), (), s32[]{:S(2)}) async-start(), calls=%async_computation.8 | async-start | bytes 8650752 | tf_op jit(solution)/shard_map/all_gather | solution.py:218
  7.2 12.6 %collective-permute-start = (bf16[128,1024]{1,0:T(8,128)(2,1)}, bf16[128,1024]{1,0:T(8,128)(2,1)S(1)}, u32[]{:S(2)}, u32[]{:S(2)}) collective-permute-start(bf16[128,1024]{1,0:T(8,128)(2,1)} %param.8), channel_id=1, source_target_pairs={{0,32},{1,224},{2,64},{3,192},{4,96},{5,160},{6,0},{7,128},{8,40},... | collective-permute-start | bytes 786440 | tf_op jit(solution)/shard_map/ppermute | solution.py:214
  19.9 0.7 copy-start.4
  43.8 48.0 %collective-permute-start.1 = (bf16[1024,1024]{1,0:T(8,128)(2,1)}, bf16[1024,1024]{1,0:T(8,128)(2,1)}, u32[]{:S(2)}, u32[]{:S(2)}) collective-permute-start(bf16[1024,1024]{1,0:T(8,128)(2,1)} %bitcast.23.refs_0_), channel_id=1, source_target_pairs={{0,2},{2,4},{4,6},{6,0},{1,3},{3,5},{5,7},{7,1},{8,10},{10,12},{12... | collective-permute-start | bytes 6291464 | tf_op jit(solution)/shard_map/ppermute | solution.py:37
  44.1 47.7 %collective-permute-start.2 = (bf16[1024,1024]{1,0:T(8,128)(2,1)}, bf16[1024,1024]{1,0:T(8,128)(2,1)}, u32[]{:S(2)}, u32[]{:S(2)}) collective-permute-start(bf16[1024,1024]{1,0:T(8,128)(2,1)} %bitcast.23.refs_0_), channel_id=1, source_target_pairs={{0,6},{2,0},{4,2},{6,4},{1,7},{3,1},{5,3},{7,5},{8,14},{10,8},{12,... | collective-permute-start | bytes 6291464 | tf_op jit(solution)/shard_map/ppermute | solution.py:37
  46.5 45.3 %collective-permute-start.3 = (bf16[1024,1024]{1,0:T(8,128)(2,1)}, bf16[1024,1024]{1,0:T(8,128)(2,1)}, u32[]{:S(2)}, u32[]{:S(2)}) collective-permute-start(bf16[1024,1024]{1,0:T(8,128)(2,1)} %bitcast.23.refs_0_), channel_id=1, source_target_pairs={{0,1},{1,0},{2,3},{3,2},{4,5},{5,4},{6,7},{7,6},{8,9},{9,8},{10,11... | collective-permute-start | bytes 6291464 | tf_op jit(solution)/shard_map/ppermute | solution.py:37
  47.8 5.3 %collective-permute-start.4 = (bf16[4,128]{1,0:T(4,128)(2,1)S(1)}, bf16[4,128]{1,0:T(4,128)(2,1)S(1)}, u32[]{:S(2)}, u32[]{:S(2)}) collective-permute-start(bf16[4,128]{1,0:T(4,128)(2,1)S(1)} %reduce_sum.27), channel_id=1, source_target_pairs={{0,0},{1,32},{2,64},{3,96},{4,128},{5,160},{6,192},{7,224},{8,8},{... | collective-permute-start | bytes 3080 | tf_op jit(solution)/shard_map/ppermute | solution.py:224
  53.7 24.4 %all-to-all-start.1 = ((bf16[32,4,128]{2,1,0:T(4,128)(2,1)}), bf16[32,4,128]{2,1,0:T(4,128)(2,1)S(1)}, u32[]{:S(2)}, u32[]{:S(2)}) async-start(bf16[32,4,128]{2,1,0:T(4,128)(2,1)} %broadcast_in_dim.13), calls=%async_computation.1 | async-start | bytes 65536 | tf_op jit(solution)/shard_map/all_to_all | solution.py:29
  69.4 53.3 %copy-start.5 = (s32[32]{0:T(128)S(1)}, s32[32]{0:T(128)}, u32[]{:S(2)}) copy-start(s32[32]{0:T(128)} %param.14) | copy-start | bytes 388
  69.4 53.3 %copy-start.6 = (s32[32]{0:T(128)S(1)}, s32[32]{0:T(128)}, u32[]{:S(2)}) copy-start(s32[32]{0:T(128)} %param.13) | copy-start | bytes 388
  69.4 57.4 %copy-start.2 = (bf16[512,512]{1,0:T(8,128)(2,1)S(1)}, bf16[512,512]{1,0:T(8,128)(2,1)}, u32[]{:S(2)}) copy-start(bf16[512,512]{1,0:T(8,128)(2,1)} %refs_10_.1) | copy-start | bytes 1572868
  93.6 25.4 %collective-permute-start.7 = (bf16[1024,1024]{1,0:T(8,128)(2,1)S(1)}, bf16[1024,1024]{1,0:T(8,128)(2,1)}, u32[]{:S(2)}, u32[]{:S(2)}) collective-permute-start(bf16[1024,1024]{1,0:T(8,128)(2,1)S(1)} %broadcast_select_fusion), channel_id=1, source_target_pairs={{0,2},{1,7},{2,4},{3,1},{4,6},{5,3},{6,0},{7,5},{8,10},{9,15},{10,... | collective-permute-start | bytes 6291464 | tf_op jit(solution)/shard_map/ppermute | solution.py:45
  96.1 28.7 %collective-permute-start.5 = (bf16[1024,1024]{1,0:T(8,128)(2,1)}, bf16[1024,1024]{1,0:T(8,128)(2,1)}, u32[]{:S(2)}, u32[]{:S(2)}) collective-permute-start(bf16[1024,1024]{1,0:T(8,128)(2,1)} %collective-permute-done.1.refs_2_), channel_id=1, source_target_pairs={{0,1},{1,0},{2,3},{3,2},{4,5},{5,4},{6,7},{7,6},{8,9},{9,8},{10,11... | collective-permute-start | bytes 6291464 | tf_op jit(solution)/shard_map/ppermute | solution.py:37
  96.1 28.7 %collective-permute-start.6 = (bf16[1024,1024]{1,0:T(8,128)(2,1)}, bf16[1024,1024]{1,0:T(8,128)(2,1)}, u32[]{:S(2)}, u32[]{:S(2)}) collective-permute-start(bf16[1024,1024]{1,0:T(8,128)(2,1)} %collective-permute-done.2.refs_4_), channel_id=1, source_target_pairs={{0,1},{1,0},{2,3},{3,2},{4,5},{5,4},{6,7},{7,6},{8,9},{9,8},{10,11... | collective-permute-start | bytes 6291464 | tf_op jit(solution)/shard_map/ppermute | solution.py:37
  119.1 7.7 %collective-permute-start.8 = (bf16[1024,1024]{1,0:T(8,128)(2,1)}, bf16[1024,1024]{1,0:T(8,128)(2,1)}, u32[]{:S(2)}, u32[]{:S(2)}) collective-permute-start(bf16[1024,1024]{1,0:T(8,128)(2,1)} %collective-permute-done.7.refs_6_), channel_id=1, source_target_pairs={{0,1},{1,0},{2,3},{3,2},{4,5},{5,4},{6,7},{7,6},{8,9},{9,8},{10,11... | collective-permute-start | bytes 6291464 | tf_op jit(solution)/shard_map/ppermute | solution.py:37
  126.8 22.0 %copy-start.3 = (s32[32]{0:T(128)S(1)}, s32[32]{0:T(128)}, u32[]{:S(2)}) copy-start(s32[32]{0:T(128)} %param.15) | copy-start | bytes 388
  141.3 16.0 %all-to-all-start.2 = ((bf16[8,4,2560]{2,1,0:T(4,128)(2,1)}), bf16[8,4,2560]{2,1,0:T(4,128)(2,1)S(1)}, u32[]{:S(2)}, u32[]{:S(2)}) async-start(bf16[8,4,2560]{2,1,0:T(4,128)(2,1)} %all_to_all.33), calls=%async_computation.2 | async-start | bytes 327680 | tf_op jit(solution)/shard_map/all_to_all | solution.py:29
  158.2 14.9 %all-to-all-start.3 = ((bf16[32,4,512]{2,1,0:T(4,128)(2,1)}), bf16[32,4,512]{2,1,0:T(4,128)(2,1)S(1)}, u32[]{:S(2)}, u32[]{:S(2)}) async-start(bf16[32,4,512]{2,1,0:T(4,128)(2,1)} %broadcast_in_dim.30), calls=%async_computation.3 | async-start | bytes 262144 | tf_op jit(solution)/shard_map/all_to_all | solution.py:29
  163.7 46.4 %reduce-scatter.2.cloned.1.call-start = ((), (), s32[]{:S(2)}) async-start(), calls=%async_computation.7 | async-start | bytes 2359296 | tf_op jit(solution)/shard_map/reduce_scatter | solution.py:249
  175.8 1.3 copy-start.1
  177.9 11.9 %all-to-all-start.4 = ((bf16[8,4,2560]{2,1,0:T(4,128)(2,1)}), bf16[8,4,2560]{2,1,0:T(4,128)(2,1)S(1)}, u32[]{:S(2)}, u32[]{:S(2)}) async-start(bf16[8,4,2560]{2,1,0:T(4,128)(2,1)} %all_to_all.37), calls=%async_computation.5 | async-start | bytes 327680 | tf_op jit(solution)/shard_map/all_to_all | solution.py:29
Sparse Core Ops, SparseCore 0:
  20.7 105.1 all-gather.2
  177.3 30.8 reduce-scatter.1
